TPU v7x, 32 devices: a whole 2x2x4 slice. The times are simulated.
32 devices in a mesh: dp: 8 (over z, y), stream: 4 (over x, core).
Axes of the slice: x: 2, y: 2, z: 4, core: 2. Of those that a mesh axis runs over, the one named last changes fastest.
Arguments:
- text_input: bfloat16 [2, 128, 40, 768], P(None, ('dp', 'stream')), may hold values from -6 to 6
- patch_input: bfloat16 [2, 32, 145, 1024], P(None, ('dp', 'stream')), may hold values from -6 to 6
- text_lengths: int32 [2, 128], P(None, ('dp', 'stream')), may hold values from 6 to 40, as said below
- image_of_row: int32 [2, 128], P(None, ('dp', 'stream')), may hold values from 0 to 3, as said below
- cotangent: bfloat16 [2, 128, 40, 768], P(None, ('dp', 'stream')), may hold values from -6 to 6
- self_qkv: bfloat16 [3, 768, 768], P(None, 'dp'), may hold values from -0.21875 to 0.21875
- self_out: bfloat16 [768, 768], P('dp'), may hold values from -0.4375 to 0.4375
- cross_q: bfloat16 [768, 768], P('dp'), may hold values from -0.21875 to 0.21875
- cross_kv: bfloat16 [2, 1024, 768], P(None, 'dp'), may hold values from -0.1875 to 0.1875
- cross_out: bfloat16 [768, 768], P('dp'), may hold values from -0.75 to 0.75
- ffn_in: bfloat16 [768, 3072], P('dp'), may hold values from -0.21875 to 0.21875
- ffn_out: bfloat16 [3072, 768], P('dp'), may hold values from -0.109375 to 0.109375
- biases: bfloat16 [10, 768], P(None, 'dp'), may hold values from -1 to 1
- norm_gains: bfloat16 [3, 768], P(None, 'dp'), may hold values from 0.25 to 1.75
- ffn_bias: bfloat16 [3072], P('dp'), may hold values from -1 to 1
Outputs:
- layer_out: bfloat16 [2, 128, 40, 768], P(None, ('dp', 'stream'))
- text_grad: bfloat16 [2, 128, 40, 768], P(None, ('dp', 'stream'))
- patch_grad: bfloat16 [2, 32, 145, 1024], P(None, ('dp', 'stream'))
- grad_self_qkv: float32 [3, 768, 768], P(None, 'dp')
- grad_self_out: float32 [768, 768], P('dp')
- grad_cross_q: float32 [768, 768], P('dp')
- grad_cross_kv: float32 [2, 1024, 768], P(None, 'dp')
- grad_cross_out: float32 [768, 768], P('dp')
- grad_ffn_in: float32 [768, 3072], P('dp')
- grad_ffn_out: float32 [3072, 768], P('dp')
- grad_biases: float32 [10, 768], P(None, 'dp')
- grad_norm_gains: float32 [3, 768], P(None, 'dp')
- grad_ffn_bias: float32 [3072], P('dp')
Inputs may be any that keep to these rules, and one draw needn't show every extreme that they name: `text_lengths`: valid tokens of each row, counted from the row's start. `image_of_row`: each row names one of the 4 images of its group.
All inputs are finite; a program needn't handle non-finite values.
Results may differ from a plain program's by a relative error of at most 0.02.
Values may be sent and summed in bfloat16 or wider, within the bound.
No kernel may reach another device: no remote copies, remote signals or barrier semaphores. Data moves between devices by JAX's collectives and lax.ppermute only.
A program may use at most 512 MiB of HBM per device.

v0:
```python
import functools
import types

import jax
import jax.numpy as jnp
from jax import lax
from jax.experimental import pallas as pl
from jax.experimental.pallas import tpu as pltpu
from jax.sharding import PartitionSpec as P

HEADS = 12
LANES = 384
PAD_ROWS = 16
MIB = 2**20
DP, STREAM = "dp", "stream"

EPSILON = 1e-06
ROOT_HALF = 0.7071067811865476
INV_ROOT_TAU = 0.3989422804014327

CORE = ((0, 1), (1, 0), (2, 3), (3, 2))
ACROSS = ((0, 2), (2, 0), (1, 3), (3, 1))
BESIDE = ((0, 1), (1, 0), (2, 3), (3, 2), (4, 5), (5, 4), (6, 7), (7, 6))
PAIR = ((0, 2), (2, 0), (1, 3), (3, 1), (4, 6), (6, 4), (5, 7), (7, 5))
HALFWAY = ((0, 4), (4, 0), (1, 5), (5, 1), (2, 6), (6, 2), (3, 7), (7, 3))
MIRROR = ((0, 6), (6, 0), (1, 7), (7, 1), (2, 4), (4, 2), (3, 5), (5, 3))

B_Q, B_V, B_SO, B_N1, B_CQ, B_CV, B_CO, B_N2, B_FO, B_N3, G_1, G_2, G_3 = range(13)


def low(value):
    return value.astype(jnp.bfloat16)


def wide(value):
    return value.astype(jnp.float32)


def dot(left, right):
    return jnp.dot(left, right, preferred_element_type=jnp.float32)


def dot_last(left, right):
    return lax.dot_general(
        left, right, (((1,), (1,)), ((), ())), preferred_element_type=jnp.float32
    )


def dot_first(left, right):
    return lax.dot_general(
        left, right, (((0,), (0,)), ((), ())), preferred_element_type=jnp.float32
    )


def pick(array, index, axis=0):
    return lax.dynamic_index_in_dim(array, index, axis, keepdims=False)


def place():
    dp_at, stream_at = lax.axis_index(DP), lax.axis_index(STREAM)
    return dp_at // 2, dp_at % 2, stream_at // 2, stream_at % 2


class Base:
    def __init__(self, array):
        self.array = array.reshape(-1, LANES)
        self.twin = None

    def exchange(self, tie):
        if self.twin is None:
            self.twin = lax.ppermute(tie(self.array), STREAM, CORE)
        return self.twin


class Piece:
    def __init__(self, base, row, dims):
        self.base, self.row, self.dims = base, row, dims

    def value(self):
        rows = 1
        for size in self.dims[:-1]:
            rows *= size
        return self.base.array[self.row : self.row + rows].reshape(self.dims)


class Clock:
    def __init__(self):
        self.before = []
        self.came = []

    def take(self, arrays):
        given = {}
        for array, (_, sends) in zip(arrays, self.came):
            row = 0
            base = Base(array) if sends[0][0].pieces else None
            for mover, at, sent in sends:
                part = array
                if base is not None:
                    part = Piece(base, row, sent.shape)
                    row += sent.size // LANES
                elif len(sends) > 1:
                    rows = sent.size // LANES
                    part = array[row : row + rows].reshape(sent.shape)
                    row += rows
                given.setdefault(mover, {})[at] = part
        self.came = []
        for mover, parts in given.items():
            mover.give([parts[at] for at in range(len(parts))])

    def step(self, moving=(), compute=(), eager=False):
        arrays = [array for array, _ in self.came]
        arrays, self.before = lax.optimization_barrier((arrays, self.before + arrays[:1]))
        self.take(arrays)
        ways = {}
        for mover in moving:
            if mover.done:
                continue
            for at, (array, axis, hops) in enumerate(mover.requests):
                alone = hops is CORE or array.shape[-1] != LANES
                key = (axis, hops, (mover, at) if alone else None)
                ways.setdefault(key, []).append((mover, at, array))
        joined = [
            sends[0][2]
            if len(sends) == 1
            else jnp.concatenate([array.reshape(-1, LANES) for _, _, array in sends])
            for sends in ways.values()
        ]
        joined, self.before = lax.optimization_barrier((joined, self.before))
        self.came = [
            (lax.ppermute(array, axis, hops), sends)
            for array, ((axis, hops, _), sends) in zip(joined, ways.items())
        ]
        after = []
        if eager:
            movers = [mover for sends in ways.values() for mover, _, _ in sends]
            self.take([array for array, _ in self.came])
            for mover in dict.fromkeys(movers):
                if mover.done:
                    after += jax.tree.leaves(mover.result)
                else:
                    after += [array for array, _, _ in mover.requests]
        for work in compute() if callable(compute) else compute:
            after += jax.tree.leaves(work(self.tie))
        if after:
            self.before = after

    def tie(self, array):
        return lax.optimization_barrier((array, self.before))[0]


class Mover:
    def __init__(self, steps, pieces=False):
        self.steps = steps
        self.pieces = pieces
        self.done = False
        self.result = None
        self.requests = next(steps)

    def give(self, came):
        try:
            self.requests = self.steps.send(came)
        except StopIteration as stop:
            self.done, self.result = True, stop.value


def special_mesh():
    return lax.axis_size(DP) == 8 and lax.axis_size(STREAM) == 4


VMEM = pl.BlockSpec(memory_space=pltpu.VMEM)
SMEM = pl.BlockSpec(memory_space=pltpu.SMEM)
ANY = pl.BlockSpec(memory_space=pl.ANY)


def call(kernel, out_shape, in_specs, scratch=(), mib=24, flops=0, out_specs=None, **more):
    return pl.pallas_call(
        kernel,
        out_shape=out_shape,
        in_specs=in_specs,
        out_specs=jax.tree.map(lambda _: VMEM, out_shape) if out_specs is None else out_specs,
        scratch_shapes=list(scratch),
        compiler_params=pltpu.CompilerParams(vmem_limit_bytes=mib * MIB),
        cost_estimate=pl.CostEstimate(flops=flops, bytes_accessed=4 * MIB, transcendentals=0),
        **more,
    )


def shape(dims, dtype=jnp.bfloat16):
    return jax.ShapeDtypeStruct(tuple(dims), dtype)


F32 = jnp.float32


def pack_shard(shard, units):
    if shard.ndim == 2:
        rows, _ = shard.shape
        split = shard.reshape(2, rows // 2, 2, units, LANES).transpose(2, 0, 3, 1, 4)
    else:
        _, rows, _ = shard.shape
        split = shard.reshape(units, 2, rows // 2, 2, LANES).transpose(3, 1, 0, 2, 4)
    return split.reshape(2, 2, units * rows // 2, LANES)


def pack_kernel(units, *refs):
    _, _, x_at, core_at = place()
    shards, (both, own, own_x) = refs[: len(units)], refs[len(units) :]
    row = 0
    for shard, (count, depth) in zip(shards, units):
        if len(shard.shape) == 4:
            both[:, :, row : row + depth] = shard[...]
            row += depth
            continue
        for unit in range(count):
            rows = slice(row, row + depth)
            for x in range(2):
                for c in range(2):
                    if len(shard.shape) == 3:
                        block = shard[unit, x * depth : (x + 1) * depth, c * LANES : (c + 1) * LANES]
                    else:
                        start = (c * count + unit) * LANES
                        block = shard[x * depth : (x + 1) * depth, start : start + LANES]
                    both[c, x, rows] = block
            row += depth
    own[...] = both[core_at]
    own_x[...] = both[core_at, x_at]


def pack_own_kernel(units, *refs):
    _, _, x_at, core_at = place()
    shards, out = refs[:-1], refs[-1]
    row = 0
    for shard, (count, depth) in zip(shards, units):
        for unit in range(count):
            start = (core_at * count + unit) * LANES
            out[row : row + depth] = shard[
                pl.ds(pl.multiple_of(x_at * depth, 16), depth),
                pl.ds(pl.multiple_of(start, 128), LANES),
            ]
            row += depth


def pack_group(shards, units):
    rows = sum(count * depth for count, depth in units)
    return call(
        functools.partial(pack_kernel, units),
        [shape((2, 2, rows, LANES)), shape((2, rows, LANES)), shape((rows, LANES))],
        [VMEM] * len(shards),
    )(*shards)


def pack_own(shards, units):
    rows = sum(count * depth for count, depth in units)
    return call(
        functools.partial(pack_own_kernel, units), shape((rows, LANES)), [VMEM] * len(shards)
    )(*shards)


def gather_steps(own_both, own, own_x):
    x_at = lax.axis_index(STREAM) // 2
    mate, half_z, mirror_z, beside = yield [
        (own, DP, PAIR),
        (own_x, DP, HALFWAY),
        (own_x, DP, MIRROR),
        (own, DP, BESIDE),
    ]
    mate_halves = mate.value()
    others = jnp.stack((pick(mate_halves, x_at), half_z.value(), mirror_z.value()))
    beside_others, half_x, mirror_x = yield [
        (others, DP, BESIDE),
        (half_z.value(), STREAM, ACROSS),
        (mirror_z.value(), STREAM, ACROSS),
    ]
    others_x, mate_x = yield [
        (beside_others.value()[1:], STREAM, ACROSS),
        (pick(mate_halves, 1 - x_at), DP, BESIDE),
    ]
    whole = Piece(Base(own_both), 0, own_both.shape)
    return (
        whole, mate, beside, half_z, mirror_z, half_x, mirror_x, beside_others, others_x, mate_x
    )


def piece_sources(pieces, tie):
    own, *received = pieces
    rows = own.dims[2]
    arrays, spec = [own.base.array], [(0, at * rows) for at in range(4)]
    known = {}

    def find(piece, theirs):
        key = (piece.base, theirs)
        if key not in known:
            known[key] = len(arrays)
            arrays.append(piece.base.exchange(tie) if theirs else piece.base.array)
        return known[key]

    for theirs in (False, True):
        mate, beside, half_z, mirror_z, half_x, mirror_x, others, others_x, mate_x = received
        blocks = [(mate, 0), (beside, 0), (mate, 1), (beside, 1)]
        blocks += [(half_z, 0), (mirror_z, 0), (half_x, 0), (mirror_x, 0)]
        blocks += [(others, 0), (others, 1), (others, 2), (mate_x, 0), (others_x, 0), (others_x, 1)]
        spec += [(find(piece, theirs), piece.row + block * rows) for piece, block in blocks]
    return arrays, tuple(spec)


def piece_places(spec, sources):
    z_at, y_at, x_at, core_at = place()
    _, z_mate, z_half, z_mirror = shard_slots(z_at)
    far_y, far_x = 1 - y_at, 1 - x_at
    places = [(z_at, y_at, x_from, core_from) for core_from in range(2) for x_from in range(2)]
    for core_from in (core_at, 1 - core_at):
        for x_from in range(2):
            places.append((z_mate, y_at, x_from, core_from))
            places.append((z_at, far_y, x_from, core_from))
        places += [
            (z_half, y_at, x_at, core_from),
            (z_mirror, y_at, x_at, core_from),
            (z_half, y_at, far_x, core_from),
            (z_mirror, y_at, far_x, core_from),
            (z_mate, far_y, x_at, core_from),
            (z_half, far_y, x_at, core_from),
            (z_mirror, far_y, x_at, core_from),
            (z_mate, far_y, far_x, core_from),
            (z_half, far_y, far_x, core_from),
            (z_mirror, far_y, far_x, core_from),
        ]
    return [(sources[at], row, *where) for (at, row), where in zip(spec, places)]


def piece_copies(units, spec, sources, wholes, sems):
    parts = piece_places(spec, sources)
    copies, row, sem = [], 0, 0
    for (count, depth), whole in zip(units, wholes):
        of_weight = []
        for source, first, z_from, y_from, x_from, core_from in parts:
            start = (z_from * 2 + y_from) * (2 * depth) + x_from * depth
            of_weight.append(
                pltpu.make_async_copy(
                    source.at[pl.ds(first + row, count * depth)].reshape(count, depth, LANES),
                    whole.at[core_from, :, pl.ds(pl.multiple_of(start, 16), depth)],
                    sems.at[sem],
                )
            )
            sem += 1
        copies.append(of_weight)
        row += count * depth
    return copies


def gather_plain(shards, units):
    packed = [
        shard if shard.ndim == 4 else pack_shard(shard, count)
        for shard, (count, _) in zip(shards, units)
    ]
    whole = lax.all_gather(jnp.concatenate(packed, axis=2), DP, axis=0, tiled=False)
    results = []
    row = 0
    for count, depth in units:
        part = whole[:, :, :, row : row + count * depth]
        part = part.reshape(-1, 2, 2, count, depth, LANES).transpose(1, 3, 0, 2, 4, 5)
        results.append(part.reshape(2, count, -1, LANES))
        row += count * depth
    return results


def shard_slots(z_at):
    return z_at, z_at + 1 - 2 * (z_at % 2), (z_at + 2) % 4, 3 - z_at


def grad_columns(right, core, units):
    blocks = []
    for lead in [None] if len(right.shape) == 2 else range(right.shape[0]):
        of_lead = right if lead is None else right.at[lead]
        start = pl.multiple_of(core * (units * LANES), 128)
        blocks.append(of_lead[:, pl.ds(start, units * LANES)])
    return blocks[0] if len(blocks) == 1 else jnp.concatenate(blocks, axis=1)


def sibling_grad_kernel(jobs, *refs):
    operands, out = refs[:-1], refs[-1]
    core_at = lax.axis_index(STREAM) % 2
    row = 0
    for at, (units, blocks, depth) in enumerate(jobs):
        left, right = operands[2 * at], operands[2 * at + 1]
        product = low(dot_first(left[...], grad_columns(right, 1 - core_at, units)))
        for block in range(blocks):
            columns = product[:, block * LANES : (block + 1) * LANES]
            out[:, :, row : row + depth] = columns.reshape(8, 2, depth, LANES)
            row += depth


TO_X = ((2, False, False), (3, False, False), (2, True, False), (3, True, False))
TO_Y_A = ((0, False, True), (1, False, True))
TO_Z_A = ((1, False, False), (1, True, False))
TO_Y_B = ((2, False, True), (3, False, True), (0, False, False))
TO_Z_B = ((1, True, True),)
TO_Z_C = ((2, True, True), (3, True, True))
OWN = ((0, True, True), (0, True, False))
PARTS = (TO_X, TO_Y_A, TO_Z_A, TO_Y_B, TO_Z_B, TO_Z_C, OWN)


def part_at(part):
    z_at, y_at, x_at, _ = place()
    slot, own_y, own_x = part
    return (
        shard_slots(z_at)[slot] * 2 + (y_at if own_y else 1 - y_at),
        x_at if own_x else 1 - x_at,
    )


def small_grad_rows(sums, hidden_bias, work):
    sums0, sums1, sums2, sums3, sums_kv = sums
    rows = (
        (sums0, 0), (sums0, 1), (sums1, 2), (sums1, 1), (sums1, 3), (sums_kv, 0), (sums2, 2),
        (sums2, 1), (sums3, 2), (sums3, 1), (sums1, 0), (sums2, 0), (sums3, 0),
    )
    part = sums0.shape[1] // 8
    work[...] = jnp.zeros_like(work)
    for dp_to in range(8):
        columns = slice(dp_to * part, (dp_to + 1) * part)
        for row, (array, at) in enumerate(rows):
            work[dp_to, row : row + 1, :part] = array[at : at + 1, columns]
        for j in range(hidden_bias.shape[1] // part):
            at = len(rows) + j
            work[dp_to, at : at + 1, :part] = hidden_bias[
                dp_to : dp_to + 1, j * part : (j + 1) * part
            ]


def own_grad_kernel(jobs, sent, small, *refs):
    inputs = 2 * len(jobs) + len(sent)
    operands, came = refs[: 2 * len(jobs)], refs[2 * len(jobs) : inputs]
    extra = refs[inputs : inputs + 6 * small]
    outs = refs[inputs + 6 * small : inputs + 6 * small + len(PARTS)]
    work, *small_work = refs[inputs + 6 * small + len(PARTS) :]
    core_at = lax.axis_index(STREAM) % 2
    row = 0
    for at, (units, blocks, depth) in enumerate(jobs):
        left, right = operands[2 * at], operands[2 * at + 1]
        product = dot_first(left[...], grad_columns(right, core_at, units))
        array, came_row = sent[at]
        for block in range(blocks):
            columns = product[:, block * LANES : (block + 1) * LANES]
            rows = slice(row, row + depth)
            work[:, :, :depth] = columns.reshape(8, 2, depth, LANES) + wide(
                came[array][:, :, came_row : came_row + depth]
            )
            for out, parts in zip(outs, PARTS):
                for j, part in enumerate(parts):
                    dp_from, x_from = part_at(part)
                    out[j, rows] = low(work[dp_from, x_from, :depth])
            row += depth
            came_row += depth
    if small:
        small_grad_rows(extra[:5], extra[5], small_work[0])
        for out, parts in zip(outs, PARTS):
            for j, part in enumerate(parts):
                dp_from, x_from = part_at(part)
                rows = pl.ds(pl.multiple_of(x_from * PAD_ROWS, PAD_ROWS), PAD_ROWS)
                out[j, row : row + PAD_ROWS] = low(small_work[0][dp_from, rows])


def reduce_steps(to_x, to_y_a, to_z_a, to_y_b, to_z_b, to_z_c, own):
    from_y_a, from_x, from_z_a = yield [
        (to_y_a, DP, BESIDE),
        (to_x, STREAM, ACROSS),
        (to_z_a, DP, PAIR),
    ]
    arrived = jnp.concatenate((from_x[:2], from_z_a[:1]))
    from_y_b, mate = yield [
        (low(wide(to_y_b) + wide(arrived)), DP, BESIDE),
        (low(wide(to_z_b) + wide(from_y_a[1:])), DP, PAIR),
    ]
    far = wide(to_z_c) + wide(from_x[2:]) + wide(from_y_b[:2])
    (by_mate,) = yield [(low(far[1]), DP, PAIR)]
    (half,) = yield [(low(far[0] + wide(by_mate)), DP, HALFWAY)]
    total = low(
        jnp.stack(
            (
                wide(own[0]) + wide(from_y_a[0]) + wide(mate[0]) + wide(half),
                wide(own[1]) + wide(from_y_b[2]) + wide(from_z_a[1]),
            )
        )
    )
    (from_x,) = yield [(total, STREAM, ACROSS)]
    total = low(wide(total) + wide(from_x[::-1]))
    return total, lax.ppermute(total, STREAM, CORE)


def unpack_kernel(jobs, small, mine, other, *outs):
    _, _, x_at, core_at = place()
    for source, core_from in ((mine, core_at), (other, 1 - core_at)):
        for j in range(2):
            x_from = x_at if j == 0 else 1 - x_at
            for out_at, lead, units, row, depth in jobs:
                out = outs[out_at] if lead is None else outs[out_at].at[lead]
                for unit in range(units):
                    at = row + unit * depth
                    start = core_from * (units * LANES) + unit * LANES
                    out[
                        pl.ds(pl.multiple_of(x_from * depth, 8), depth),
                        pl.ds(pl.multiple_of(start, 128), LANES),
                    ] = wide(source[j, at : at + depth])
    if small is not None:
        biases, gains, hidden_bias, work = outs[-4:]
        for j in range(2):
            x_from = x_at if j == 0 else 1 - x_at
            rows = slice(small, small + PAD_ROWS)
            work[pl.ds(pl.multiple_of(x_from * PAD_ROWS, 8), PAD_ROWS)] = wide(
                mine[j, rows]
            ) + wide(other[j, rows])
        part = biases.shape[1]
        biases[...] = work[:G_1, :part]
        gains[...] = work[G_1 : G_3 + 1, :part]
        hidden_bias[...] = work[G_3 + 1 : G_3 + 1 + hidden_bias.shape[0], :part]


def reduce_plain(parts):
    shards = []
    for left, right in parts:
        if right.ndim == 2:
            whole = low(dot_first(left, right))
            own = lax.psum_scatter(whole, DP, scatter_dimension=0, tiled=True)
        else:
            whole = low(jnp.stack([dot_first(left, r) for r in right]))
            own = lax.psum_scatter(whole, DP, scatter_dimension=1, tiled=True)
        shards.append(wide(lax.psum(own, STREAM)))
    return shards


class Group:
    def __init__(self):
        self.operands, self.jobs, self.out_jobs, self.out_shapes = [], [], [], []
        self.rows, self.flops, self.sent, self.came, self.from_sent = 0, 0, [], [], []

    def sibling(self, tie, *parts):
        jobs, operands, rows, flops = [], [], 0, 0
        for left, right in parts:
            operands += [left, right]
            depth = left.shape[1] // 16
            units = right.shape[-1] // (2 * LANES)
            leads = [None] if right.ndim == 2 else range(right.shape[0])
            jobs.append((units, units * len(leads), depth))
            self.from_sent.append((len(self.sent), rows))
            for lead in leads:
                self.out_jobs.append(
                    (len(self.out_shapes), lead, units, self.rows + rows, depth)
                )
                rows += units * depth
            self.out_shapes.append(
                shape((*right.shape[:-2], 2 * depth, right.shape[-1]), F32)
            )
            flops += left.shape[0] * left.shape[1] * right.size // right.shape[-2]
        self.sent.append(
            call(
                functools.partial(sibling_grad_kernel, jobs),
                shape((8, 2, rows, LANES)),
                [VMEM] * len(operands),
                flops=flops,
            )(tie(operands[0]), *operands[1:])
        )
        self.jobs += jobs
        self.operands += operands
        self.rows += rows
        self.flops += flops
        return self.sent[-1]

    def core_move(self):
        def steps(sent):
            (came,) = yield [(sent, STREAM, CORE)]
            self.came.append(came)

        return Mover(steps(self.sent[-1]))

    def own(self, tie, small=()):
        deepest = max(job[-1] for job in self.jobs)
        scratch = [pltpu.VMEM((8, 2, deepest, LANES), F32)]
        if small:
            scratch.append(pltpu.VMEM((8, 2 * PAD_ROWS, LANES), F32))
        rows = self.rows + PAD_ROWS * bool(small)
        came = [self.came[array] for array, _ in self.from_sent]
        self.parts = call(
            functools.partial(
                own_grad_kernel,
                self.jobs,
                [(at, row) for at, (_, row) in enumerate(self.from_sent)],
                bool(small),
            ),
            [shape((len(parts), rows, LANES)) for parts in PARTS],
            [VMEM] * (len(self.operands) + len(came) + len(small)),
            scratch,
            flops=self.flops,
        )(tie(self.operands[0]), *self.operands[1:], *came, *small)
        return self.parts

    def move(self):
        return Mover(reduce_steps(*self.parts))

    def unpack(self, moved, small=()):
        return call(
            functools.partial(unpack_kernel, self.out_jobs, self.rows if small else None),
            [*self.out_shapes, *small],
            [VMEM, VMEM],
            [pltpu.VMEM((2 * PAD_ROWS, LANES), F32)] * bool(small),
        )(*moved)


def norm_parts(summed):
    center = summed - jnp.mean(summed, axis=-1, keepdims=True)
    inverse = lax.rsqrt(jnp.mean(center * center, axis=-1, keepdims=True) + EPSILON)
    return center * inverse, inverse


def norm_back(upstream, normed, inverse, gain):
    scaled = upstream * gain
    return inverse * (
        scaled
        - jnp.mean(scaled, axis=-1, keepdims=True)
        - normed * jnp.mean(scaled * normed, axis=-1, keepdims=True)
    )


def heads_apart(four):
    head = lax.broadcasted_iota(jnp.int32, four.shape, 1) // 64
    return low(jnp.concatenate([jnp.where(head == j, four, 0.0) for j in range(4)], axis=0))


def heads_joined(stacked):
    rows = stacked.shape[0] // 4
    head = lax.broadcasted_iota(jnp.int32, (rows, stacked.shape[1]), 1) // 64
    made = stacked[:rows]
    for j in range(1, 4):
        made = jnp.where(head == j, stacked[j * rows : (j + 1) * rows], made)
    return made


def quads():
    return [slice(j * 256, (j + 1) * 256) for j in range(HEADS // 4)]


def softmax(scores):
    raised = jnp.exp(scores - jnp.max(scores, axis=-1, keepdims=True))
    return raised * (1.0 / jnp.sum(raised, axis=-1, keepdims=True))


def score_back(weight, back):
    return low(weight * (back - jnp.sum(back * weight, axis=-1, keepdims=True)))


def row_sum(value):
    return jnp.sum(value, axis=0, keepdims=True)


def self_kernel(seq, lengths, x_ref, w_ref, vec, qkv_ref, out_ref, q, k, v, o):
    tokens = x_ref.shape[0]
    for j, (scratch, bias) in enumerate(((q, B_Q), (k, None), (v, B_V))):
        for c in range(2):
            columns = slice(c * LANES, (c + 1) * LANES)
            made = dot(x_ref[...], w_ref[c, j])
            if bias is not None:
                made = made + vec[bias : bias + 1, columns]
            made = low(made)
            qkv_ref[j, :, columns] = made
            scratch[:, columns] = wide(made)

    def step(r, _):
        rows = pl.ds(pl.multiple_of(r * seq, 8), seq)
        valid = lax.broadcasted_iota(jnp.int32, (4 * seq, seq), 1) < lengths[r]
        asked = [heads_apart(q[rows, c] * 0.125) for c in quads()]
        scores = [dot_last(a, low(k[rows, c])) for a, c in zip(asked, quads())]
        weights = [softmax(jnp.where(valid, score, -jnp.inf)) for score in scores]
        made = [dot(low(w), low(v[rows, c])) for w, c in zip(weights, quads())]
        for part, c in zip(made, quads()):
            o[rows, c] = heads_joined(part)
        return 0

    lax.fori_loop(0, tokens // seq, step, 0, unroll=2)
    out_ref[...] = low(o[...])


def first_norm_kernel(seq, o_ref, x_ref, wso, wcq, vec, normed, inverse, h_low, qc, z):
    for c in range(2):
        columns = slice(c * LANES, (c + 1) * LANES)
        z[:, columns] = (
            dot(o_ref[...], wso[c, 0])
            + vec[B_SO : B_SO + 1, columns]
            + wide(x_ref[:, columns])
        )
    made, scale = norm_parts(z[...])
    normed[...] = made
    inverse[...] = scale
    h_low[...] = low(made * vec[G_1 : G_1 + 1] + vec[B_N1 : B_N1 + 1])
    for c in range(2):
        columns = slice(c * LANES, (c + 1) * LANES)
        qc[:, columns] = low(dot(h_low[...], wcq[c, 0]) + vec[B_CQ : B_CQ + 1, columns])


def pixel_kernel(patch_ref, out_ref):
    images, patches, _ = patch_ref.shape
    out_ref[:, :patches] = patch_ref[...]
    out_ref[:, patches:] = jnp.zeros_like(out_ref[:, patches:])


def image_kernel(pixels, w_ref, vec, kv_ref):
    slots, _, images, padded, _ = kv_ref.shape
    for slot in range(slots):
        for c in range(2):
            columns = slice(c * LANES, (c + 1) * LANES)
            for j in range(2):
                made = dot(pixels[slot].reshape(images * padded, -1), w_ref[c, j])
                if j == 1:
                    made = made + vec[B_CV : B_CV + 1, columns]
                kv_ref[slot, j, :, :, columns] = low(made).reshape(images, padded, LANES)


def cross_kernel(
    seq, patches, micro_rows, slots, qc, kv, n1, wco, vec, oc, n2, inverse, h_low, q, o
):
    q[...] = wide(qc[...]) * 0.125
    tokens = qc.shape[0]
    padded = kv.shape[3]
    there = lax.broadcasted_iota(jnp.int32, (4 * seq, padded), 1) < patches

    def step(r, _):
        rows = pl.ds(pl.multiple_of(r * seq, 8), seq)
        slot, m = slots[r], r // micro_rows
        asked = [heads_apart(q[rows, c]) for c in quads()]
        scores = [dot_last(a, kv[slot, 0, m, :, c]) for a, c in zip(asked, quads())]
        weights = [softmax(jnp.where(there, score, -jnp.inf)) for score in scores]
        made = [dot(low(w), kv[slot, 1, m, :, c]) for w, c in zip(weights, quads())]
        for part, c in zip(made, quads()):
            o[rows, c] = heads_joined(part)
        return 0

    lax.fori_loop(0, tokens // seq, step, 0, unroll=2)
    oc[...] = low(o[...])
    for c in range(2):
        columns = slice(c * LANES, (c + 1) * LANES)
        first = n1[:, columns] * vec[G_1 : G_1 + 1, columns] + vec[B_N1 : B_N1 + 1, columns]
        o[:, columns] = first + dot(oc[...], wco[c, 0]) + vec[B_CO : B_CO + 1, columns]
    made, scale = norm_parts(o[...])
    n2[...] = made
    inverse[...] = scale
    h_low[...] = low(made * vec[G_2 : G_2 + 1] + vec[B_N2 : B_N2 + 1])


def small_rows_kernel(shards, vec, hidden_bias, part):
    wide_rows = G_3 + 1
    vec[...] = jnp.zeros_like(vec)
    for dp_from in range(8):
        rows = wide(shards[dp_from * 2 * PAD_ROWS : (dp_from + 1) * 2 * PAD_ROWS])
        vec[:wide_rows, dp_from * part : (dp_from + 1) * part] = rows[:wide_rows, :part]
        for j in range(LANES // part):
            hidden_bias[dp_from : dp_from + 1, j * part : (j + 1) * part] = rows[
                wide_rows + j : wide_rows + j + 1, :part
            ]


def take_weights(units, spec, sources, wholes, outs, in_sems, out_sems, kept):
    if spec is None:
        copies = [
            [pltpu.make_async_copy(source, whole, in_sems.at[at])]
            for at, (source, whole) in enumerate(zip(sources, wholes))
        ]
    else:
        copies = piece_copies(units, spec, sources, wholes, in_sems)
    for of_weight in copies:
        for copy in of_weight:
            copy.start()

    def take(at):
        for copy in copies[at]:
            copy.wait()
        if outs[at] is not None:
            send(wholes[at], outs[at])

    def send(source, target):
        kept.append(pltpu.make_async_copy(source, target, out_sems.at[len(kept)]))
        kept[-1].start()

    return take, send


def text_kernel(units, gathered, spec, seq, lengths, text, *refs):
    sources, refs = refs[:gathered], refs[gathered:]
    if spec is None:
        small, refs = refs[:2], refs[2:]
    outs, refs = refs[:11], refs[11:]
    vec, hidden_bias, attended, n1, inverse1, h1, qc, qkv_out, *w_outs = outs
    wholes, (qkv, q, k, v, o, in_sems, out_sems) = refs[:4], refs[4:]
    w_small, w_qkv, w_so, w_cq = wholes
    kept = []
    take, send = take_weights(
        units, spec, sources, wholes, (None, *w_outs), in_sems, out_sems, kept
    )
    take(0)
    if spec is None:
        vec[...], hidden_bias[...] = small[0][...], small[1][...]
    else:
        small_rows_kernel(w_small.at[0, 0], vec, hidden_bias, text.shape[1] // 8)
    take(1)
    self_kernel(seq, lengths, text, w_qkv, vec, qkv, attended, q, k, v, o)
    send(qkv, qkv_out)
    take(2)
    take(3)
    first_norm_kernel(seq, attended, text, w_so, w_cq, vec, n1, inverse1, h1, qc, o)
    for copy in kept:
        copy.wait()


def patch_kernel(units, gathered, spec, seq, patches, micro_rows, slots, qc, n1, vec, *refs):
    sources, held, refs = refs[:gathered], refs[gathered : gathered + 4], refs[gathered + 4 :]
    (oc, n2, inverse2, h2, kv_out, pixels_out, *w_outs), refs = refs[:8], refs[8:]
    wholes, (kv, pixels, q, o, in_sems, pixel_sems, out_sems) = refs[:2], refs[2:]
    w_kv, w_co = wholes
    pixel_copies = [
        pltpu.make_async_copy(image, pixels.at[at], pixel_sems.at[at])
        for at, image in enumerate(held)
    ]
    for copy in pixel_copies:
        copy.start()
    kept = []
    take, send = take_weights(units, spec, sources, wholes, w_outs, in_sems, out_sems, kept)
    for copy in pixel_copies:
        copy.wait()
    send(pixels, pixels_out)
    take(0)
    image_kernel(pixels, w_kv, vec, kv)
    send(kv, kv_out)
    take(1)
    cross_kernel(
        seq, patches, micro_rows, slots, qc, kv, n1, w_co, vec, oc, n2, inverse2, h2, q, o
    )
    for copy in kept:
        copy.wait()


def hidden_weights(w, block, in_units):
    core, unit = divmod(block, in_units)
    depth = w.shape[3] // 2 // in_units
    return w[:, :, core, unit * depth : (unit + 1) * depth].reshape(-1, LANES)


def ffn_kernel(
    gathered, spec, in_units, seq, lengths, h2, bias, n2, cot, vec, *refs
):
    sources, refs = refs[:gathered], refs[gathered:]
    out, dz, df, rows_out, active, slope, w_out, w, total, in_sems, out_sem = refs
    if spec is None:
        copies = [pltpu.make_async_copy(sources[0], w, in_sems.at[0])]
    else:
        copies = [
            pltpu.make_async_copy(
                source.at[pl.ds(first, w.shape[3])],
                w.at[z_from * 2 + y_from, x_from, core_from],
                in_sems.at[at],
            )
            for at, (source, first, z_from, y_from, x_from, core_from) in enumerate(
                piece_places(spec, sources)
            )
        ]
    for copy in copies:
        copy.start()
    for copy in copies:
        copy.wait()
    keep = pltpu.make_async_copy(w, w_out, out_sem.at[0])
    keep.start()
    for block in range(2 * in_units):
        columns = slice(block * LANES, (block + 1) * LANES)
        pre = dot(h2[...], hidden_weights(w, block, in_units)) + bias[block : block + 1]
        cumulative = 0.5 * (1.0 + lax.erf(pre * ROOT_HALF))
        active[:, columns] = low(pre * cumulative)
        slope[:, columns] = low(cumulative + pre * INV_ROOT_TAU * jnp.exp(-0.5 * pre * pre))
    half_rows = w.shape[3] // 2
    for c in range(2):
        columns = slice(c * LANES, (c + 1) * LANES)
        made = None
        for part in range(4):
            weights = w[2 * part : 2 * part + 2, :, c, half_rows:].reshape(-1, LANES)
            depth = weights.shape[0]
            term = dot(active[:, part * depth : (part + 1) * depth], weights)
            made = term if made is None else made + term
        total[:, columns] = made

    def step(r, sums):
        rows = pl.ds(pl.multiple_of(r * seq, 8), seq)
        second = n2[rows, :] * vec[G_2 : G_2 + 1] + vec[B_N2 : B_N2 + 1]
        made, scale = norm_parts(second + total[rows, :] + vec[B_FO : B_FO + 1])
        out[r] = low(made * vec[G_3 : G_3 + 1] + vec[B_N3 : B_N3 + 1])
        valid = lax.broadcasted_iota(jnp.int32, made.shape, 0) < lengths[r]
        upstream = jnp.where(valid, wide(cot[r]), 0.0)
        back = norm_back(upstream, made, scale, vec[G_3 : G_3 + 1])
        dz[rows, :] = back
        gain, shift, lowered = sums
        return (
            gain + row_sum(upstream * made),
            shift + row_sum(upstream),
            lowered + row_sum(wide(low(back))),
        )

    zero = jnp.zeros((1, total.shape[1]), F32)
    sums = lax.fori_loop(0, out.shape[0], step, (zero, zero, zero), unroll=2)
    df[...] = low(dz[...])
    for j in range(3):
        rows_out[j : j + 1] = sums[j]
    rows_out[3:8] = jnp.zeros((5, total.shape[1]), F32)
    keep.wait()


def norm_back_rows(total, dz_ref, normed, inverse, gain, dz, low_ref, rows_out, step_rows):
    def step(r, sums):
        rows = pl.ds(pl.multiple_of(r * step_rows, 8), step_rows)
        upstream = total[rows, :] + dz_ref[rows, :]
        made = normed[rows, :]
        back = norm_back(upstream, made, inverse[rows, :], gain)
        dz[rows, :] = back
        return (
            sums[0] + row_sum(upstream * made),
            sums[1] + row_sum(upstream),
            sums[2] + row_sum(wide(low(back))),
        )

    zero = jnp.zeros((1, total.shape[1]), F32)
    sums = lax.fori_loop(0, total.shape[0] // step_rows, step, (zero, zero, zero))
    low_ref[...] = low(dz[...])
    for j in range(3):
        rows_out[j : j + 1] = sums[j]
    rows_out[3:8] = jnp.zeros((5, total.shape[1]), F32)


def hidden_back_kernel(
    seq, df, wout, win, slope, dz3, n2, inverse, vec, du, bias_out, dz2, dac, rows_out, total
):
    i = pl.program_id(0)

    @pl.when(i == 0)
    def _():
        total[...] = jnp.zeros_like(total)

    raw = dot_last(df[:, :LANES], wout[0, :, 0].reshape(-1, LANES))
    raw = raw + dot_last(df[:, LANES:], wout[0, :, 1].reshape(-1, LANES))
    made = low(raw * wide(slope[...]))
    du[...] = made
    bias_out[pl.ds(i, 1), :] = row_sum(wide(made))
    total[...] += dot_last(made, win[:, :, 0].reshape(-1, LANES))

    @pl.when(i == pl.num_programs(0) - 1)
    def _():
        norm_back_rows(
            total, dz3, n2, inverse, vec[G_2 : G_2 + 1], dz2, dac, rows_out, seq
        )


def cross_back_kernel(
    seq, patches, micro_rows, slots, dac, qc, kv, wco, dqc, dkv_out, dkv, q, do, dq
):
    q[...] = wide(qc[...]) * 0.125
    do[...] = wide(
        low(dot_last(dac[:, :LANES], wco[0, 0]) + dot_last(dac[:, LANES:], wco[1, 0]))
    )
    dkv[...] = jnp.zeros_like(dkv)
    tokens = qc.shape[0]
    padded = kv.shape[3]
    there = lax.broadcasted_iota(jnp.int32, (4 * seq, padded), 1) < patches

    def step(r, _):
        rows = pl.ds(pl.multiple_of(r * seq, 8), seq)
        slot, m = slots[r], r // micro_rows
        asked = [heads_apart(q[rows, c]) for c in quads()]
        came = [heads_apart(do[rows, c]) for c in quads()]
        keys = [kv[slot, 0, m, :, c] for c in quads()]
        values = [kv[slot, 1, m, :, c] for c in quads()]
        scores = [dot_last(a, key) for a, key in zip(asked, keys)]
        backs = [dot_last(d, value) for d, value in zip(came, values)]
        weights = [softmax(jnp.where(there, score, -jnp.inf)) for score in scores]
        backs = [score_back(w, b) for w, b in zip(weights, backs)]
        queries = [heads_joined(dot(b, key)) for b, key in zip(backs, keys)]
        key_parts = [dot_first(b, a) for b, a in zip(backs, asked)]
        value_parts = [dot_first(low(w), d) for w, d in zip(weights, came)]
        for j, c in enumerate(quads()):
            dq[rows, c] = queries[j] * 0.125
            dkv[0, slot, m, :, c] += key_parts[j]
            dkv[1, slot, m, :, c] += value_parts[j]
        return 0

    lax.fori_loop(0, tokens // seq, step, 0, unroll=2)
    dqc[...] = low(dq[...])
    dkv_out[...] = low(dkv[...])


def first_back_kernel(seq, dqc, wcq, dz2, n1, inverse, vec, dz1, da, rows_out, total):
    total[...] = dot_last(dqc[:, :LANES], wcq[0, 0]) + dot_last(dqc[:, LANES:], wcq[1, 0])
    norm_back_rows(total, dz2, n1, inverse, vec[G_1 : G_1 + 1], dz1, da, rows_out, seq)
    rows_out[3:4] = row_sum(wide(dqc[...]))


def self_back_kernel(seq, lengths, da, qkv, wso, dqkv, rows_out, q, k, v, do, dq, dk, dv):
    q[...] = wide(qkv[0]) * 0.125
    k[...] = wide(qkv[1])
    v[...] = wide(qkv[2])
    do[...] = wide(low(dot_last(da[:, :LANES], wso[0, 0]) + dot_last(da[:, LANES:], wso[1, 0])))
    tokens = da.shape[0]

    def step(r, _):
        rows = pl.ds(pl.multiple_of(r * seq, 8), seq)
        valid = lax.broadcasted_iota(jnp.int32, (4 * seq, seq), 1) < lengths[r]
        asked = [heads_apart(q[rows, c]) for c in quads()]
        came = [heads_apart(do[rows, c]) for c in quads()]
        keys = [low(k[rows, c]) for c in quads()]
        values = [low(v[rows, c]) for c in quads()]
        scores = [dot_last(a, key) for a, key in zip(asked, keys)]
        backs = [dot_last(d, value) for d, value in zip(came, values)]
        weights = [softmax(jnp.where(valid, score, -jnp.inf)) for score in scores]
        backs = [score_back(w, b) for w, b in zip(weights, backs)]
        queries = [heads_joined(dot(b, key)) for b, key in zip(backs, keys)]
        key_parts = [dot_first(b, a) for b, a in zip(backs, asked)]
        value_parts = [dot_first(low(w), d) for w, d in zip(weights, came)]
        for j, c in enumerate(quads()):
            dq[rows, c] = queries[j] * 0.125
            dk[rows, c] = key_parts[j]
            dv[rows, c] = value_parts[j]
        return 0

    lax.fori_loop(0, tokens // seq, step, 0, unroll=2)
    for j, made in enumerate((dq, dk, dv)):
        dqkv[j] = low(made[...])
    rows_out[0:1] = row_sum(wide(dqkv[0]))
    rows_out[1:2] = row_sum(wide(dqkv[2]))
    rows_out[2:8] = jnp.zeros((6, q.shape[1]), F32)


def text_grad_kernel(dz1, dqkv, w_ref, out, total):
    total[...] = dz1[...]
    for j in range(3):
        for c in range(2):
            total[...] += dot_last(dqkv[j, :, c * LANES : (c + 1) * LANES], w_ref[c, j])
    seq = out.shape[1]
    for r in range(out.shape[0]):
        out[r] = low(total[r * seq : (r + 1) * seq, :])


def patch_grad_kernel(dkv, w_ref, kept, sent, rows_out):
    _, slots, images, padded, width = dkv.shape
    rows = images * padded
    total = jnp.zeros((1, width), F32)
    for slot in range(slots):
        made = None
        for j in range(2):
            grad = dkv[j, slot].reshape(rows, width)
            for c in range(2):
                term = dot_last(grad[:, c * LANES : (c + 1) * LANES], w_ref[c, j])
                made = term if made is None else made + term
        out = sent if slot % 2 else kept
        out[slot // 2] = low(made).reshape(images, padded, w_ref.shape[2])
        total = total + row_sum(wide(grad))
    rows_out[0:1] = total
    rows_out[1:8] = jnp.zeros((7, width), F32)


def on_device(
    text_input,
    patch_input,
    text_lengths,
    image_of_row,
    cotangent,
    self_qkv,
    self_out,
    cross_q,
    cross_kv,
    cross_out,
    ffn_in,
    ffn_out,
    biases,
    norm_gains,
    ffn_bias,
):
    dp = lax.axis_size(DP)
    micros, row_count, seq, width = text_input.shape
    patches, patch_width = patch_input.shape[2:]
    rows_all = micros * row_count
    tokens = rows_all * seq
    hidden = ffn_in.shape[1]
    padded = -(-patches // 16) * 16
    images = micros * patch_input.shape[1]

    part = biases.shape[1]
    small = jnp.concatenate((biases, norm_gains, ffn_bias.reshape(-1, part)))
    small_rows = small.shape[0]
    wide_rows = biases.shape[0] + norm_gains.shape[0]
    small = jnp.pad(small, ((0, 2 * PAD_ROWS - small_rows), (0, LANES - part)))
    small = jnp.broadcast_to(small.reshape(2, PAD_ROWS, LANES), (2, 2, PAD_ROWS, LANES))

    half = width // dp // 2
    half_v = cross_kv.shape[1] // 2
    in_units = hidden // (2 * LANES)
    text_group = (
        (small, self_qkv, self_out, cross_q),
        ((1, PAD_ROWS), (3, half), (1, half), (1, half)),
    )
    patch_group = ((cross_kv, cross_out), ((2, half_v), (1, half)))
    hidden_group = ((ffn_in, ffn_out), ((in_units, half), (1, ffn_out.shape[0] // 2)))

    text = text_input.reshape(tokens, width)
    pixels = call(pixel_kernel, shape((images, padded, patch_width)), [VMEM])(
        patch_input.reshape(images, patches, patch_width)
    )
    lengths = text_lengths.reshape(-1)
    slots = image_of_row.reshape(-1) ^ lax.axis_index(STREAM)
    flat = (tokens, width)
    full = pltpu.VMEM(flat, F32)
    flops = 2 * tokens * width * width
    steps = hidden // LANES
    chunks = hidden // width
    kv_shape = (4, 2, images, padded, width)
    in_block = pl.BlockSpec(
        (8, 2, 1, width // 16, LANES), lambda i: (0, 0, i // in_units, i % in_units, 0)
    )
    v = types.SimpleNamespace()

    bf16 = jnp.bfloat16

    def pixel_steps():
        (v.across,) = yield [(pixels, STREAM, ACROSS)]
        v.beside, v.apart = yield [(pixels, STREAM, CORE), (v.across, STREAM, CORE)]

    def run_text(tie, sources, spec=None, small_inputs=()):
        units = text_group[1]
        wholes = [(2, 1, 16 * PAD_ROWS, LANES)]
        wholes += [(2, count, depth * 2 * dp, LANES) for count, depth in units[1:]]
        outs = [
            shape((16, width), F32), shape((steps, LANES), F32), shape(flat), shape(flat, F32),
            shape((tokens, 1), F32), shape(flat), shape(flat), shape((3, *flat)),
            *[shape(dims) for dims in wholes[1:]],
        ]
        (
            v.vec, v.hidden_bias, v.attended, v.n1, v.inverse1, v.h1, v.qc, v.qkv,
            v.w_qkv, v.w_so, v.w_cq,
        ) = call(
            functools.partial(text_kernel, units, len(sources), spec, seq),
            outs,
            [SMEM, VMEM] + [ANY] * len(sources) + [VMEM] * len(small_inputs),
            [
                *[pltpu.VMEM(dims, bf16) for dims in wholes],
                pltpu.VMEM((3, *flat), bf16), full, full, full, full,
                pltpu.SemaphoreType.DMA((32 * len(units),)), pltpu.SemaphoreType.DMA((4,)),
            ],
            out_specs=[VMEM] * 7 + [ANY] * 4,
            mib=60,
            flops=8 * flops,
        )(lengths, tie(text), *sources, *small_inputs)
        return v.qc

    def run_patch(tie, sources, spec=None):
        units = patch_group[1]
        wholes = [(2, count, depth * 2 * dp, LANES) for count, depth in units]
        pixels_shape = (4, images, padded, patch_width)
        outs = [
            shape(flat), shape(flat, F32), shape((tokens, 1), F32), shape(flat),
            shape(kv_shape), shape(pixels_shape), *[shape(dims) for dims in wholes],
        ]
        v.oc, v.n2, v.inverse2, v.h2, v.kv, pixels_all, v.w_kv, v.w_co = call(
            functools.partial(patch_kernel, units, len(sources), spec, seq, patches, row_count),
            outs,
            [SMEM, VMEM, VMEM, VMEM] + [ANY] * (len(sources) + 4),
            [
                *[pltpu.VMEM(dims, bf16) for dims in wholes],
                pltpu.VMEM(kv_shape, bf16), pltpu.VMEM(pixels_shape, bf16), full, full,
                pltpu.SemaphoreType.DMA((32 * len(units),)), pltpu.SemaphoreType.DMA((4,)),
                pltpu.SemaphoreType.DMA((4,)),
            ],
            out_specs=[VMEM] * 4 + [ANY] * 4,
            mib=60,
            flops=18 * flops,
        )(slots, tie(v.qc), v.n1, v.vec, *sources, pixels, v.beside, v.across, v.apart)
        v.pixels_all = pixels_all.reshape(-1, patch_width)
        return v.h2

    def run_ffn(tie, sources, spec=None):
        w_shape = (8, 2, 2, hidden // 8, LANES)
        v.out_rows, v.dz3, v.df, v.sums3, v.active, v.slope, v.w_hidden = call(
            functools.partial(ffn_kernel, len(sources), spec, in_units, seq),
            [
                shape((rows_all, seq, width)), shape(flat, F32), shape(flat),
                shape((8, width), F32), shape((tokens, hidden)), shape((tokens, hidden)),
                shape(w_shape),
            ],
            [SMEM] + [VMEM] * 5 + [ANY] * len(sources),
            [
                pltpu.VMEM(w_shape, bf16), full, pltpu.SemaphoreType.DMA((32,)),
                pltpu.SemaphoreType.DMA((1,)),
            ],
            out_specs=[VMEM] * 6 + [ANY],
            flops=8 * flops,
        )(
            lengths, tie(v.h2), v.hidden_bias, v.n2,
            cotangent.reshape(rows_all, seq, width), v.vec, *sources,
        )
        return v.df

    def run_hidden_back(tie):
        v.du, v.hidden_bias_grad, v.dz2, v.dac, v.sums2 = call(
            functools.partial(hidden_back_kernel, seq),
            [
                shape((tokens, hidden)),
                shape((steps, LANES), F32),
                shape(flat, F32),
                shape(flat),
                shape((8, width), F32),
            ],
            [
                VMEM,
                pl.BlockSpec((1, 2, 2, hidden // 16, LANES), lambda i: (i, 0, 0, 1, 0)),
                in_block,
                pl.BlockSpec((tokens, LANES), lambda i: (0, i)),
                VMEM,
                VMEM,
                VMEM,
                VMEM,
            ],
            [full],
            out_specs=[pl.BlockSpec((tokens, LANES), lambda i: (0, i)), VMEM, VMEM, VMEM, VMEM],
            grid=(steps,),
            flops=8 * flops,
        )(
            tie(v.df), v.w_hidden, v.w_hidden, v.slope, v.dz3, v.n2, v.inverse2,
            v.vec,
        )
        return v.dac

    def run_cross_back(tie):
        v.dqc, v.dkv_all = call(
            functools.partial(cross_back_kernel, seq, patches, row_count),
            [shape(flat), shape((2, 4, images, padded, width))],
            [SMEM, VMEM, VMEM, VMEM, VMEM],
            [pltpu.VMEM((2, 4, images, padded, width), F32), full, full, full],
            flops=4 * flops,
        )(slots, tie(v.dac), v.qc, v.kv, v.w_co)
        return v.dqc

    def patch_steps():
        (came,) = yield [(v.patch_sent, STREAM, CORE)]
        made = wide(v.patch_kept) + wide(came)
        (across,) = yield [(low(made[1]), STREAM, ACROSS)]
        v.patch_rows = low(made[0] + wide(across))[:, :patches].reshape(patch_input.shape)

    def run_first_back(tie):
        v.dz1, v.da, v.sums1 = call(
            functools.partial(first_back_kernel, seq),
            [shape(flat, F32), shape(flat), shape((8, width), F32)],
            [VMEM] * 6,
            [full],
            flops=flops,
        )(tie(v.dqc), v.w_cq, v.dz2, v.n1, v.inverse1, v.vec)
        return v.da

    def run_self_back(tie):
        v.dqkv, v.sums0 = call(
            functools.partial(self_back_kernel, seq),
            [shape((3, *flat)), shape((8, width), F32)],
            [SMEM, VMEM, VMEM, VMEM],
            [full] * 7,
            flops=4 * flops,
        )(lengths, tie(v.da), v.qkv, v.w_so)
        return v.dqkv

    def run_patch_grad(tie):
        v.patch_kept, v.patch_sent, v.sums_kv = call(
            patch_grad_kernel,
            [shape((2, images, padded, patch_width))] * 2 + [shape((8, width), F32)],
            [VMEM] * 2,
            flops=16 * flops,
        )(tie(v.dkv_all), v.w_kv)
        return v.patch_sent

    def run_text_grad(tie):
        v.text_rows = call(
            text_grad_kernel,
            shape((rows_all, seq, width)),
            [VMEM] * 3,
            [full],
            flops=3 * flops,
        )(tie(v.dz1), v.dqkv, v.w_qkv)
        return v.text_rows

    def small_grads():
        sums0, sums1, sums2, sums3, sums_kv = v.sums0, v.sums1, v.sums2, v.sums3, v.sums_kv
        grads = jnp.concatenate(
            (
                sums0[0:2], sums1[2:3], sums1[1:2], sums1[3:4], sums_kv[0:1], sums2[2:3],
                sums2[1:2], sums3[2:3], sums3[1:2], sums1[0:1], sums2[0:1], sums3[0:1],
            )
        )
        return jnp.concatenate(
            (
                grads.reshape(wide_rows, dp, part).transpose(1, 0, 2),
                v.hidden_bias_grad.reshape(dp, -1, part),
            ),
            axis=1,
        )

    def run_all(moves):
        mover = Mover(moves)
        while not mover.done:
            mover.give([lax.ppermute(array, axis, hops) for array, axis, hops in mover.requests])

    if not special_mesh():
        def free(array):
            return array

        w_small, *wholes = gather_plain(*text_group)
        patch_wholes = gather_plain(*patch_group)
        values = wide(w_small[0, 0].reshape(dp, 2 * PAD_ROWS, LANES)[:, :small_rows, :part])
        vec = values[:, :wide_rows].transpose(1, 0, 2).reshape(wide_rows, width)
        vec = jnp.pad(vec, ((0, 16 - wide_rows), (0, 0)))
        hidden_bias = values[:, wide_rows:].reshape(-1, LANES)
        w_small = w_small[:, :, : 16 * PAD_ROWS]
        w_in = lax.all_gather(ffn_in, DP, axis=0, tiled=True)
        w_out = lax.all_gather(ffn_out, DP, axis=0, tiled=True)
        w_in = w_in.reshape(8, 2, width // 16, 2, in_units, LANES).transpose(0, 1, 3, 4, 2, 5)
        w_in = w_in.reshape(8, 2, 2, -1, LANES)
        w_out = w_out.reshape(8, 2, hidden // 16, 2, LANES).transpose(0, 1, 3, 2, 4)
        w_hidden = jnp.concatenate((w_in, w_out), axis=3)
        run_all(pixel_steps())
        run_text(free, (w_small, *wholes), None, (vec, hidden_bias))
        run_patch(free, patch_wholes)
        run_ffn(free, (w_hidden,))
        for work in (run_hidden_back, run_cross_back, run_patch_grad):
            work(free)
        run_all(patch_steps())
        for work in (run_first_back, run_self_back, run_text_grad):
            work(free)
        s_out, s_in, s_co, s_cq, s_so, s_kv, s_qkv = reduce_plain(
            (
                (v.active, v.df), (v.h2, v.du), (v.oc, v.dac), (v.h1, v.dqc),
                (v.attended, v.da), (v.pixels_all, v.dkv_all.reshape(2, -1, width)), (text, v.dqkv),
            )
        )
        s_small = lax.psum_scatter(low(small_grads()), DP, scatter_dimension=0, tiled=True)
        s_small = wide(lax.psum(s_small, STREAM))[0]
        s_biases = s_small[: biases.shape[0]]
        s_gains = s_small[biases.shape[0] : wide_rows]
        s_hidden_bias = s_small[wide_rows:]
    else:
        clock = Clock()
        gather_text, gather_patch, gather_hidden = (
            Mover(gather_steps(*pack_group(*group)), pieces=True)
            for group in (text_group, patch_group, hidden_group)
        )
        move_pixels = Mover(pixel_steps())
        clock.step([gather_text, move_pixels])
        clock.step([gather_text, gather_patch])
        clock.step([gather_hidden, gather_text, gather_patch])
        clock.step(
            [gather_hidden, gather_patch, move_pixels], [lambda tie: run_text(tie, *piece_sources(gather_text.result, tie))]
        )
        clock.step([gather_hidden], [lambda tie: run_patch(tie, *piece_sources(gather_patch.result, tie))])
        clock.step([gather_hidden], [lambda tie: run_ffn(tie, *piece_sources(gather_hidden.result, tie))])

        out_group, in_group, mid_group, last_group = Group(), Group(), Group(), Group()

        def begin_out(tie):
            return out_group.sibling(tie, (v.active, v.df))

        def begin_in(tie):
            return in_group.sibling(tie, (v.h2, v.du))

        def begin_mid(tie):
            return mid_group.sibling(
                tie,
                (v.oc, v.dac),
                (v.h1, v.dqc),
                (v.attended, v.da),
                (v.pixels_all, v.dkv_all.reshape(2, -1, width)),
            )

        def begin_last(tie):
            return last_group.sibling(tie, (text, v.dqkv))

        def own_last(tie):
            return last_group.own(
                tie, (v.sums0, v.sums1, v.sums2, v.sums3, v.sums_kv, v.hidden_bias_grad)
            )

        clock.step([], [begin_out])
        clock.step([out_group.core_move()], [run_hidden_back, out_group.own], eager=True)
        move_out = out_group.move()
        clock.step([], [begin_in])
        clock.step(
            [move_out, in_group.core_move()],
            [run_cross_back, run_first_back, in_group.own, begin_mid],
            eager=True,
        )
        move_in = in_group.move()
        clock.step(
            [move_out, move_in, mid_group.core_move()],
            [run_self_back, run_patch_grad, mid_group.own, begin_last],
            eager=True,
        )
        move_mid, move_patch = mid_group.move(), Mover(patch_steps())
        clock.step(
            [move_out, move_in, move_mid, last_group.core_move(), move_patch],
            [own_last, run_text_grad],
            eager=True,
        )
        move_last = last_group.move()
        movers = [move_out, move_in, move_mid, move_last, move_patch]
        results = {}

        small_shapes = [
            shape((rows, part), F32)
            for rows in (biases.shape[0], norm_gains.shape[0], small_rows - wide_rows)
        ]

        def unpack(group, mover):
            def work(tie):
                results[mover] = group.unpack(
                    (tie(mover.result[0]), mover.result[1]),
                    small_shapes if group is last_group else (),
                )
                return results[mover]
            return work

        groups = [
            (out_group, move_out), (in_group, move_in), (mid_group, move_mid), (last_group, move_last)
        ]
        def ready():
            return [
                unpack(group, mover)
                for group, mover in groups
                if mover.done and mover not in results
            ]

        while not all(mover.done for mover in movers):
            clock.step(movers, ready, eager=True)
        for work in ready():
            work(clock.tie)
        (s_out,), (s_in,) = results[move_out], results[move_in]
        s_co, s_cq, s_so, s_kv = results[move_mid]
        s_qkv, s_biases, s_gains, s_hidden_bias = results[move_last]
    return (
        v.out_rows.reshape(text_input.shape),
        v.text_rows.reshape(text_input.shape),
        v.patch_rows,
        s_qkv,
        s_so,
        s_cq,
        s_kv,
        s_co,
        s_in,
        s_out,
        s_biases,
        s_gains,
        s_hidden_bias.reshape(-1),
    )


def solution(mesh):
    placed = (
        P(None, (DP, STREAM), None, None),
        P(None, (DP, STREAM), None, None),
        P(None, (DP, STREAM)),
        P(None, (DP, STREAM)),
        P(None, (DP, STREAM), None, None),
        P(None, DP, None),
        P(DP, None),
        P(DP, None),
        P(None, DP, None),
        P(DP, None),
        P(DP, None),
        P(DP, None),
        P(None, DP),
        P(None, DP),
        P(DP),
    )
    return jax.shard_map(
        on_device,
        mesh=mesh,
        in_specs=placed,
        out_specs=(
            P(None, (DP, STREAM), None, None),
            P(None, (DP, STREAM), None, None),
            P(None, (DP, STREAM), None, None),
            P(None, DP, None),
            P(DP, None),
            P(DP, None),
            P(None, DP, None),
            P(DP, None),
            P(DP, None),
            P(DP, None),
            P(None, DP),
            P(None, DP),
            P(DP),
        ),
        check_vma=False,
    )
```

profile of v0, /device:TPU:1, one launch (start us, length us, event | category | flops | bytes accessed | tf_op | source)
XLA Modules:
  0.0 317.1 jit_solution(2569336568286960340)
XLA Ops:
  1.5 1.3 copy.31
  4.8 2.0 collective-permute-start.4
  6.8 1.3 collective-permute-start
  8.1 1.2 collective-permute-start.3
  9.4 2.3 collective-permute-start.1
  11.8 8.1 %collective-permute-done.1.refs_3_ = bf16[256,384]{1,0:T(8,128)(2,1)S(1)} collective-permute-done((bf16[256,384]{1,0:T(8,128)(2,1)S(1)}, bf16[256,384]{1,0:T(8,128)(2,1)S(1)}, u32[]{:S(2)}, u32[]{:S(2)}) %collective-permute-start.1) | collective-permute-done | bytes 196640 | tf_op jit(solution)/shard_map/ppermute | solution.py:130
  19.8 7.1 %collective-permute-done.2.refs_4_ = bf16[256,384]{1,0:T(8,128)(2,1)S(1)} collective-permute-done((bf16[256,384]{1,0:T(8,128)(2,1)S(1)}, bf16[256,384]{1,0:T(8,128)(2,1)S(1)}, u32[]{:S(2)}, u32[]{:S(2)}) %collective-permute-start.2) | collective-permute-done | bytes 196640 | tf_op jit(solution)/shard_map/ppermute | solution.py:130
  27.8 1.2 collective-permute-start.5
  29.3 1.3 collective-permute-start.8
  30.6 2.2 collective-permute-start.9
  33.0 1.8 collective-permute-done.8.refs_3_
  34.9 5.4 %collective-permute-done.9.refs_4_ = bf16[176,384]{1,0:T(8,128)(2,1)S(1)} collective-permute-done((bf16[176,384]{1,0:T(8,128)(2,1)S(1)}, bf16[176,384]{1,0:T(8,128)(2,1)S(1)}, u32[]{:S(2)}, u32[]{:S(2)}) %collective-permute-start.9) | collective-permute-done | bytes 135200 | tf_op jit(solution)/shard_map/ppermute | solution.py:130
  40.7 5.8 %collective-permute-done.5.refs_6_.refs_2_ = bf16[1120,384]{1,0:T(8,128)(2,1)S(1)} collective-permute-done((bf16[1120,384]{1,0:T(8,128)(2,1)S(1)}, bf16[1120,384]{1,0:T(8,128)(2,1)S(1)}, u32[]{:S(2)}, u32[]{:S(2)}) %collective-permute-start.5) | collective-permute-done | bytes 860192 | tf_op jit(solution)/shard_map/ppermute | solution.py:130
  46.5 1.3 constant_dynamic-slice_fusion.1
  48.1 1.3 collective-permute-start.13
  49.7 1.2 collective-permute-start.11
  50.9 2.3 collective-permute-start.12
  53.2 12.3 %collective-permute-done.11.refs_3_ = bf16[384,384]{1,0:T(8,128)(2,1)S(1)} collective-permute-done((bf16[384,384]{1,0:T(8,128)(2,1)S(1)}, bf16[384,384]{1,0:T(8,128)(2,1)S(1)}, u32[]{:S(2)}, u32[]{:S(2)}) %collective-permute-start.11) | collective-permute-done | bytes 294944 | tf_op jit(solution)/shard_map/ppermute | solution.py:130
  65.5 7.9 %collective-permute-done.12.refs_4_ = bf16[384,384]{1,0:T(8,128)(2,1)S(1)} collective-permute-done((bf16[384,384]{1,0:T(8,128)(2,1)S(1)}, bf16[384,384]{1,0:T(8,128)(2,1)S(1)}, u32[]{:S(2)}, u32[]{:S(2)}) %collective-permute-start.12) | collective-permute-done | bytes 294944 | tf_op jit(solution)/shard_map/ppermute | solution.py:130
  76.7 5.0 %collective-permute-start.15 = (bf16[512,384]{1,0:T(8,128)(2,1)S(1)}, bf16[512,384]{1,0:T(8,128)(2,1)S(1)}, u32[]{:S(2)}, u32[]{:S(2)}) collective-permute-start(bf16[512,384]{1,0:T(8,128)(2,1)S(1)} %bitcast.212), channel_id=1, source_target_pairs={{0,1},{1,0},{2,3},{3,2},{4,5},{5,4},{6,7},{7,6},{8,9},{9,8},{10,11... | collective-permute-start | bytes 1179656 | tf_op jit(solution)/shard_map/ppermute | solution.py:71
  84.3 2.7 collective-permute-done.16.refs_10_
  87.1 1.3 collective-permute-start.23
  92.9 13.5 %shard_map.250 = (f32[16,768]{1,0:T(8,128)}, f32[8,384]{1,0:T(8,128)}, bf16[320,768]{1,0:T(8,128)(2,1)}, f32[320,768]{1,0:T(8,128)}, f32[320,1]{1,0:T(8,128)}, /...) custom-call(s32[8]{0:T(128)} %reshape.233.lengths, ...), custom_call_target="tpu_custom_call" | custom-call | flops 3019898880 | bytes 4194304 | tf_op jit(solution)/shard_map/pallas_call | solution.py:1138
  106.5 2.7 collective-permute-done.24.refs_8_.refs_5_
  109.2 1.9 collective-permute-done.23.refs_7_.refs_6_
  114.9 2.4 collective-permute-done.28.refs_11_
  117.2 1.3 collective-permute-start.33
  120.8 17.1 %shard_map.251 = (bf16[320,768]{1,0:T(8,128)(2,1)}, f32[320,768]{1,0:T(8,128)}, f32[320,1]{1,0:T(8,128)}, bf16[320,768]{1,0:T(8,128)(2,1)}, bf16[4,2,2,160,768]{...) custom-call(s32[8]{0:T(128)} %xor.10.slots, ...), custom_call_target="tpu_custom_call" | custom-call | flops 6794772480 | bytes 4194304 | tf_op jit(solution)/shard_map/pallas_call | solution.py:1161
  139.9 1.5 collective-permute-done.35.refs_11_
  146.3 1.3 copy-done.14
  148.8 11.3 %shard_map.252 = (bf16[8,40,768]{2,1,0:T(8,128)(2,1)}, f32[320,768]{1,0:T(8,128)S(1)}, bf16[320,768]{1,0:T(8,128)(2,1)S(1)}, f32[8,768]{1,0:T(8,128)S(1)}, bf16[...) custom-call(s32[8]{0:T(128)S(1)} %copy-done.33, ...), custom_call_target="tpu_custom_call" | custom-call | flops 3019898880 | bytes 4194304 | tf_op jit(solution)/shard_map/pallas_call | solution.py:1180
  160.1 1.7 shard_map.253
  162.2 10.3 %shard_map.254 = (bf16[320,3072]{1,0:T(8,128)(2,1)S(1)}, f32[8,384]{1,0:T(8,128)S(1)}, f32[320,768]{1,0:T(8,128)S(1)}, bf16[320,768]{1,0:T(8,128)(2,1)S(1)}, f32[8,768]{1,0:T(8,128)S(1)}) custom-call(bf16[320,768]{1,0:T(8,128)(2,1)S(1)} %get-tuple-element.376.refs_1_.df, bf16[8,2,2,384,384]{4,3,2,1,0:T(8,128)(2,1)S(1)} %get-tuple-element.377.wout.win, ...), custom_call_target="tpu_custom_call" | custom-call | flops 3019898880 | bytes 4194304 | tf_op jit(solution)/shard_map/pallas_call | solution.py:1201
  172.5 1.4 shard_map.256
  173.9 1.9 shard_map.255
  177.5 8.8 %shard_map.257 = (bf16[320,768]{1,0:T(8,128)(2,1)S(1)}, bf16[2,4,2,160,768]{4,3,2,1,0:T(8,128)(2,1)S(1)}) custom-call(s32[8]{0:T(128)S(1)} %copy-done.34, bf16[320,768]{1,0:T(8,128)(2,1)S(1)} %get-tuple-element.389.dac.refs_1_, bf16[320,768]{1,0:T(8,128)(2,1)S(1)} %copy-done.23, bf16[4,2,2,160,768]{4,3,2,1,0:T(8,128)(2,1)S(1)} %copy-done.2, ...), custom_call_target="tpu_custom_call" | custom-call | flops 1509949440 | bytes 4194304 | tf_op jit(solution)/shard_map/pallas_call | solution.py:1231
  186.4 2.1 shard_map.258
  188.5 3.4 %shard_map.260 = bf16[8,2,272,384]{3,2,1,0:T(8,128)(2,1)S(1)} custom-call(bf16[320,768]{1,0:T(8,128)(2,1)S(1)} %copy-done.10, bf16[320,768]{1,0:T(8,128)(2,1)S(1)} %get-tuple-element.389.dac.refs_1_, bf16[320,768]{1,0:T(8,128)(2,1)S(1)} %copy-done.9, bf16[320,768]{1,0:T(8,128)(2,1)S(1)} %get-tuple-element.435.dqc.refs_3_, bf16[320,768]{1,0:T(8,128)(2,1)S(1)} %copy-done.8, ...), custom_call_target="tpu_custom_call" | custom-call | flops 2579496960 | bytes 4194304 | tf_op jit(solution)/shard_map/pallas_call | solution.py:555
  192.2 2.0 shard_map.259
  197.3 1.3 collective-permute-start.44
  198.6 5.7 %shard_map.264 = (bf16[2,2,160,1024]{3,2,1,0:T(8,128)(2,1)S(1)}, bf16[2,2,160,1024]{3,2,1,0:T(8,128)(2,1)S(1)}, f32[8,768]{1,0:T(8,128)S(1)}) custom-call(bf16[2,4,2,160,768]{4,3,2,1,0:T(8,128)(2,1)S(1)} %get-tuple-element.457.dkv, bf16[2,2,1024,384]{3,2,1,0:T(8,128)(2,1)S(1)} %copy-done.39), custom_call_target="tpu_custom_call" | custom-call | flops 6039797760 | bytes 4194304 | tf_op jit(solution)/shard_map/pallas_call | solution.py:1267
  204.3 7.1 %shard_map.262 = (bf16[3,320,768]{2,1,0:T(8,128)(2,1)S(1)}, f32[8,768]{1,0:T(8,128)S(1)}) custom-call(s32[8]{0:T(128)S(1)} %copy-done.33, bf16[320,768]{1,0:T(8,128)(2,1)S(1)} %get-tuple-element.453.refs_5_.da, bf16[3,320,768]{2,1,0:T(8,128)(2,1)S(1)} %copy-done.37, bf16[2,1,768,384]{3,2,1,0:T(8,128)(2,1)S(1)} %copy-done.38), custom_call_target="tpu_custom_call" | custom-call | flops 1509949440 | bytes 4194304 | tf_op jit(solution)/shard_map/pallas_call | solution.py:1257
  212.8 1.9 collective-permute-done.44
  215.0 4.0 %shard_map.261 = (bf16[4,272,384]{2,1,0:T(8,128)(2,1)S(1)}, bf16[2,272,384]{2,1,0:T(8,128)(2,1)S(1)}, bf16[2,272,384]{2,1,0:T(8,128)(2,1)S(1)}, bf16[3,272,384]{...) custom-call(bf16[320,768]{1,0:T(8,128)(2,1)S(1)} %copy-done.10, ...), custom_call_target="tpu_custom_call" | custom-call | flops 2579496960 | bytes 4194304 | tf_op jit(solution)/shard_map/pallas_call | solution.py:582
  221.0 2.1 collective-permute-start.48
  223.1 12.1 %collective-permute-done.49 = bf16[928,384]{1,0:T(8,128)(2,1)S(1)} collective-permute-done((bf16[928,384]{1,0:T(8,128)(2,1)S(1)}, bf16[928,384]{1,0:T(8,128)(2,1)S(1)}, u32[]{:S(2)}, u32[]{:S(2)}) %collective-permute-start.49) | collective-permute-done | bytes 712736 | tf_op jit(solution)/shard_map/ppermute | solution.py:130
  235.3 3.2 collective-permute-done.52
  239.8 1.5 shard_map.266
  242.1 2.5 shard_map.265
  244.6 1.4 collective-permute-start.55
  247.3 1.4 collective-permute-start.54
  248.8 6.4 %collective-permute-done.55 = bf16[192,384]{1,0:T(8,128)(2,1)S(1)} collective-permute-done((bf16[192,384]{1,0:T(8,128)(2,1)S(1)}, bf16[192,384]{1,0:T(8,128)(2,1)S(1)}, u32[]{:S(2)}, u32[]{:S(2)}) %collective-permute-start.55) | collective-permute-done | bytes 147488 | tf_op jit(solution)/shard_map/ppermute | solution.py:130
  255.3 1.4 collective-permute-done.56
  256.9 7.5 %collective-permute-done.54 = bf16[1136,384]{1,0:T(8,128)(2,1)S(1)} collective-permute-done((bf16[1136,384]{1,0:T(8,128)(2,1)S(1)}, bf16[1136,384]{1,0:T(8,128)(2,1)S(1)}, u32[]{:S(2)}, u32[]{:S(2)}) %collective-permute-start.54) | collective-permute-done | bytes 872480 | tf_op jit(solution)/shard_map/ppermute | solution.py:130
  269.3 2.1 collective-permute-done.59
  271.6 4.8 %collective-permute-done.58 = bf16[432,384]{1,0:T(8,128)(2,1)S(1)} collective-permute-done((bf16[432,384]{1,0:T(8,128)(2,1)S(1)}, bf16[432,384]{1,0:T(8,128)(2,1)S(1)}, u32[]{:S(2)}, u32[]{:S(2)}) %collective-permute-start.58) | collective-permute-done | bytes 331808 | tf_op jit(solution)/shard_map/ppermute | solution.py:130
  276.7 1.6 collective-permute-start.61
  278.5 4.9 %collective-permute-done.62 = bf16[160,384]{1,0:T(8,128)(2,1)S(1)} collective-permute-done((bf16[160,384]{1,0:T(8,128)(2,1)S(1)}, bf16[160,384]{1,0:T(8,128)(2,1)S(1)}, u32[]{:S(2)}, u32[]{:S(2)}) %collective-permute-start.62) | collective-permute-done | bytes 122912 | tf_op jit(solution)/shard_map/ppermute | solution.py:130
  285.5 8.9 %collective-permute-done.63 = bf16[160,384]{1,0:T(8,128)(2,1)S(1)} collective-permute-done((bf16[160,384]{1,0:T(8,128)(2,1)S(1)}, bf16[160,384]{1,0:T(8,128)(2,1)S(1)}, u32[]{:S(2)}, u32[]{:S(2)}) %collective-permute-start.63) | collective-permute-done | bytes 122912 | tf_op jit(solution)/shard_map/ppermute | solution.py:130
  294.9 7.8 %collective-permute-start.71 = (bf16[2,192,384]{2,1,0:T(8,128)(2,1)S(1)}, bf16[2,192,384]{2,1,0:T(8,128)(2,1)S(1)}, u32[]{:S(2)}, u32[]{:S(2)}) collective-permute-start(bf16[2,192,384]{2,1,0:T(8,128)(2,1)S(1)} %add_convert_fusion.5.mine), channel_id=1, source_target_pairs={{0,1},{1,0},{2,3},{3,2},{4,5},{5,4},{6,7},{7,6},{8,9},{9,8},{10,11... | collective-permute-start | bytes 884744 | tf_op jit(solution)/shard_map/ppermute | solution.py:487
  302.8 4.7 %collective-permute-start.67 = (bf16[2,272,384]{2,1,0:T(8,128)(2,1)S(1)}, bf16[2,272,384]{2,1,0:T(8,128)(2,1)S(1)}, u32[]{:S(2)}, u32[]{:S(2)}) collective-permute-start(bf16[2,272,384]{2,1,0:T(8,128)(2,1)S(1)} %add_convert_fusion.3.mine), channel_id=1, source_target_pairs={{0,1},{1,0},{2,3},{3,2},{4,5},{5,4},{6,7},{7,6},{8,9},{9,8},{10,11... | collective-permute-start | bytes 1253384 | tf_op jit(solution)/shard_map/ppermute | solution.py:487
  307.7 2.3 collective-permute-start.65
  310.3 1.4 copy.29
  315.6 1.3 shard_map.268
  (314 shorter events, 54.8 us)
Async XLA Ops:
  4.8 22.2 %collective-permute-start.4 = (bf16[2,160,1024]{2,1,0:T(8,128)(2,1)}, bf16[2,160,1024]{2,1,0:T(8,128)(2,1)}, u32[]{:S(2)}, u32[]{:S(2)}) collective-permute-start(bf16[2,160,1024]{2,1,0:T(8,128)(2,1)} %shard_map.248.refs_17_), channel_id=1, source_target_pairs={{0,2},{2,0},{1,3},{3,1},{4,6},{6,4},{5,7},{7,5},{8,10},{10,8},{9,1... | collective-permute-start | bytes 1966088 | tf_op jit(solution)/shard_map/ppermute | solution.py:130
  6.8 20.2 %collective-permute-start = (bf16[2,256,384]{2,1,0:T(8,128)(2,1)S(1)}, bf16[2,256,384]{2,1,0:T(8,128)(2,1)S(1)}, u32[]{:S(2)}, u32[]{:S(2)}) collective-permute-start(bf16[2,256,384]{2,1,0:T(8,128)(2,1)S(1)} %get-tuple-element.281), channel_id=1, source_target_pairs={{0,8},{8,0},{4,12},{12,4},{16,24},{24,16},{20,28},{28,20},{1,9},{9... | collective-permute-start | bytes 1179656 | tf_op jit(solution)/shard_map/ppermute | solution.py:130
  8.1 18.9 %collective-permute-start.3 = (bf16[2,256,384]{2,1,0:T(8,128)(2,1)S(1)}, bf16[2,256,384]{2,1,0:T(8,128)(2,1)S(1)}, u32[]{:S(2)}, u32[]{:S(2)}) collective-permute-start(bf16[2,256,384]{2,1,0:T(8,128)(2,1)S(1)} %get-tuple-element.281), channel_id=1, source_target_pairs={{0,4},{4,0},{8,12},{12,8},{16,20},{20,16},{24,28},{28,24},{1,5},{5... | collective-permute-start | bytes 1179656 | tf_op jit(solution)/shard_map/ppermute | solution.py:130
  9.4 10.5 %collective-permute-start.1 = (bf16[256,384]{1,0:T(8,128)(2,1)S(1)}, bf16[256,384]{1,0:T(8,128)(2,1)S(1)}, u32[]{:S(2)}, u32[]{:S(2)}) collective-permute-start(bf16[256,384]{1,0:T(8,128)(2,1)S(1)} %get-tuple-element.280), channel_id=1, source_target_pairs={{0,16},{16,0},{4,20},{20,4},{8,24},{24,8},{12,28},{28,12},{1,17},{... | collective-permute-start | bytes 589832 | tf_op jit(solution)/shard_map/ppermute | solution.py:130
  11.7 15.3 %collective-permute-start.2 = (bf16[256,384]{1,0:T(8,128)(2,1)S(1)}, bf16[256,384]{1,0:T(8,128)(2,1)S(1)}, u32[]{:S(2)}, u32[]{:S(2)}) collective-permute-start(bf16[256,384]{1,0:T(8,128)(2,1)S(1)} %get-tuple-element.280), channel_id=1, source_target_pairs={{0,24},{24,0},{4,28},{28,4},{8,16},{16,8},{12,20},{20,12},{1,25},{... | collective-permute-start | bytes 589832 | tf_op jit(solution)/shard_map/ppermute | solution.py:130
  27.8 18.7 %collective-permute-start.5 = (bf16[1120,384]{1,0:T(8,128)(2,1)S(1)}, bf16[1120,384]{1,0:T(8,128)(2,1)S(1)}, u32[]{:S(2)}, u32[]{:S(2)}) collective-permute-start(bf16[1120,384]{1,0:T(8,128)(2,1)S(1)} %pad_maximum_fusion.4), channel_id=1, source_target_pairs={{0,4},{4,0},{8,12},{12,8},{16,20},{20,16},{24,28},{28,24},{1,5},{5... | collective-permute-start | bytes 2580488 | tf_op jit(solution)/shard_map/ppermute | solution.py:130
  29.0 11.6 %collective-permute-start.6 = (bf16[512,384]{1,0:T(8,128)(2,1)S(1)}, bf16[512,384]{1,0:T(8,128)(2,1)S(1)}, u32[]{:S(2)}, u32[]{:S(2)}) collective-permute-start(bf16[512,384]{1,0:T(8,128)(2,1)S(1)} %pad_maximum_fusion.15), channel_id=1, source_target_pairs={{0,2},{2,0},{1,3},{3,1},{4,6},{6,4},{5,7},{7,5},{8,10},{10,8},{9,1... | collective-permute-start | bytes 1179656 | tf_op jit(solution)/shard_map/ppermute | solution.py:130
  29.3 11.4 %collective-permute-start.7 = (bf16[2,176,384]{2,1,0:T(8,128)(2,1)S(1)}, bf16[2,176,384]{2,1,0:T(8,128)(2,1)}, u32[]{:S(2)}, u32[]{:S(2)}) collective-permute-start(bf16[2,176,384]{2,1,0:T(8,128)(2,1)S(1)} %get-tuple-element.291), channel_id=1, source_target_pairs={{0,8},{8,0},{4,12},{12,4},{16,24},{24,16},{20,28},{28,20},{1,9},{9... | collective-permute-start | bytes 811016 | tf_op jit(solution)/shard_map/ppermute | solution.py:130
  29.3 5.6 %collective-permute-start.8 = (bf16[176,384]{1,0:T(8,128)(2,1)S(1)}, bf16[176,384]{1,0:T(8,128)(2,1)S(1)}, u32[]{:S(2)}, u32[]{:S(2)}) collective-permute-start(bf16[176,384]{1,0:T(8,128)(2,1)S(1)} %get-tuple-element.293), channel_id=1, source_target_pairs={{0,16},{16,0},{4,20},{20,4},{8,24},{24,8},{12,28},{28,12},{1,17},{... | collective-permute-start | bytes 405512 | tf_op jit(solution)/shard_map/ppermute | solution.py:130
  30.6 9.6 %collective-permute-start.9 = (bf16[176,384]{1,0:T(8,128)(2,1)S(1)}, bf16[176,384]{1,0:T(8,128)(2,1)S(1)}, u32[]{:S(2)}, u32[]{:S(2)}) collective-permute-start(bf16[176,384]{1,0:T(8,128)(2,1)S(1)} %get-tuple-element.293), channel_id=1, source_target_pairs={{0,24},{24,0},{4,28},{28,4},{8,16},{16,8},{12,20},{20,12},{1,25},{... | collective-permute-start | bytes 405512 | tf_op jit(solution)/shard_map/ppermute | solution.py:130
  48.1 25.3 %collective-permute-start.13 = (bf16[1552,384]{1,0:T(8,128)(2,1)S(1)}, bf16[1552,384]{1,0:T(8,128)(2,1)S(1)}, u32[]{:S(2)}, u32[]{:S(2)}) collective-permute-start(bf16[1552,384]{1,0:T(8,128)(2,1)S(1)} %pad_maximum_fusion), channel_id=1, source_target_pairs={{0,4},{4,0},{8,12},{12,8},{16,20},{20,16},{24,28},{28,24},{1,5},{5... | collective-permute-start | bytes 3575816 | tf_op jit(solution)/shard_map/ppermute | solution.py:130
  49.4 24.0 %collective-permute-start.14 = (bf16[864,384]{1,0:T(8,128)(2,1)S(1)}, bf16[864,384]{1,0:T(8,128)(2,1)S(1)}, u32[]{:S(2)}, u32[]{:S(2)}) collective-permute-start(bf16[864,384]{1,0:T(8,128)(2,1)S(1)} %pad_maximum_fusion.9), channel_id=1, source_target_pairs={{0,2},{2,0},{1,3},{3,1},{4,6},{6,4},{5,7},{7,5},{8,10},{10,8},{9,1... | collective-permute-start | bytes 1990664 | tf_op jit(solution)/shard_map/ppermute | solution.py:130
  49.7 23.7 %collective-permute-start.10 = (bf16[2,384,384]{2,1,0:T(8,128)(2,1)S(1)}, bf16[2,384,384]{2,1,0:T(8,128)(2,1)S(1)}, u32[]{:S(2)}, u32[]{:S(2)}) collective-permute-start(bf16[2,384,384]{2,1,0:T(8,128)(2,1)S(1)} %get-tuple-element.301), channel_id=1, source_target_pairs={{0,8},{8,0},{4,12},{12,4},{16,24},{24,16},{20,28},{28,20},{1,9},{9... | collective-permute-start | bytes 1769480 | tf_op jit(solution)/shard_map/ppermute | solution.py:130
  49.7 15.8 %collective-permute-start.11 = (bf16[384,384]{1,0:T(8,128)(2,1)S(1)}, bf16[384,384]{1,0:T(8,128)(2,1)S(1)}, u32[]{:S(2)}, u32[]{:S(2)}) collective-permute-start(bf16[384,384]{1,0:T(8,128)(2,1)S(1)} %get-tuple-element.303), channel_id=1, source_target_pairs={{0,16},{16,0},{4,20},{20,4},{8,24},{24,8},{12,28},{28,12},{1,17},{... | collective-permute-start | bytes 884744 | tf_op jit(solution)/shard_map/ppermute | solution.py:130
  50.9 22.5 %collective-permute-start.12 = (bf16[384,384]{1,0:T(8,128)(2,1)S(1)}, bf16[384,384]{1,0:T(8,128)(2,1)S(1)}, u32[]{:S(2)}, u32[]{:S(2)}) collective-permute-start(bf16[384,384]{1,0:T(8,128)(2,1)S(1)} %get-tuple-element.303), channel_id=1, source_target_pairs={{0,24},{24,0},{4,28},{28,4},{8,16},{16,8},{12,20},{20,12},{1,25},{... | collective-permute-start | bytes 884744 | tf_op jit(solution)/shard_map/ppermute | solution.py:130
  76.7 7.3 %collective-permute-start.15 = (bf16[512,384]{1,0:T(8,128)(2,1)S(1)}, bf16[512,384]{1,0:T(8,128)(2,1)S(1)}, u32[]{:S(2)}, u32[]{:S(2)}) collective-permute-start(bf16[512,384]{1,0:T(8,128)(2,1)S(1)} %bitcast.212), channel_id=1, source_target_pairs={{0,1},{1,0},{2,3},{3,2},{4,5},{5,4},{6,7},{7,6},{8,9},{9,8},{10,11... | collective-permute-start | bytes 1179656 | tf_op jit(solution)/shard_map/ppermute | solution.py:71
  82.2 8.3 %collective-permute-start.20 = (bf16[1120,384]{1,0:T(8,128)(2,1)S(1)}, bf16[1120,384]{1,0:T(8,128)(2,1)S(1)}, u32[]{:S(2)}, u32[]{:S(2)}) collective-permute-start(bf16[1120,384]{1,0:T(8,128)(2,1)S(1)} %collective-permute-done.5.refs_6_.refs_2_), channel_id=1, source_target_pairs={{0,1},{1,0},{2,3},{3,2},{4,5},{5,4},{6,7},{7,6},{8,9},{9,8},{10,11... | collective-permute-start | bytes 2580488 | tf_op jit(solution)/shard_map/ppermute | solution.py:71
  82.3 10.7 %collective-permute-start.21 = (bf16[1552,384]{1,0:T(8,128)(2,1)S(1)}, bf16[1552,384]{1,0:T(8,128)(2,1)}, u32[]{:S(2)}, u32[]{:S(2)}) collective-permute-start(bf16[1552,384]{1,0:T(8,128)(2,1)S(1)} %collective-permute-done.13.refs_7_.refs_6_.refs_2_), channel_id=1, source_target_pairs={{0,1},{1,0},{2,3},{3,2},{4,5},{5,4},{6,7},{7,6},{8,9},{9,8},{10,11... | collective-permute-start | bytes 3575816 | tf_op jit(solution)/shard_map/ppermute | solution.py:71
  83.7 6.1 %collective-permute-start.22 = (bf16[864,384]{1,0:T(8,128)(2,1)S(1)}, bf16[864,384]{1,0:T(8,128)(2,1)S(1)}, u32[]{:S(2)}, u32[]{:S(2)}) collective-permute-start(bf16[864,384]{1,0:T(8,128)(2,1)S(1)} %collective-permute-done.14.refs_8_.refs_5_), channel_id=1, source_target_pairs={{0,1},{1,0},{2,3},{3,2},{4,5},{5,4},{6,7},{7,6},{8,9},{9,8},{10,11... | collective-permute-start | bytes 1990664 | tf_op jit(solution)/shard_map/ppermute | solution.py:71
  84.0 4.6 %collective-permute-start.19 = (bf16[512,384]{1,0:T(8,128)(2,1)S(1)}, bf16[512,384]{1,0:T(8,128)(2,1)S(1)}, u32[]{:S(2)}, u32[]{:S(2)}) collective-permute-start(bf16[512,384]{1,0:T(8,128)(2,1)S(1)} %collective-permute-done.6.refs_5_), channel_id=1, source_target_pairs={{0,1},{1,0},{2,3},{3,2},{4,5},{5,4},{6,7},{7,6},{8,9},{9,8},{10,11... | collective-permute-start | bytes 1179656 | tf_op jit(solution)/shard_map/ppermute | solution.py:71
  87.1 24.0 %collective-permute-start.23 = (bf16[1328,384]{1,0:T(8,128)(2,1)}, bf16[1328,384]{1,0:T(8,128)(2,1)S(1)}, u32[]{:S(2)}, u32[]{:S(2)}) collective-permute-start(bf16[1328,384]{1,0:T(8,128)(2,1)} %pad_maximum_fusion.1), channel_id=1, source_target_pairs={{0,4},{4,0},{8,12},{12,8},{16,20},{20,16},{24,28},{28,24},{1,5},{5... | collective-permute-start | bytes 3059720 | tf_op jit(solution)/shard_map/ppermute | solution.py:130
  88.6 20.6 %collective-permute-start.24 = (bf16[1120,384]{1,0:T(8,128)(2,1)}, bf16[1120,384]{1,0:T(8,128)(2,1)}, u32[]{:S(2)}, u32[]{:S(2)}) collective-permute-start(bf16[1120,384]{1,0:T(8,128)(2,1)} %pad_maximum_fusion.5), channel_id=1, source_target_pairs={{0,2},{2,0},{1,3},{3,1},{4,6},{6,4},{5,7},{7,5},{8,10},{10,8},{9,1... | collective-permute-start | bytes 2580488 | tf_op jit(solution)/shard_map/ppermute | solution.py:130
  89.8 16.6 %collective-permute-start.25 = (bf16[2,160,1024]{2,1,0:T(8,128)(2,1)}, bf16[2,160,1024]{2,1,0:T(8,128)(2,1)}, u32[]{:S(2)}, u32[]{:S(2)}) collective-permute-start(bf16[2,160,1024]{2,1,0:T(8,128)(2,1)} %shard_map.248.refs_17_), channel_id=1, source_target_pairs={{0,1},{1,0},{2,3},{3,2},{4,5},{5,4},{6,7},{7,6},{8,9},{9,8},{10,11... | collective-permute-start | bytes 1966088 | tf_op jit(solution)/shard_map/ppermute | solution.py:130
  91.6 14.8 %collective-permute-start.26 = (bf16[2,160,1024]{2,1,0:T(8,128)(2,1)}, bf16[2,160,1024]{2,1,0:T(8,128)(2,1)}, u32[]{:S(2)}, u32[]{:S(2)}) collective-permute-start(bf16[2,160,1024]{2,1,0:T(8,128)(2,1)} %collective-permute-done.4.refs_19_), channel_id=1, source_target_pairs={{0,1},{1,0},{2,3},{3,2},{4,5},{5,4},{6,7},{7,6},{8,9},{9,8},{10,11... | collective-permute-start | bytes 1966088 | tf_op jit(solution)/shard_map/ppermute | solution.py:130
  112.0 7.7 %collective-permute-start.30 = (bf16[1328,384]{1,0:T(8,128)(2,1)S(1)}, bf16[1328,384]{1,0:T(8,128)(2,1)S(1)}, u32[]{:S(2)}, u32[]{:S(2)}) collective-permute-start(bf16[1328,384]{1,0:T(8,128)(2,1)S(1)} %collective-permute-done.23.refs_7_.refs_6_), channel_id=1, source_target_pairs={{0,1},{1,0},{2,3},{3,2},{4,5},{5,4},{6,7},{7,6},{8,9},{9,8},{10,11... | collective-permute-start | bytes 3059720 | tf_op jit(solution)/shard_map/ppermute | solution.py:71
  113.2 6.5 %collective-permute-start.31 = (bf16[1120,384]{1,0:T(8,128)(2,1)}, bf16[1120,384]{1,0:T(8,128)(2,1)}, u32[]{:S(2)}, u32[]{:S(2)}) collective-permute-start(bf16[1120,384]{1,0:T(8,128)(2,1)} %collective-permute-done.24.refs_8_.refs_5_), channel_id=1, source_target_pairs={{0,1},{1,0},{2,3},{3,2},{4,5},{5,4},{6,7},{7,6},{8,9},{9,8},{10,11... | collective-permute-start | bytes 2580488 | tf_op jit(solution)/shard_map/ppermute | solution.py:71
  113.2 6.5 %collective-permute-start.27 = (bf16[352,384]{1,0:T(8,128)(2,1)}, bf16[352,384]{1,0:T(8,128)(2,1)}, u32[]{:S(2)}, u32[]{:S(2)}) collective-permute-start(bf16[352,384]{1,0:T(8,128)(2,1)} %bitcast.22.refs_1_), channel_id=1, source_target_pairs={{0,1},{1,0},{2,3},{3,2},{4,5},{5,4},{6,7},{7,6},{8,9},{9,8},{10,11... | collective-permute-start | bytes 811016 | tf_op jit(solution)/shard_map/ppermute | solution.py:71
  113.8 4.8 %collective-permute-start.29 = (bf16[176,384]{1,0:T(8,128)(2,1)S(1)}, bf16[176,384]{1,0:T(8,128)(2,1)}, u32[]{:S(2)}, u32[]{:S(2)}) collective-permute-start(bf16[176,384]{1,0:T(8,128)(2,1)S(1)} %copy-done.46), channel_id=1, source_target_pairs={{0,1},{1,0},{2,3},{3,2},{4,5},{5,4},{6,7},{7,6},{8,9},{9,8},{10,11... | collective-permute-start | bytes 405512 | tf_op jit(solution)/shard_map/ppermute | solution.py:71
  117.2 20.6 %collective-permute-start.33 = (bf16[384,384]{1,0:T(8,128)(2,1)}, bf16[384,384]{1,0:T(8,128)(2,1)}, u32[]{:S(2)}, u32[]{:S(2)}) collective-permute-start(bf16[384,384]{1,0:T(8,128)(2,1)} %get-tuple-element.356), channel_id=1, source_target_pairs={{0,4},{4,0},{8,12},{12,8},{16,20},{20,16},{24,28},{28,24},{1,5},{5... | collective-permute-start | bytes 884744 | tf_op jit(solution)/shard_map/ppermute | solution.py:130
  118.5 19.4 %collective-permute-start.32 = (bf16[2,384,384]{2,1,0:T(8,128)(2,1)}, bf16[2,384,384]{2,1,0:T(8,128)(2,1)}, u32[]{:S(2)}, u32[]{:S(2)}) collective-permute-start(bf16[2,384,384]{2,1,0:T(8,128)(2,1)} %bitcast.207), channel_id=1, source_target_pairs={{0,2},{2,0},{1,3},{3,1},{4,6},{6,4},{5,7},{7,5},{8,10},{10,8},{9,1... | collective-permute-start | bytes 1769480 | tf_op jit(solution)/shard_map/ppermute | solution.py:130
  137.9 4.9 %collective-permute-start.34 = (bf16[768,384]{1,0:T(8,128)(2,1)S(1)}, bf16[768,384]{1,0:T(8,128)(2,1)S(1)}, u32[]{:S(2)}, u32[]{:S(2)}) collective-permute-start(bf16[768,384]{1,0:T(8,128)(2,1)S(1)} %bitcast.178), channel_id=1, source_target_pairs={{0,1},{1,0},{2,3},{3,2},{4,5},{5,4},{6,7},{7,6},{8,9},{9,8},{10,11... | collective-permute-start | bytes 1769480 | tf_op jit(solution)/shard_map/ppermute | solution.py:71
  161.7 12.2 %collective-permute-start.39 = (bf16[8,2,192,384]{3,2,1,0:T(8,128)(2,1)S(1)}, bf16[8,2,192,384]{3,2,1,0:T(8,128)(2,1)S(1)}, u32[]{:S(2)}, u32[]{:S(2)}) collective-permute-start(bf16[8,2,192,384]{3,2,1,0:T(8,128)(2,1)S(1)} %shard_map.253), channel_id=1, source_target_pairs={{0,1},{1,0},{2,3},{3,2},{4,5},{5,4},{6,7},{7,6},{8,9},{9,8},{10,11... | collective-permute-start | bytes 7077896 | tf_op jit(solution)/shard_map/ppermute | solution.py:130
  175.9 16.3 %collective-permute-start.42 = (bf16[8,2,192,384]{3,2,1,0:T(8,128)(2,1)S(1)}, bf16[8,2,192,384]{3,2,1,0:T(8,128)(2,1)S(1)}, u32[]{:S(2)}, u32[]{:S(2)}) collective-permute-start(bf16[8,2,192,384]{3,2,1,0:T(8,128)(2,1)S(1)} %shard_map.256), channel_id=1, source_target_pairs={{0,1},{1,0},{2,3},{3,2},{4,5},{5,4},{6,7},{7,6},{8,9},{9,8},{10,11... | collective-permute-start | bytes 7077896 | tf_op jit(solution)/shard_map/ppermute | solution.py:130
  176.1 15.8 %collective-permute-start.41 = (bf16[2,192,384]{2,1,0:T(8,128)(2,1)S(1)}, bf16[2,192,384]{2,1,0:T(8,128)(2,1)S(1)}, u32[]{:S(2)}, u32[]{:S(2)}) collective-permute-start(bf16[2,192,384]{2,1,0:T(8,128)(2,1)S(1)} %get-tuple-element.401), channel_id=1, source_target_pairs={{0,8},{8,0},{4,12},{12,4},{16,24},{24,16},{20,28},{28,20},{1,9},{9... | collective-permute-start | bytes 884744 | tf_op jit(solution)/shard_map/ppermute | solution.py:130
  176.1 15.8 %collective-permute-start.43 = (bf16[2,192,384]{2,1,0:T(8,128)(2,1)S(1)}, bf16[2,192,384]{2,1,0:T(8,128)(2,1)S(1)}, u32[]{:S(2)}, u32[]{:S(2)}) collective-permute-start(bf16[2,192,384]{2,1,0:T(8,128)(2,1)S(1)} %get-tuple-element.406), channel_id=1, source_target_pairs={{0,4},{4,0},{8,12},{12,8},{16,20},{20,16},{24,28},{28,24},{1,5},{5... | collective-permute-start | bytes 884744 | tf_op jit(solution)/shard_map/ppermute | solution.py:130
  177.2 14.8 %collective-permute-start.40 = (bf16[4,192,384]{2,1,0:T(8,128)(2,1)S(1)}, bf16[4,192,384]{2,1,0:T(8,128)(2,1)S(1)}, u32[]{:S(2)}, u32[]{:S(2)}) collective-permute-start(bf16[4,192,384]{2,1,0:T(8,128)(2,1)S(1)} %get-tuple-element.399), channel_id=1, source_target_pairs={{0,2},{2,0},{1,3},{3,1},{4,6},{6,4},{5,7},{7,5},{8,10},{10,8},{9,1... | collective-permute-start | bytes 1769480 | tf_op jit(solution)/shard_map/ppermute | solution.py:130
  194.3 20.7 %collective-permute-start.45 = (bf16[8,2,272,384]{3,2,1,0:T(8,128)(2,1)S(1)}, bf16[8,2,272,384]{3,2,1,0:T(8,128)(2,1)S(1)}, u32[]{:S(2)}, u32[]{:S(2)}) collective-permute-start(bf16[8,2,272,384]{3,2,1,0:T(8,128)(2,1)S(1)} %shard_map.260), channel_id=1, source_target_pairs={{0,1},{1,0},{2,3},{3,2},{4,5},{5,4},{6,7},{7,6},{8,9},{9,8},{10,11... | collective-permute-start | bytes 10027016 | tf_op jit(solution)/shard_map/ppermute | solution.py:130
  195.5 17.1 %collective-permute-start.47 = (bf16[576,384]{1,0:T(8,128)(2,1)S(1)}, bf16[576,384]{1,0:T(8,128)(2,1)S(1)}, u32[]{:S(2)}, u32[]{:S(2)}) collective-permute-start(bf16[576,384]{1,0:T(8,128)(2,1)S(1)} %pad_maximum_fusion.12), channel_id=1, source_target_pairs={{0,8},{8,0},{4,12},{12,4},{16,24},{24,16},{20,28},{28,20},{1,9},{9... | collective-permute-start | bytes 1327112 | tf_op jit(solution)/shard_map/ppermute | solution.py:130
  196.1 16.6 %collective-permute-start.46 = (bf16[4,192,384]{2,1,0:T(8,128)(2,1)S(1)}, bf16[4,192,384]{2,1,0:T(8,128)(2,1)S(1)}, u32[]{:S(2)}, u32[]{:S(2)}) collective-permute-start(bf16[4,192,384]{2,1,0:T(8,128)(2,1)S(1)} %get-tuple-element.448), channel_id=1, source_target_pairs={{0,2},{2,0},{1,3},{3,1},{4,6},{6,4},{5,7},{7,5},{8,10},{10,8},{9,1... | collective-permute-start | bytes 1769480 | tf_op jit(solution)/shard_map/ppermute | solution.py:130
  197.3 17.4 %collective-permute-start.44 = (bf16[960,384]{1,0:T(8,128)(2,1)S(1)}, bf16[960,384]{1,0:T(8,128)(2,1)S(1)}, u32[]{:S(2)}, u32[]{:S(2)}) collective-permute-start(bf16[960,384]{1,0:T(8,128)(2,1)S(1)} %pad_maximum_fusion.7), channel_id=1, source_target_pairs={{0,4},{4,0},{8,12},{12,8},{16,20},{20,16},{24,28},{28,24},{1,5},{5... | collective-permute-start | bytes 2211848 | tf_op jit(solution)/shard_map/ppermute | solution.py:130
  219.2 16.0 %collective-permute-start.49 = (bf16[928,384]{1,0:T(8,128)(2,1)S(1)}, bf16[928,384]{1,0:T(8,128)(2,1)S(1)}, u32[]{:S(2)}, u32[]{:S(2)}) collective-permute-start(bf16[928,384]{1,0:T(8,128)(2,1)S(1)} %pad_maximum_fusion.8), channel_id=1, source_target_pairs={{0,8},{8,0},{4,12},{12,4},{16,24},{24,16},{20,28},{28,20},{1,9},{9... | collective-permute-start | bytes 2138120 | tf_op jit(solution)/shard_map/ppermute | solution.py:130
  220.1 18.3 %collective-permute-start.52 = (bf16[4,272,384]{2,1,0:T(8,128)(2,1)S(1)}, bf16[4,272,384]{2,1,0:T(8,128)(2,1)S(1)}, u32[]{:S(2)}, u32[]{:S(2)}) collective-permute-start(bf16[4,272,384]{2,1,0:T(8,128)(2,1)S(1)} %get-tuple-element.505), channel_id=1, source_target_pairs={{0,2},{2,0},{1,3},{3,1},{4,6},{6,4},{5,7},{7,5},{8,10},{10,8},{9,1... | collective-permute-start | bytes 2506760 | tf_op jit(solution)/shard_map/ppermute | solution.py:130
  220.4 18.5 %collective-permute-start.50 = (bf16[1120,384]{1,0:T(8,128)(2,1)S(1)}, bf16[1120,384]{1,0:T(8,128)(2,1)S(1)}, u32[]{:S(2)}, u32[]{:S(2)}) collective-permute-start(bf16[1120,384]{1,0:T(8,128)(2,1)S(1)} %pad_maximum_fusion.6), channel_id=1, source_target_pairs={{0,4},{4,0},{8,12},{12,8},{16,20},{20,16},{24,28},{28,24},{1,5},{5... | collective-permute-start | bytes 2580488 | tf_op jit(solution)/shard_map/ppermute | solution.py:130
  221.0 18.2 %collective-permute-start.48 = (bf16[2,2,160,1024]{3,2,1,0:T(8,128)(2,1)S(1)}, bf16[2,2,160,1024]{3,2,1,0:T(8,128)(2,1)S(1)}, u32[]{:S(2)}, u32[]{:S(2)}) collective-permute-start(bf16[2,2,160,1024]{3,2,1,0:T(8,128)(2,1)S(1)} %get-tuple-element.493), channel_id=1, source_target_pairs={{0,1},{1,0},{2,3},{3,2},{4,5},{5,4},{6,7},{7,6},{8,9},{9,8},{10,11... | collective-permute-start | bytes 3932168 | tf_op jit(solution)/shard_map/ppermute | solution.py:130
  223.1 16.6 %collective-permute-start.51 = (bf16[8,2,144,384]{3,2,1,0:T(8,128)(2,1)S(1)}, bf16[8,2,144,384]{3,2,1,0:T(8,128)(2,1)S(1)}, u32[]{:S(2)}, u32[]{:S(2)}) collective-permute-start(bf16[8,2,144,384]{3,2,1,0:T(8,128)(2,1)S(1)} %shard_map.263), channel_id=1, source_target_pairs={{0,1},{1,0},{2,3},{3,2},{4,5},{5,4},{6,7},{7,6},{8,9},{9,8},{10,11... | collective-permute-start | bytes 5308424 | tf_op jit(solution)/shard_map/ppermute | solution.py:130
  241.5 15.3 %collective-permute-start.56 = (bf16[784,384]{1,0:T(8,128)(2,1)S(1)}, bf16[784,384]{1,0:T(8,128)(2,1)S(1)}, u32[]{:S(2)}, u32[]{:S(2)}) collective-permute-start(bf16[784,384]{1,0:T(8,128)(2,1)S(1)} %pad_maximum_fusion.10), channel_id=1, source_target_pairs={{0,8},{8,0},{4,12},{12,4},{16,24},{24,16},{20,28},{28,20},{1,9},{9... | collective-permute-start | bytes 1806344 | tf_op jit(solution)/shard_map/ppermute | solution.py:130
  244.6 10.5 %collective-permute-start.55 = (bf16[192,384]{1,0:T(8,128)(2,1)S(1)}, bf16[192,384]{1,0:T(8,128)(2,1)S(1)}, u32[]{:S(2)}, u32[]{:S(2)}) collective-permute-start(bf16[192,384]{1,0:T(8,128)(2,1)S(1)} %fusion.13), channel_id=1, source_target_pairs={{0,16},{16,0},{4,20},{20,4},{8,24},{24,8},{12,28},{28,12},{1,17},{... | collective-permute-start | bytes 442376 | tf_op jit(solution)/shard_map/ppermute | solution.py:130
  246.1 9.2 %collective-permute-start.57 = (bf16[4,160,384]{2,1,0:T(8,128)(2,1)S(1)}, bf16[4,160,384]{2,1,0:T(8,128)(2,1)S(1)}, u32[]{:S(2)}, u32[]{:S(2)}) collective-permute-start(bf16[4,160,384]{2,1,0:T(8,128)(2,1)S(1)} %get-tuple-element.516), channel_id=1, source_target_pairs={{0,2},{2,0},{1,3},{3,1},{4,6},{6,4},{5,7},{7,5},{8,10},{10,8},{9,1... | collective-permute-start | bytes 1474568 | tf_op jit(solution)/shard_map/ppermute | solution.py:130
  247.3 17.1 %collective-permute-start.54 = (bf16[1136,384]{1,0:T(8,128)(2,1)S(1)}, bf16[1136,384]{1,0:T(8,128)(2,1)S(1)}, u32[]{:S(2)}, u32[]{:S(2)}) collective-permute-start(bf16[1136,384]{1,0:T(8,128)(2,1)S(1)} %pad_maximum_fusion.3), channel_id=1, source_target_pairs={{0,4},{4,0},{8,12},{12,8},{16,20},{20,16},{24,28},{28,24},{1,5},{5... | collective-permute-start | bytes 2617352 | tf_op jit(solution)/shard_map/ppermute | solution.py:130
  264.8 6.6 %collective-permute-start.59 = (bf16[192,384]{1,0:T(8,128)(2,1)S(1)}, bf16[192,384]{1,0:T(8,128)(2,1)S(1)}, u32[]{:S(2)}, u32[]{:S(2)}) collective-permute-start(bf16[192,384]{1,0:T(8,128)(2,1)S(1)} %fusion.11), channel_id=1, source_target_pairs={{0,16},{16,0},{4,20},{20,4},{8,24},{24,8},{12,28},{28,12},{1,17},{... | collective-permute-start | bytes 442376 | tf_op jit(solution)/shard_map/ppermute | solution.py:130
  265.9 44.2 %collective-permute-start.53 = (bf16[2,160,1024]{2,1,0:T(8,128)(2,1)S(1)}, bf16[2,160,1024]{2,1,0:T(8,128)(2,1)S(1)}, u32[]{:S(2)}, u32[]{:S(2)}) collective-permute-start(bf16[2,160,1024]{2,1,0:T(8,128)(2,1)S(1)} %fusion.1), channel_id=1, source_target_pairs={{0,2},{2,0},{1,3},{3,1},{4,6},{6,4},{5,7},{7,5},{8,10},{10,8},{9,1... | collective-permute-start | bytes 1966088 | tf_op jit(solution)/shard_map/ppermute | solution.py:130
  266.2 28.6 %collective-permute-start.70 = (bf16[2,192,384]{2,1,0:T(8,128)(2,1)S(1)}, bf16[2,192,384]{2,1,0:T(8,128)(2,1)S(1)}, u32[]{:S(2)}, u32[]{:S(2)}) collective-permute-start(bf16[2,192,384]{2,1,0:T(8,128)(2,1)S(1)} %pad_maximum_fusion.17), channel_id=1, source_target_pairs={{0,2},{2,0},{1,3},{3,1},{4,6},{6,4},{5,7},{7,5},{8,10},{10,8},{9,1... | collective-permute-start | bytes 884744 | tf_op jit(solution)/shard_map/ppermute | solution.py:130
  267.4 8.9 %collective-permute-start.58 = (bf16[432,384]{1,0:T(8,128)(2,1)S(1)}, bf16[432,384]{1,0:T(8,128)(2,1)S(1)}, u32[]{:S(2)}, u32[]{:S(2)}) collective-permute-start(bf16[432,384]{1,0:T(8,128)(2,1)S(1)} %pad_maximum_fusion.16), channel_id=1, source_target_pairs={{0,8},{8,0},{4,12},{12,4},{16,24},{24,16},{20,28},{28,20},{1,9},{9... | collective-permute-start | bytes 995336 | tf_op jit(solution)/shard_map/ppermute | solution.py:130
  268.3 8.1 %collective-permute-start.60 = (bf16[3,160,384]{2,1,0:T(8,128)(2,1)S(1)}, bf16[3,160,384]{2,1,0:T(8,128)(2,1)S(1)}, u32[]{:S(2)}, u32[]{:S(2)}) collective-permute-start(bf16[3,160,384]{2,1,0:T(8,128)(2,1)S(1)} %add_convert_fusion.4), channel_id=1, source_target_pairs={{0,4},{4,0},{8,12},{12,8},{16,20},{20,16},{24,28},{28,24},{1,5},{5... | collective-permute-start | bytes 1105928 | tf_op jit(solution)/shard_map/ppermute | solution.py:130
  276.5 6.9 %collective-permute-start.62 = (bf16[160,384]{1,0:T(8,128)(2,1)S(1)}, bf16[160,384]{1,0:T(8,128)(2,1)S(1)}, u32[]{:S(2)}, u32[]{:S(2)}) collective-permute-start(bf16[160,384]{1,0:T(8,128)(2,1)S(1)} %fusion.39), channel_id=1, source_target_pairs={{0,8},{8,0},{4,12},{12,4},{16,24},{24,16},{20,28},{28,20},{1,9},{9... | collective-permute-start | bytes 368648 | tf_op jit(solution)/shard_map/ppermute | solution.py:130
  276.7 7.9 %collective-permute-start.61 = (bf16[272,384]{1,0:T(8,128)(2,1)S(1)}, bf16[272,384]{1,0:T(8,128)(2,1)S(1)}, u32[]{:S(2)}, u32[]{:S(2)}) collective-permute-start(bf16[272,384]{1,0:T(8,128)(2,1)S(1)} %fusion.4), channel_id=1, source_target_pairs={{0,16},{16,0},{4,20},{20,4},{8,24},{24,8},{12,28},{28,12},{1,17},{... | collective-permute-start | bytes 626696 | tf_op jit(solution)/shard_map/ppermute | solution.py:130
  278.2 29.2 %collective-permute-start.68 = (bf16[2,192,384]{2,1,0:T(8,128)(2,1)S(1)}, bf16[2,192,384]{2,1,0:T(8,128)(2,1)S(1)}, u32[]{:S(2)}, u32[]{:S(2)}) collective-permute-start(bf16[2,192,384]{2,1,0:T(8,128)(2,1)S(1)} %pad_maximum_fusion.18), channel_id=1, source_target_pairs={{0,2},{2,0},{1,3},{3,1},{4,6},{6,4},{5,7},{7,5},{8,10},{10,8},{9,1... | collective-permute-start | bytes 884744 | tf_op jit(solution)/shard_map/ppermute | solution.py:130
  284.7 9.6 %collective-permute-start.63 = (bf16[160,384]{1,0:T(8,128)(2,1)S(1)}, bf16[160,384]{1,0:T(8,128)(2,1)S(1)}, u32[]{:S(2)}, u32[]{:S(2)}) collective-permute-start(bf16[160,384]{1,0:T(8,128)(2,1)S(1)} %fusion.24), channel_id=1, source_target_pairs={{0,16},{16,0},{4,20},{20,4},{8,24},{24,8},{12,28},{28,12},{1,17},{... | collective-permute-start | bytes 368648 | tf_op jit(solution)/shard_map/ppermute | solution.py:130
  285.1 17.5 %collective-permute-start.66 = (bf16[2,272,384]{2,1,0:T(8,128)(2,1)S(1)}, bf16[2,272,384]{2,1,0:T(8,128)(2,1)S(1)}, u32[]{:S(2)}, u32[]{:S(2)}) collective-permute-start(bf16[2,272,384]{2,1,0:T(8,128)(2,1)S(1)} %pad_maximum_fusion.13), channel_id=1, source_target_pairs={{0,2},{2,0},{1,3},{3,1},{4,6},{6,4},{5,7},{7,5},{8,10},{10,8},{9,1... | collective-permute-start | bytes 1253384 | tf_op jit(solution)/shard_map/ppermute | solution.py:130
  294.5 13.1 %collective-permute-start.64 = (bf16[2,160,384]{2,1,0:T(8,128)(2,1)S(1)}, bf16[2,160,384]{2,1,0:T(8,128)(2,1)S(1)}, u32[]{:S(2)}, u32[]{:S(2)}) collective-permute-start(bf16[2,160,384]{2,1,0:T(8,128)(2,1)S(1)} %pad_maximum_fusion.19), channel_id=1, source_target_pairs={{0,2},{2,0},{1,3},{3,1},{4,6},{6,4},{5,7},{7,5},{8,10},{10,8},{9,1... | collective-permute-start | bytes 737288 | tf_op jit(solution)/shard_map/ppermute | solution.py:130
  294.9 16.9 %collective-permute-start.71 = (bf16[2,192,384]{2,1,0:T(8,128)(2,1)S(1)}, bf16[2,192,384]{2,1,0:T(8,128)(2,1)S(1)}, u32[]{:S(2)}, u32[]{:S(2)}) collective-permute-start(bf16[2,192,384]{2,1,0:T(8,128)(2,1)S(1)} %add_convert_fusion.5.mine), channel_id=1, source_target_pairs={{0,1},{1,0},{2,3},{3,2},{4,5},{5,4},{6,7},{7,6},{8,9},{9,8},{10,11... | collective-permute-start | bytes 884744 | tf_op jit(solution)/shard_map/ppermute | solution.py:487
  302.8 12.8 %collective-permute-start.67 = (bf16[2,272,384]{2,1,0:T(8,128)(2,1)S(1)}, bf16[2,272,384]{2,1,0:T(8,128)(2,1)S(1)}, u32[]{:S(2)}, u32[]{:S(2)}) collective-permute-start(bf16[2,272,384]{2,1,0:T(8,128)(2,1)S(1)} %add_convert_fusion.3.mine), channel_id=1, source_target_pairs={{0,1},{1,0},{2,3},{3,2},{4,5},{5,4},{6,7},{7,6},{8,9},{9,8},{10,11... | collective-permute-start | bytes 1253384 | tf_op jit(solution)/shard_map/ppermute | solution.py:487
  307.6 5.3 %collective-permute-start.69 = (bf16[2,192,384]{2,1,0:T(8,128)(2,1)S(1)}, bf16[2,192,384]{2,1,0:T(8,128)(2,1)S(1)}, u32[]{:S(2)}, u32[]{:S(2)}) collective-permute-start(bf16[2,192,384]{2,1,0:T(8,128)(2,1)S(1)} %add_convert_fusion.6.mine), channel_id=1, source_target_pairs={{0,1},{1,0},{2,3},{3,2},{4,5},{5,4},{6,7},{7,6},{8,9},{9,8},{10,11... | collective-permute-start | bytes 884744 | tf_op jit(solution)/shard_map/ppermute | solution.py:487
  307.7 6.2 %collective-permute-start.65 = (bf16[2,160,384]{2,1,0:T(8,128)(2,1)S(1)}, bf16[2,160,384]{2,1,0:T(8,128)(2,1)S(1)}, u32[]{:S(2)}, u32[]{:S(2)}) collective-permute-start(bf16[2,160,384]{2,1,0:T(8,128)(2,1)S(1)} %add_convert_fusion.7.mine), channel_id=1, source_target_pairs={{0,1},{1,0},{2,3},{3,2},{4,5},{5,4},{6,7},{7,6},{8,9},{9,8},{10,11... | collective-permute-start | bytes 737288 | tf_op jit(solution)/shard_map/ppermute | solution.py:487
  (72 other events, 662.4 us)
where the time goes:
time: 322 us; the launch traced here: 317 us
  waiting for transfers between devices  117 us (36%)
  Pallas kernels  101 us (31%)
  starting transfers between devices  71.9 us (22%)
  local copies, waits for them, and re-layouts  18.8 us (6%)
  other arithmetic  6.26 us (2%)
    ppermute x50, waiting for transfers between devices, step(): lax.ppermute(array, axis, hops)  108 us
    ppermute x50, starting transfers between devices, step(): lax.ppermute(array, axis, hops)  45.7 us
    pallas_call x1, Pallas kernels, run_patch(): call(functools.partial(patch_kernel, units, len(sources), spec, seq, patc...  17.1 us
    ppermute x4, starting transfers between devices, reduce_steps(): return (total, lax.ppermute(total, STREAM, CORE))  14.9 us
    pallas_call x1, Pallas kernels, run_text(): call(functools.partial(text_kernel, units, len(sources), spec, seq), outs...  13.5 us
    unnamed x130, local copies, waits for them, and re-layouts  12.2 us
    ppermute x18, starting transfers between devices, exchange(): self.twin = lax.ppermute(tie(self.array), STREAM, CORE)  11.3 us
    pallas_call x1, Pallas kernels, run_ffn(): call(functools.partial(ffn_kernel, len(sources), spec, in_units, seq), [s...  11.3 us
  transfers between devices with their start and end apart: 72, of which 29 were waited for; matrix products, arithmetic and copies ran while one was open for 2% of the time, Pallas kernels for 24%

commit v1 on v0

--- a/solution.py
+++ b/solution.py
@@ -87,6 +87,7 @@
     def __init__(self):
         self.before = []
         self.came = []
+        self.bases = []
 
     def take(self, arrays):
         given = {}
@@ -109,7 +110,13 @@
 
     def step(self, moving=(), compute=(), eager=False):
         arrays = [array for array, _ in self.came]
-        arrays, self.before = lax.optimization_barrier((arrays, self.before + arrays[:1]))
+        twins = [base.exchange(self.tie) for base in self.bases]
+        arrays, twins, self.before = lax.optimization_barrier(
+            (arrays, twins, self.before + arrays[:1])
+        )
+        for base, twin in zip(self.bases, twins):
+            base.twin = twin
+        self.bases = []
         self.take(arrays)
         ways = {}
         for mover in moving:
@@ -150,6 +157,7 @@
 
 class Mover:
     def __init__(self, steps, pieces=False):
+        self.given = []
         self.steps = steps
         self.pieces = pieces
         self.done = False
@@ -157,6 +165,7 @@
         self.requests = next(steps)
 
     def give(self, came):
+        self.given = came
         try:
             self.requests = self.steps.send(came)
         except StopIteration as stop:
@@ -702,15 +711,16 @@
 
 
 def image_kernel(pixels, w_ref, vec, kv_ref):
-    slots, _, images, padded, _ = kv_ref.shape
-    for slot in range(slots):
-        for c in range(2):
-            columns = slice(c * LANES, (c + 1) * LANES)
-            for j in range(2):
-                made = dot(pixels[slot].reshape(images * padded, -1), w_ref[c, j])
-                if j == 1:
-                    made = made + vec[B_CV : B_CV + 1, columns]
-                kv_ref[slot, j, :, :, columns] = low(made).reshape(images, padded, LANES)
+    slots, _, images, padded, width = kv_ref.shape
+    rows = images * padded
+    flat = pixels[...].reshape(slots * rows, -1)
+    for j in range(2):
+        made = dot(flat, jnp.concatenate((w_ref[0, j], w_ref[1, j]), axis=1))
+        if j == 1:
+            made = made + vec[B_CV : B_CV + 1]
+        for slot in range(slots):
+            part = made[slot * rows : (slot + 1) * rows]
+            kv_ref[slot, j] = low(part).reshape(images, padded, width)
 
 
 def cross_kernel(
@@ -1299,7 +1309,9 @@
         )
 
     def run_all(moves):
-        mover = Mover(moves)
+        finish(Mover(moves))
+
+    def finish(mover):
         while not mover.done:
             mover.give([lax.ppermute(array, axis, hops) for array, axis, hops in mover.requests])
 
@@ -1350,10 +1362,19 @@
         clock.step([gather_text, move_pixels])
         clock.step([gather_text, gather_patch])
         clock.step([gather_hidden, gather_text, gather_patch])
+        first_hidden = gather_hidden.given
         clock.step(
             [gather_hidden, gather_patch, move_pixels], [lambda tie: run_text(tie, *piece_sources(gather_text.result, tie))]
         )
-        clock.step([gather_hidden], [lambda tie: run_patch(tie, *piece_sources(gather_patch.result, tie))])
+        hidden_bases = [piece.base for piece in (*first_hidden, *gather_hidden.given)]
+
+        def early(tie):
+            for base in dict.fromkeys(hidden_bases):
+                base.exchange(tie)
+                clock.bases.append(base)
+            return ()
+
+        clock.step([gather_hidden], [early, lambda tie: run_patch(tie, *piece_sources(gather_patch.result, tie))])
         clock.step([gather_hidden], [lambda tie: run_ffn(tie, *piece_sources(gather_hidden.result, tie))])
 
         out_group, in_group, mid_group, last_group = Group(), Group(), Group(), Group()
@@ -1430,8 +1451,11 @@
                 if mover.done and mover not in results
             ]
 
-        while not all(mover.done for mover in movers):
+        for _ in range(3):
             clock.step(movers, ready, eager=True)
+        for mover in movers:
+            if not mover.done:
+                finish(mover)
         for work in ready():
             work(clock.tie)
         (s_out,), (s_in,) = results[move_out], results[move_in]

time: 322 us -> 312 us (0.969)
  waiting for transfers between devices: 117 us -> 106 us
    ppermute x50 -> x47, waiting for transfers between devices: 108 us -> 94.4 us  [step(): lax.ppermute(array, axis, hops)]
    ppermute x0 -> x3, waiting for transfers between devices: none -> 3.94 us  [finish(): lax.ppermute(array, axis, hops)]
    ppermute x50 -> x47, starting transfers between devices: 45.7 us -> 45.3 us  [step(): lax.ppermute(array, axis, hops)]
  transfers between devices with their start and end apart: 72 -> 72, of which waited for: 29 -> 27; matrix products, arithmetic and copies ran while one was open for 2% -> 2% of each run, Pallas kernels for 24% -> 24%
where the time goes in v1:
time: 312 us; the launch traced here: 307 us
  waiting for transfers between devices  106 us (34%)
  Pallas kernels  100 us (32%)
  starting transfers between devices  73.9 us (24%)
  local copies, waits for them, and re-layouts  18.2 us (6%)
  other arithmetic  6.27 us (2%)
    ppermute x47, waiting for transfers between devices, step(): lax.ppermute(array, axis, hops)  94.4 us
    ppermute x47, starting transfers between devices, step(): lax.ppermute(array, axis, hops)  45.3 us
    ppermute x4, starting transfers between devices, reduce_steps(): return (total, lax.ppermute(total, STREAM, CORE))  15.8 us
    pallas_call x1, Pallas kernels, run_patch(): call(functools.partial(patch_kernel, units, len(sources), spec, seq, patc...  15.7 us
    pallas_call x1, Pallas kernels, run_text(): call(functools.partial(text_kernel, units, len(sources), spec, seq), outs...  13.5 us
    unnamed x130, local copies, waits for them, and re-layouts  11.7 us
    pallas_call x1, Pallas kernels, run_ffn(): call(functools.partial(ffn_kernel, len(sources), spec, in_units, seq), [s...  11.5 us
    ppermute x18, starting transfers between devices, exchange(): self.twin = lax.ppermute(tie(self.array), STREAM, CORE)  11 us
  transfers between devices with their start and end apart: 72, of which 27 were waited for; matrix products, arithmetic and copies ran while one was open for 2% of the time, Pallas kernels for 24%

profile of v1, /device:TPU:1, one launch (start us, length us, event | category | flops | bytes accessed | tf_op | source)
XLA Modules:
  0.0 306.8 jit_solution(4090732952374375798)
XLA Ops:
  1.5 1.3 copy.31
  4.8 2.0 collective-permute-start.4
  6.9 1.3 collective-permute-start
  8.1 1.2 collective-permute-start.3
  9.4 2.3 collective-permute-start.1
  11.8 8.1 %collective-permute-done.1.refs_3_ = bf16[256,384]{1,0:T(8,128)(2,1)S(1)} collective-permute-done((bf16[256,384]{1,0:T(8,128)(2,1)S(1)}, bf16[256,384]{1,0:T(8,128)(2,1)S(1)}, u32[]{:S(2)}, u32[]{:S(2)}) %collective-permute-start.1) | collective-permute-done | bytes 196640 | tf_op jit(solution)/shard_map/ppermute | solution.py:137
  19.9 7.1 %collective-permute-done.2.refs_4_ = bf16[256,384]{1,0:T(8,128)(2,1)S(1)} collective-permute-done((bf16[256,384]{1,0:T(8,128)(2,1)S(1)}, bf16[256,384]{1,0:T(8,128)(2,1)S(1)}, u32[]{:S(2)}, u32[]{:S(2)}) %collective-permute-start.2) | collective-permute-done | bytes 196640 | tf_op jit(solution)/shard_map/ppermute | solution.py:137
  28.0 1.2 collective-permute-start.5
  29.5 1.3 collective-permute-start.8
  30.8 2.2 collective-permute-start.9
  33.2 1.8 collective-permute-done.8.refs_3_
  35.0 5.4 %collective-permute-done.9.refs_4_ = bf16[176,384]{1,0:T(8,128)(2,1)S(1)} collective-permute-done((bf16[176,384]{1,0:T(8,128)(2,1)S(1)}, bf16[176,384]{1,0:T(8,128)(2,1)S(1)}, u32[]{:S(2)}, u32[]{:S(2)}) %collective-permute-start.9) | collective-permute-done | bytes 135200 | tf_op jit(solution)/shard_map/ppermute | solution.py:137
  40.8 5.8 %collective-permute-done.5.refs_6_.refs_2_ = bf16[1120,384]{1,0:T(8,128)(2,1)S(1)} collective-permute-done((bf16[1120,384]{1,0:T(8,128)(2,1)S(1)}, bf16[1120,384]{1,0:T(8,128)(2,1)S(1)}, u32[]{:S(2)}, u32[]{:S(2)}) %collective-permute-start.5) | collective-permute-done | bytes 860192 | tf_op jit(solution)/shard_map/ppermute | solution.py:137
  46.6 1.3 constant_dynamic-slice_fusion.1
  48.3 1.3 collective-permute-start.13
  49.8 1.2 collective-permute-start.11
  51.1 2.3 collective-permute-start.12
  53.4 12.3 %collective-permute-done.11.refs_3_ = bf16[384,384]{1,0:T(8,128)(2,1)S(1)} collective-permute-done((bf16[384,384]{1,0:T(8,128)(2,1)S(1)}, bf16[384,384]{1,0:T(8,128)(2,1)S(1)}, u32[]{:S(2)}, u32[]{:S(2)}) %collective-permute-start.11) | collective-permute-done | bytes 294944 | tf_op jit(solution)/shard_map/ppermute | solution.py:137
  65.7 7.9 %collective-permute-done.12.refs_4_ = bf16[384,384]{1,0:T(8,128)(2,1)S(1)} collective-permute-done((bf16[384,384]{1,0:T(8,128)(2,1)S(1)}, bf16[384,384]{1,0:T(8,128)(2,1)S(1)}, u32[]{:S(2)}, u32[]{:S(2)}) %collective-permute-start.12) | collective-permute-done | bytes 294944 | tf_op jit(solution)/shard_map/ppermute | solution.py:137
  76.8 5.0 %collective-permute-start.15 = (bf16[512,384]{1,0:T(8,128)(2,1)S(1)}, bf16[512,384]{1,0:T(8,128)(2,1)S(1)}, u32[]{:S(2)}, u32[]{:S(2)}) collective-permute-start(bf16[512,384]{1,0:T(8,128)(2,1)S(1)} %bitcast.213), channel_id=1, source_target_pairs={{0,1},{1,0},{2,3},{3,2},{4,5},{5,4},{6,7},{7,6},{8,9},{9,8},{10,11... | collective-permute-start | bytes 1179656 | tf_op jit(solution)/shard_map/ppermute | solution.py:71
  85.0 2.2 collective-permute-done.16.refs_10_
  87.3 1.3 collective-permute-start.23
  93.1 13.5 %shard_map.250 = (f32[16,768]{1,0:T(8,128)}, f32[8,384]{1,0:T(8,128)}, bf16[320,768]{1,0:T(8,128)(2,1)}, f32[320,768]{1,0:T(8,128)}, f32[320,1]{1,0:T(8,128)}, /...) custom-call(s32[8]{0:T(128)} %reshape.233.lengths, ...), custom_call_target="tpu_custom_call" | custom-call | flops 3019898880 | bytes 4194304 | tf_op jit(solution)/shard_map/pallas_call | solution.py:1148
  106.7 2.7 collective-permute-done.24.refs_8_.refs_5_
  109.4 1.9 collective-permute-done.23.refs_7_.refs_6_
  115.0 2.4 collective-permute-done.28.refs_11_
  118.1 1.3 collective-permute-start.33
  121.2 15.7 %shard_map.251 = (bf16[320,768]{1,0:T(8,128)(2,1)}, f32[320,768]{1,0:T(8,128)}, f32[320,1]{1,0:T(8,128)}, bf16[320,768]{1,0:T(8,128)(2,1)}, bf16[4,2,2,160,768]{...) custom-call(s32[8]{0:T(128)} %xor.10.slots, ...), custom_call_target="tpu_custom_call" | custom-call | flops 6794772480 | bytes 4194304 | tf_op jit(solution)/shard_map/pallas_call | solution.py:1171
  137.6 2.1 collective-permute-done.37.refs_15_
  143.2 1.3 copy-done.14
  145.7 11.5 %shard_map.252 = (bf16[8,40,768]{2,1,0:T(8,128)(2,1)}, f32[320,768]{1,0:T(8,128)S(1)}, bf16[320,768]{1,0:T(8,128)(2,1)S(1)}, f32[8,768]{1,0:T(8,128)S(1)}, bf16[...) custom-call(s32[8]{0:T(128)S(1)} %copy-done.33, ...), custom_call_target="tpu_custom_call" | custom-call | flops 3019898880 | bytes 4194304 | tf_op jit(solution)/shard_map/pallas_call | solution.py:1190
  157.2 1.7 shard_map.253
  159.3 10.3 %shard_map.254 = (bf16[320,3072]{1,0:T(8,128)(2,1)S(1)}, f32[8,384]{1,0:T(8,128)S(1)}, f32[320,768]{1,0:T(8,128)S(1)}, bf16[320,768]{1,0:T(8,128)(2,1)S(1)}, f32[8,768]{1,0:T(8,128)S(1)}) custom-call(bf16[320,768]{1,0:T(8,128)(2,1)S(1)} %get-tuple-element.384.refs_1_.df, bf16[8,2,2,384,384]{4,3,2,1,0:T(8,128)(2,1)S(1)} %get-tuple-element.385.wout.win, ...), custom_call_target="tpu_custom_call" | custom-call | flops 3019898880 | bytes 4194304 | tf_op jit(solution)/shard_map/pallas_call | solution.py:1211
  169.6 1.4 shard_map.256
  171.1 2.0 shard_map.255
  175.4 8.8 %shard_map.257 = (bf16[320,768]{1,0:T(8,128)(2,1)S(1)}, bf16[2,4,2,160,768]{4,3,2,1,0:T(8,128)(2,1)S(1)}) custom-call(s32[8]{0:T(128)S(1)} %copy-done.34, bf16[320,768]{1,0:T(8,128)(2,1)S(1)} %get-tuple-element.397.dac.refs_1_, bf16[320,768]{1,0:T(8,128)(2,1)S(1)} %copy-done.23, bf16[4,2,2,160,768]{4,3,2,1,0:T(8,128)(2,1)S(1)} %copy-done.2, ...), custom_call_target="tpu_custom_call" | custom-call | flops 1509949440 | bytes 4194304 | tf_op jit(solution)/shard_map/pallas_call | solution.py:1241
  184.3 2.1 shard_map.258
  186.4 3.4 %shard_map.260 = bf16[8,2,272,384]{3,2,1,0:T(8,128)(2,1)S(1)} custom-call(bf16[320,768]{1,0:T(8,128)(2,1)S(1)} %copy-done.10, bf16[320,768]{1,0:T(8,128)(2,1)S(1)} %get-tuple-element.397.dac.refs_1_, bf16[320,768]{1,0:T(8,128)(2,1)S(1)} %copy-done.9, bf16[320,768]{1,0:T(8,128)(2,1)S(1)} %get-tuple-element.443.dqc.refs_3_, bf16[320,768]{1,0:T(8,128)(2,1)S(1)} %copy-done.8, ...), custom_call_target="tpu_custom_call" | custom-call | flops 2579496960 | bytes 4194304 | tf_op jit(solution)/shard_map/pallas_call | solution.py:564
  190.1 2.0 shard_map.259
  194.5 1.3 collective-permute-start.44
  195.8 5.6 %shard_map.264 = (bf16[2,2,160,1024]{3,2,1,0:T(8,128)(2,1)S(1)}, bf16[2,2,160,1024]{3,2,1,0:T(8,128)(2,1)S(1)}, f32[8,768]{1,0:T(8,128)S(1)}) custom-call(bf16[2,4,2,160,768]{4,3,2,1,0:T(8,128)(2,1)S(1)} %get-tuple-element.465.dkv, bf16[2,2,1024,384]{3,2,1,0:T(8,128)(2,1)S(1)} %copy-done.39), custom_call_target="tpu_custom_call" | custom-call | flops 6039797760 | bytes 4194304 | tf_op jit(solution)/shard_map/pallas_call | solution.py:1277
  201.4 7.1 %shard_map.262 = (bf16[3,320,768]{2,1,0:T(8,128)(2,1)S(1)}, f32[8,768]{1,0:T(8,128)S(1)}) custom-call(s32[8]{0:T(128)S(1)} %copy-done.33, bf16[320,768]{1,0:T(8,128)(2,1)S(1)} %get-tuple-element.461.refs_5_.da, bf16[3,320,768]{2,1,0:T(8,128)(2,1)S(1)} %copy-done.37, bf16[2,1,768,384]{3,2,1,0:T(8,128)(2,1)S(1)} %copy-done.38), custom_call_target="tpu_custom_call" | custom-call | flops 1509949440 | bytes 4194304 | tf_op jit(solution)/shard_map/pallas_call | solution.py:1267
  210.0 2.0 collective-permute-done.44
  212.2 4.0 %shard_map.261 = (bf16[4,272,384]{2,1,0:T(8,128)(2,1)S(1)}, bf16[2,272,384]{2,1,0:T(8,128)(2,1)S(1)}, bf16[2,272,384]{2,1,0:T(8,128)(2,1)S(1)}, bf16[3,272,384]{...) custom-call(bf16[320,768]{1,0:T(8,128)(2,1)S(1)} %copy-done.10, ...), custom_call_target="tpu_custom_call" | custom-call | flops 2579496960 | bytes 4194304 | tf_op jit(solution)/shard_map/pallas_call | solution.py:591
  218.8 2.1 collective-permute-start.48
  220.9 2.5 shard_map.265
  223.4 9.1 %collective-permute-done.49 = bf16[928,384]{1,0:T(8,128)(2,1)S(1)} collective-permute-done((bf16[928,384]{1,0:T(8,128)(2,1)S(1)}, bf16[928,384]{1,0:T(8,128)(2,1)S(1)}, u32[]{:S(2)}, u32[]{:S(2)}) %collective-permute-start.49) | collective-permute-done | bytes 712736 | tf_op jit(solution)/shard_map/ppermute | solution.py:137
  232.6 3.2 %collective-permute-done.52 = bf16[4,272,384]{2,1,0:T(8,128)(2,1)S(1)} collective-permute-done((bf16[4,272,384]{2,1,0:T(8,128)(2,1)S(1)}, bf16[4,272,384]{2,1,0:T(8,128)(2,1)S(1)}, u32[]{:S(2)}, u32[]{:S(2)}) %collective-permute-start.52) | collective-permute-done | bytes 835616 | tf_op jit(solution)/shard_map/ppermute | solution.py:137
  237.7 1.5 shard_map.266
  243.1 1.4 collective-permute-start.54
  244.5 1.5 collective-permute-done.55
  246.1 3.7 %collective-permute-done.57 = bf16[4,160,384]{2,1,0:T(8,128)(2,1)S(1)} collective-permute-done((bf16[4,160,384]{2,1,0:T(8,128)(2,1)S(1)}, bf16[4,160,384]{2,1,0:T(8,128)(2,1)S(1)}, u32[]{:S(2)}, u32[]{:S(2)}) %collective-permute-start.57) | collective-permute-done | bytes 491552 | tf_op jit(solution)/shard_map/ppermute | solution.py:137
  249.9 7.5 %collective-permute-done.56 = bf16[784,384]{1,0:T(8,128)(2,1)S(1)} collective-permute-done((bf16[784,384]{1,0:T(8,128)(2,1)S(1)}, bf16[784,384]{1,0:T(8,128)(2,1)S(1)}, u32[]{:S(2)}, u32[]{:S(2)}) %collective-permute-start.56) | collective-permute-done | bytes 602144 | tf_op jit(solution)/shard_map/ppermute | solution.py:137
  257.5 2.4 collective-permute-done.54
  263.9 2.9 collective-permute-done.60
  267.0 2.8 collective-permute-done.58
  270.2 1.4 collective-permute-start.66
  272.5 5.2 %collective-permute-done.61 = bf16[160,384]{1,0:T(8,128)(2,1)S(1)} collective-permute-done((bf16[160,384]{1,0:T(8,128)(2,1)S(1)}, bf16[160,384]{1,0:T(8,128)(2,1)S(1)}, u32[]{:S(2)}, u32[]{:S(2)}) %collective-permute-start.61) | collective-permute-done | bytes 122912 | tf_op jit(solution)/shard_map/ppermute | solution.py:137
  278.8 3.9 %collective-permute-done.62 = bf16[160,384]{1,0:T(8,128)(2,1)S(1)} collective-permute-done((bf16[160,384]{1,0:T(8,128)(2,1)S(1)}, bf16[160,384]{1,0:T(8,128)(2,1)S(1)}, u32[]{:S(2)}, u32[]{:S(2)}) %collective-permute-start.62) | collective-permute-done | bytes 122912 | tf_op jit(solution)/shard_map/ppermute | solution.py:1316
  283.8 10.3 %collective-permute-start.71 = (bf16[2,192,384]{2,1,0:T(8,128)(2,1)S(1)}, bf16[2,192,384]{2,1,0:T(8,128)(2,1)S(1)}, u32[]{:S(2)}, u32[]{:S(2)}) collective-permute-start(bf16[2,192,384]{2,1,0:T(8,128)(2,1)S(1)} %add_convert_fusion.5.mine), channel_id=1, source_target_pairs={{0,1},{1,0},{2,3},{3,2},{4,5},{5,4},{6,7},{7,6},{8,9},{9,8},{10,11... | collective-permute-start | bytes 884744 | tf_op jit(solution)/shard_map/ppermute | solution.py:496
  294.2 3.1 collective-permute-start.69
  297.5 2.3 collective-permute-start.67
  300.0 1.4 copy.29
  305.3 1.3 shard_map.269
  (314 shorter events, 55.3 us)
Async XLA Ops:
  4.8 22.2 %collective-permute-start.4 = (bf16[2,160,1024]{2,1,0:T(8,128)(2,1)}, bf16[2,160,1024]{2,1,0:T(8,128)(2,1)}, u32[]{:S(2)}, u32[]{:S(2)}) collective-permute-start(bf16[2,160,1024]{2,1,0:T(8,128)(2,1)} %shard_map.248.refs_17_), channel_id=1, source_target_pairs={{0,2},{2,0},{1,3},{3,1},{4,6},{6,4},{5,7},{7,5},{8,10},{10,8},{9,1... | collective-permute-start | bytes 1966088 | tf_op jit(solution)/shard_map/ppermute | solution.py:137
  6.9 20.2 %collective-permute-start = (bf16[2,256,384]{2,1,0:T(8,128)(2,1)S(1)}, bf16[2,256,384]{2,1,0:T(8,128)(2,1)S(1)}, u32[]{:S(2)}, u32[]{:S(2)}) collective-permute-start(bf16[2,256,384]{2,1,0:T(8,128)(2,1)S(1)} %get-tuple-element.285), channel_id=1, source_target_pairs={{0,8},{8,0},{4,12},{12,4},{16,24},{24,16},{20,28},{28,20},{1,9},{9... | collective-permute-start | bytes 1179656 | tf_op jit(solution)/shard_map/ppermute | solution.py:137
  8.1 18.9 %collective-permute-start.3 = (bf16[2,256,384]{2,1,0:T(8,128)(2,1)S(1)}, bf16[2,256,384]{2,1,0:T(8,128)(2,1)S(1)}, u32[]{:S(2)}, u32[]{:S(2)}) collective-permute-start(bf16[2,256,384]{2,1,0:T(8,128)(2,1)S(1)} %get-tuple-element.285), channel_id=1, source_target_pairs={{0,4},{4,0},{8,12},{12,8},{16,20},{20,16},{24,28},{28,24},{1,5},{5... | collective-permute-start | bytes 1179656 | tf_op jit(solution)/shard_map/ppermute | solution.py:137
  9.4 10.5 %collective-permute-start.1 = (bf16[256,384]{1,0:T(8,128)(2,1)S(1)}, bf16[256,384]{1,0:T(8,128)(2,1)S(1)}, u32[]{:S(2)}, u32[]{:S(2)}) collective-permute-start(bf16[256,384]{1,0:T(8,128)(2,1)S(1)} %get-tuple-element.284), channel_id=1, source_target_pairs={{0,16},{16,0},{4,20},{20,4},{8,24},{24,8},{12,28},{28,12},{1,17},{... | collective-permute-start | bytes 589832 | tf_op jit(solution)/shard_map/ppermute | solution.py:137
  11.7 15.3 %collective-permute-start.2 = (bf16[256,384]{1,0:T(8,128)(2,1)S(1)}, bf16[256,384]{1,0:T(8,128)(2,1)S(1)}, u32[]{:S(2)}, u32[]{:S(2)}) collective-permute-start(bf16[256,384]{1,0:T(8,128)(2,1)S(1)} %get-tuple-element.284), channel_id=1, source_target_pairs={{0,24},{24,0},{4,28},{28,4},{8,16},{16,8},{12,20},{20,12},{1,25},{... | collective-permute-start | bytes 589832 | tf_op jit(solution)/shard_map/ppermute | solution.py:137
  28.0 18.7 %collective-permute-start.5 = (bf16[1120,384]{1,0:T(8,128)(2,1)S(1)}, bf16[1120,384]{1,0:T(8,128)(2,1)S(1)}, u32[]{:S(2)}, u32[]{:S(2)}) collective-permute-start(bf16[1120,384]{1,0:T(8,128)(2,1)S(1)} %pad_maximum_fusion.4), channel_id=1, source_target_pairs={{0,4},{4,0},{8,12},{12,8},{16,20},{20,16},{24,28},{28,24},{1,5},{5... | collective-permute-start | bytes 2580488 | tf_op jit(solution)/shard_map/ppermute | solution.py:137
  29.2 11.6 %collective-permute-start.6 = (bf16[512,384]{1,0:T(8,128)(2,1)S(1)}, bf16[512,384]{1,0:T(8,128)(2,1)S(1)}, u32[]{:S(2)}, u32[]{:S(2)}) collective-permute-start(bf16[512,384]{1,0:T(8,128)(2,1)S(1)} %pad_maximum_fusion.15), channel_id=1, source_target_pairs={{0,2},{2,0},{1,3},{3,1},{4,6},{6,4},{5,7},{7,5},{8,10},{10,8},{9,1... | collective-permute-start | bytes 1179656 | tf_op jit(solution)/shard_map/ppermute | solution.py:137
  29.4 11.4 %collective-permute-start.7 = (bf16[2,176,384]{2,1,0:T(8,128)(2,1)S(1)}, bf16[2,176,384]{2,1,0:T(8,128)(2,1)}, u32[]{:S(2)}, u32[]{:S(2)}) collective-permute-start(bf16[2,176,384]{2,1,0:T(8,128)(2,1)S(1)} %get-tuple-element.295), channel_id=1, source_target_pairs={{0,8},{8,0},{4,12},{12,4},{16,24},{24,16},{20,28},{28,20},{1,9},{9... | collective-permute-start | bytes 811016 | tf_op jit(solution)/shard_map/ppermute | solution.py:137
  29.5 5.6 %collective-permute-start.8 = (bf16[176,384]{1,0:T(8,128)(2,1)S(1)}, bf16[176,384]{1,0:T(8,128)(2,1)S(1)}, u32[]{:S(2)}, u32[]{:S(2)}) collective-permute-start(bf16[176,384]{1,0:T(8,128)(2,1)S(1)} %get-tuple-element.297), channel_id=1, source_target_pairs={{0,16},{16,0},{4,20},{20,4},{8,24},{24,8},{12,28},{28,12},{1,17},{... | collective-permute-start | bytes 405512 | tf_op jit(solution)/shard_map/ppermute | solution.py:137
  30.8 9.6 %collective-permute-start.9 = (bf16[176,384]{1,0:T(8,128)(2,1)S(1)}, bf16[176,384]{1,0:T(8,128)(2,1)S(1)}, u32[]{:S(2)}, u32[]{:S(2)}) collective-permute-start(bf16[176,384]{1,0:T(8,128)(2,1)S(1)} %get-tuple-element.297), channel_id=1, source_target_pairs={{0,24},{24,0},{4,28},{28,4},{8,16},{16,8},{12,20},{20,12},{1,25},{... | collective-permute-start | bytes 405512 | tf_op jit(solution)/shard_map/ppermute | solution.py:137
  48.3 25.3 %collective-permute-start.13 = (bf16[1552,384]{1,0:T(8,128)(2,1)S(1)}, bf16[1552,384]{1,0:T(8,128)(2,1)S(1)}, u32[]{:S(2)}, u32[]{:S(2)}) collective-permute-start(bf16[1552,384]{1,0:T(8,128)(2,1)S(1)} %pad_maximum_fusion), channel_id=1, source_target_pairs={{0,4},{4,0},{8,12},{12,8},{16,20},{20,16},{24,28},{28,24},{1,5},{5... | collective-permute-start | bytes 3575816 | tf_op jit(solution)/shard_map/ppermute | solution.py:137
  49.6 24.0 %collective-permute-start.14 = (bf16[864,384]{1,0:T(8,128)(2,1)S(1)}, bf16[864,384]{1,0:T(8,128)(2,1)S(1)}, u32[]{:S(2)}, u32[]{:S(2)}) collective-permute-start(bf16[864,384]{1,0:T(8,128)(2,1)S(1)} %pad_maximum_fusion.9), channel_id=1, source_target_pairs={{0,2},{2,0},{1,3},{3,1},{4,6},{6,4},{5,7},{7,5},{8,10},{10,8},{9,1... | collective-permute-start | bytes 1990664 | tf_op jit(solution)/shard_map/ppermute | solution.py:137
  49.8 23.7 %collective-permute-start.10 = (bf16[2,384,384]{2,1,0:T(8,128)(2,1)S(1)}, bf16[2,384,384]{2,1,0:T(8,128)(2,1)S(1)}, u32[]{:S(2)}, u32[]{:S(2)}) collective-permute-start(bf16[2,384,384]{2,1,0:T(8,128)(2,1)S(1)} %get-tuple-element.305), channel_id=1, source_target_pairs={{0,8},{8,0},{4,12},{12,4},{16,24},{24,16},{20,28},{28,20},{1,9},{9... | collective-permute-start | bytes 1769480 | tf_op jit(solution)/shard_map/ppermute | solution.py:137
  49.8 15.8 %collective-permute-start.11 = (bf16[384,384]{1,0:T(8,128)(2,1)S(1)}, bf16[384,384]{1,0:T(8,128)(2,1)S(1)}, u32[]{:S(2)}, u32[]{:S(2)}) collective-permute-start(bf16[384,384]{1,0:T(8,128)(2,1)S(1)} %get-tuple-element.307), channel_id=1, source_target_pairs={{0,16},{16,0},{4,20},{20,4},{8,24},{24,8},{12,28},{28,12},{1,17},{... | collective-permute-start | bytes 884744 | tf_op jit(solution)/shard_map/ppermute | solution.py:137
  51.1 22.5 %collective-permute-start.12 = (bf16[384,384]{1,0:T(8,128)(2,1)S(1)}, bf16[384,384]{1,0:T(8,128)(2,1)S(1)}, u32[]{:S(2)}, u32[]{:S(2)}) collective-permute-start(bf16[384,384]{1,0:T(8,128)(2,1)S(1)} %get-tuple-element.307), channel_id=1, source_target_pairs={{0,24},{24,0},{4,28},{28,4},{8,16},{16,8},{12,20},{20,12},{1,25},{... | collective-permute-start | bytes 884744 | tf_op jit(solution)/shard_map/ppermute | solution.py:137
  76.8 8.0 %collective-permute-start.15 = (bf16[512,384]{1,0:T(8,128)(2,1)S(1)}, bf16[512,384]{1,0:T(8,128)(2,1)S(1)}, u32[]{:S(2)}, u32[]{:S(2)}) collective-permute-start(bf16[512,384]{1,0:T(8,128)(2,1)S(1)} %bitcast.213), channel_id=1, source_target_pairs={{0,1},{1,0},{2,3},{3,2},{4,5},{5,4},{6,7},{7,6},{8,9},{9,8},{10,11... | collective-permute-start | bytes 1179656 | tf_op jit(solution)/shard_map/ppermute | solution.py:71
  82.4 8.3 %collective-permute-start.20 = (bf16[1120,384]{1,0:T(8,128)(2,1)S(1)}, bf16[1120,384]{1,0:T(8,128)(2,1)S(1)}, u32[]{:S(2)}, u32[]{:S(2)}) collective-permute-start(bf16[1120,384]{1,0:T(8,128)(2,1)S(1)} %collective-permute-done.5.refs_6_.refs_2_), channel_id=1, source_target_pairs={{0,1},{1,0},{2,3},{3,2},{4,5},{5,4},{6,7},{7,6},{8,9},{9,8},{10,11... | collective-permute-start | bytes 2580488 | tf_op jit(solution)/shard_map/ppermute | solution.py:71
  82.4 10.7 %collective-permute-start.21 = (bf16[1552,384]{1,0:T(8,128)(2,1)S(1)}, bf16[1552,384]{1,0:T(8,128)(2,1)}, u32[]{:S(2)}, u32[]{:S(2)}) collective-permute-start(bf16[1552,384]{1,0:T(8,128)(2,1)S(1)} %collective-permute-done.13.refs_7_.refs_6_.refs_2_), channel_id=1, source_target_pairs={{0,1},{1,0},{2,3},{3,2},{4,5},{5,4},{6,7},{7,6},{8,9},{9,8},{10,11... | collective-permute-start | bytes 3575816 | tf_op jit(solution)/shard_map/ppermute | solution.py:71
  84.4 5.5 %collective-permute-start.22 = (bf16[864,384]{1,0:T(8,128)(2,1)S(1)}, bf16[864,384]{1,0:T(8,128)(2,1)S(1)}, u32[]{:S(2)}, u32[]{:S(2)}) collective-permute-start(bf16[864,384]{1,0:T(8,128)(2,1)S(1)} %collective-permute-done.14.refs_8_.refs_5_), channel_id=1, source_target_pairs={{0,1},{1,0},{2,3},{3,2},{4,5},{5,4},{6,7},{7,6},{8,9},{9,8},{10,11... | collective-permute-start | bytes 1990664 | tf_op jit(solution)/shard_map/ppermute | solution.py:71
  87.3 24.0 %collective-permute-start.23 = (bf16[1328,384]{1,0:T(8,128)(2,1)}, bf16[1328,384]{1,0:T(8,128)(2,1)S(1)}, u32[]{:S(2)}, u32[]{:S(2)}) collective-permute-start(bf16[1328,384]{1,0:T(8,128)(2,1)} %pad_maximum_fusion.1), channel_id=1, source_target_pairs={{0,4},{4,0},{8,12},{12,8},{16,20},{20,16},{24,28},{28,24},{1,5},{5... | collective-permute-start | bytes 3059720 | tf_op jit(solution)/shard_map/ppermute | solution.py:137
  88.8 20.6 %collective-permute-start.24 = (bf16[1120,384]{1,0:T(8,128)(2,1)}, bf16[1120,384]{1,0:T(8,128)(2,1)}, u32[]{:S(2)}, u32[]{:S(2)}) collective-permute-start(bf16[1120,384]{1,0:T(8,128)(2,1)} %pad_maximum_fusion.5), channel_id=1, source_target_pairs={{0,2},{2,0},{1,3},{3,1},{4,6},{6,4},{5,7},{7,5},{8,10},{10,8},{9,1... | collective-permute-start | bytes 2580488 | tf_op jit(solution)/shard_map/ppermute | solution.py:137
  90.0 16.7 %collective-permute-start.25 = (bf16[2,160,1024]{2,1,0:T(8,128)(2,1)}, bf16[2,160,1024]{2,1,0:T(8,128)(2,1)}, u32[]{:S(2)}, u32[]{:S(2)}) collective-permute-start(bf16[2,160,1024]{2,1,0:T(8,128)(2,1)} %shard_map.248.refs_17_), channel_id=1, source_target_pairs={{0,1},{1,0},{2,3},{3,2},{4,5},{5,4},{6,7},{7,6},{8,9},{9,8},{10,11... | collective-permute-start | bytes 1966088 | tf_op jit(solution)/shard_map/ppermute | solution.py:137
  91.8 14.9 %collective-permute-start.26 = (bf16[2,160,1024]{2,1,0:T(8,128)(2,1)}, bf16[2,160,1024]{2,1,0:T(8,128)(2,1)}, u32[]{:S(2)}, u32[]{:S(2)}) collective-permute-start(bf16[2,160,1024]{2,1,0:T(8,128)(2,1)} %collective-permute-done.4.refs_19_), channel_id=1, source_target_pairs={{0,1},{1,0},{2,3},{3,2},{4,5},{5,4},{6,7},{7,6},{8,9},{9,8},{10,11... | collective-permute-start | bytes 1966088 | tf_op jit(solution)/shard_map/ppermute | solution.py:137
  112.2 7.7 %collective-permute-start.30 = (bf16[1328,384]{1,0:T(8,128)(2,1)S(1)}, bf16[1328,384]{1,0:T(8,128)(2,1)S(1)}, u32[]{:S(2)}, u32[]{:S(2)}) collective-permute-start(bf16[1328,384]{1,0:T(8,128)(2,1)S(1)} %collective-permute-done.23.refs_7_.refs_6_), channel_id=1, source_target_pairs={{0,1},{1,0},{2,3},{3,2},{4,5},{5,4},{6,7},{7,6},{8,9},{9,8},{10,11... | collective-permute-start | bytes 3059720 | tf_op jit(solution)/shard_map/ppermute | solution.py:71
  113.4 6.0 %collective-permute-start.31 = (bf16[1120,384]{1,0:T(8,128)(2,1)}, bf16[1120,384]{1,0:T(8,128)(2,1)}, u32[]{:S(2)}, u32[]{:S(2)}) collective-permute-start(bf16[1120,384]{1,0:T(8,128)(2,1)} %collective-permute-done.24.refs_8_.refs_5_), channel_id=1, source_target_pairs={{0,1},{1,0},{2,3},{3,2},{4,5},{5,4},{6,7},{7,6},{8,9},{9,8},{10,11... | collective-permute-start | bytes 2580488 | tf_op jit(solution)/shard_map/ppermute | solution.py:71
  113.4 4.8 %collective-permute-start.27 = (bf16[352,384]{1,0:T(8,128)(2,1)}, bf16[352,384]{1,0:T(8,128)(2,1)}, u32[]{:S(2)}, u32[]{:S(2)}) collective-permute-start(bf16[352,384]{1,0:T(8,128)(2,1)} %bitcast.22.refs_1_), channel_id=1, source_target_pairs={{0,1},{1,0},{2,3},{3,2},{4,5},{5,4},{6,7},{7,6},{8,9},{9,8},{10,11... | collective-permute-start | bytes 811016 | tf_op jit(solution)/shard_map/ppermute | solution.py:71
  117.4 19.6 %collective-permute-start.35 = (bf16[384,384]{1,0:T(8,128)(2,1)S(1)}, bf16[384,384]{1,0:T(8,128)(2,1)}, u32[]{:S(2)}, u32[]{:S(2)}) collective-permute-start(bf16[384,384]{1,0:T(8,128)(2,1)S(1)} %collective-permute-done.11.refs_3_), channel_id=1, source_target_pairs={{0,1},{1,0},{2,3},{3,2},{4,5},{5,4},{6,7},{7,6},{8,9},{9,8},{10,11... | collective-permute-start | bytes 884744 | tf_op jit(solution)/shard_map/ppermute | solution.py:71
  117.8 19.2 %collective-permute-start.36 = (bf16[384,384]{1,0:T(8,128)(2,1)S(1)}, bf16[384,384]{1,0:T(8,128)(2,1)}, u32[]{:S(2)}, u32[]{:S(2)}) collective-permute-start(bf16[384,384]{1,0:T(8,128)(2,1)S(1)} %collective-permute-done.12.refs_4_), channel_id=1, source_target_pairs={{0,1},{1,0},{2,3},{3,2},{4,5},{5,4},{6,7},{7,6},{8,9},{9,8},{10,11... | collective-permute-start | bytes 884744 | tf_op jit(solution)/shard_map/ppermute | solution.py:71
  118.1 18.8 %collective-permute-start.33 = (bf16[384,384]{1,0:T(8,128)(2,1)}, bf16[384,384]{1,0:T(8,128)(2,1)}, u32[]{:S(2)}, u32[]{:S(2)}) collective-permute-start(bf16[384,384]{1,0:T(8,128)(2,1)} %get-tuple-element.360), channel_id=1, source_target_pairs={{0,4},{4,0},{8,12},{12,8},{16,20},{20,16},{24,28},{28,24},{1,5},{5... | collective-permute-start | bytes 884744 | tf_op jit(solution)/shard_map/ppermute | solution.py:137
  119.4 17.6 %collective-permute-start.34 = (bf16[768,384]{1,0:T(8,128)(2,1)S(1)}, bf16[768,384]{1,0:T(8,128)(2,1)}, u32[]{:S(2)}, u32[]{:S(2)}) collective-permute-start(bf16[768,384]{1,0:T(8,128)(2,1)S(1)} %bitcast.178), channel_id=1, source_target_pairs={{0,1},{1,0},{2,3},{3,2},{4,5},{5,4},{6,7},{7,6},{8,9},{9,8},{10,11... | collective-permute-start | bytes 1769480 | tf_op jit(solution)/shard_map/ppermute | solution.py:71
  119.9 17.1 %collective-permute-start.32 = (bf16[2,384,384]{2,1,0:T(8,128)(2,1)}, bf16[2,384,384]{2,1,0:T(8,128)(2,1)}, u32[]{:S(2)}, u32[]{:S(2)}) collective-permute-start(bf16[2,384,384]{2,1,0:T(8,128)(2,1)} %bitcast.207), channel_id=1, source_target_pairs={{0,2},{2,0},{1,3},{3,1},{4,6},{6,4},{5,7},{7,5},{8,10},{10,8},{9,1... | collective-permute-start | bytes 1769480 | tf_op jit(solution)/shard_map/ppermute | solution.py:137
  158.9 12.2 %collective-permute-start.39 = (bf16[8,2,192,384]{3,2,1,0:T(8,128)(2,1)S(1)}, bf16[8,2,192,384]{3,2,1,0:T(8,128)(2,1)S(1)}, u32[]{:S(2)}, u32[]{:S(2)}) collective-permute-start(bf16[8,2,192,384]{3,2,1,0:T(8,128)(2,1)S(1)} %shard_map.253), channel_id=1, source_target_pairs={{0,1},{1,0},{2,3},{3,2},{4,5},{5,4},{6,7},{7,6},{8,9},{9,8},{10,11... | collective-permute-start | bytes 7077896 | tf_op jit(solution)/shard_map/ppermute | solution.py:137
  173.1 17.0 %collective-permute-start.42 = (bf16[8,2,192,384]{3,2,1,0:T(8,128)(2,1)S(1)}, bf16[8,2,192,384]{3,2,1,0:T(8,128)(2,1)S(1)}, u32[]{:S(2)}, u32[]{:S(2)}) collective-permute-start(bf16[8,2,192,384]{3,2,1,0:T(8,128)(2,1)S(1)} %shard_map.256), channel_id=1, source_target_pairs={{0,1},{1,0},{2,3},{3,2},{4,5},{5,4},{6,7},{7,6},{8,9},{9,8},{10,11... | collective-permute-start | bytes 7077896 | tf_op jit(solution)/shard_map/ppermute | solution.py:137
  173.3 16.5 %collective-permute-start.41 = (bf16[2,192,384]{2,1,0:T(8,128)(2,1)S(1)}, bf16[2,192,384]{2,1,0:T(8,128)(2,1)S(1)}, u32[]{:S(2)}, u32[]{:S(2)}) collective-permute-start(bf16[2,192,384]{2,1,0:T(8,128)(2,1)S(1)} %get-tuple-element.409), channel_id=1, source_target_pairs={{0,8},{8,0},{4,12},{12,4},{16,24},{24,16},{20,28},{28,20},{1,9},{9... | collective-permute-start | bytes 884744 | tf_op jit(solution)/shard_map/ppermute | solution.py:137
  173.3 16.5 %collective-permute-start.43 = (bf16[2,192,384]{2,1,0:T(8,128)(2,1)S(1)}, bf16[2,192,384]{2,1,0:T(8,128)(2,1)S(1)}, u32[]{:S(2)}, u32[]{:S(2)}) collective-permute-start(bf16[2,192,384]{2,1,0:T(8,128)(2,1)S(1)} %get-tuple-element.414), channel_id=1, source_target_pairs={{0,4},{4,0},{8,12},{12,8},{16,20},{20,16},{24,28},{28,24},{1,5},{5... | collective-permute-start | bytes 884744 | tf_op jit(solution)/shard_map/ppermute | solution.py:137
  174.3 15.5 %collective-permute-start.40 = (bf16[4,192,384]{2,1,0:T(8,128)(2,1)S(1)}, bf16[4,192,384]{2,1,0:T(8,128)(2,1)S(1)}, u32[]{:S(2)}, u32[]{:S(2)}) collective-permute-start(bf16[4,192,384]{2,1,0:T(8,128)(2,1)S(1)} %get-tuple-element.407), channel_id=1, source_target_pairs={{0,2},{2,0},{1,3},{3,1},{4,6},{6,4},{5,7},{7,5},{8,10},{10,8},{9,1... | collective-permute-start | bytes 1769480 | tf_op jit(solution)/shard_map/ppermute | solution.py:137
  192.2 20.0 %collective-permute-start.45 = (bf16[8,2,272,384]{3,2,1,0:T(8,128)(2,1)S(1)}, bf16[8,2,272,384]{3,2,1,0:T(8,128)(2,1)S(1)}, u32[]{:S(2)}, u32[]{:S(2)}) collective-permute-start(bf16[8,2,272,384]{3,2,1,0:T(8,128)(2,1)S(1)} %shard_map.260), channel_id=1, source_target_pairs={{0,1},{1,0},{2,3},{3,2},{4,5},{5,4},{6,7},{7,6},{8,9},{9,8},{10,11... | collective-permute-start | bytes 10027016 | tf_op jit(solution)/shard_map/ppermute | solution.py:137
  193.2 16.6 %collective-permute-start.47 = (bf16[576,384]{1,0:T(8,128)(2,1)S(1)}, bf16[576,384]{1,0:T(8,128)(2,1)S(1)}, u32[]{:S(2)}, u32[]{:S(2)}) collective-permute-start(bf16[576,384]{1,0:T(8,128)(2,1)S(1)} %pad_maximum_fusion.12), channel_id=1, source_target_pairs={{0,8},{8,0},{4,12},{12,4},{16,24},{24,16},{20,28},{28,20},{1,9},{9... | collective-permute-start | bytes 1327112 | tf_op jit(solution)/shard_map/ppermute | solution.py:137
  193.8 16.0 %collective-permute-start.46 = (bf16[4,192,384]{2,1,0:T(8,128)(2,1)S(1)}, bf16[4,192,384]{2,1,0:T(8,128)(2,1)S(1)}, u32[]{:S(2)}, u32[]{:S(2)}) collective-permute-start(bf16[4,192,384]{2,1,0:T(8,128)(2,1)S(1)} %get-tuple-element.456), channel_id=1, source_target_pairs={{0,2},{2,0},{1,3},{3,1},{4,6},{6,4},{5,7},{7,5},{8,10},{10,8},{9,1... | collective-permute-start | bytes 1769480 | tf_op jit(solution)/shard_map/ppermute | solution.py:137
  194.5 17.4 %collective-permute-start.44 = (bf16[960,384]{1,0:T(8,128)(2,1)S(1)}, bf16[960,384]{1,0:T(8,128)(2,1)S(1)}, u32[]{:S(2)}, u32[]{:S(2)}) collective-permute-start(bf16[960,384]{1,0:T(8,128)(2,1)S(1)} %pad_maximum_fusion.7), channel_id=1, source_target_pairs={{0,4},{4,0},{8,12},{12,8},{16,20},{20,16},{24,28},{28,24},{1,5},{5... | collective-permute-start | bytes 2211848 | tf_op jit(solution)/shard_map/ppermute | solution.py:137
  216.4 16.1 %collective-permute-start.49 = (bf16[928,384]{1,0:T(8,128)(2,1)S(1)}, bf16[928,384]{1,0:T(8,128)(2,1)S(1)}, u32[]{:S(2)}, u32[]{:S(2)}) collective-permute-start(bf16[928,384]{1,0:T(8,128)(2,1)S(1)} %pad_maximum_fusion.8), channel_id=1, source_target_pairs={{0,8},{8,0},{4,12},{12,4},{16,24},{24,16},{20,28},{28,20},{1,9},{9... | collective-permute-start | bytes 2138120 | tf_op jit(solution)/shard_map/ppermute | solution.py:137
  217.4 18.3 %collective-permute-start.52 = (bf16[4,272,384]{2,1,0:T(8,128)(2,1)S(1)}, bf16[4,272,384]{2,1,0:T(8,128)(2,1)S(1)}, u32[]{:S(2)}, u32[]{:S(2)}) collective-permute-start(bf16[4,272,384]{2,1,0:T(8,128)(2,1)S(1)} %get-tuple-element.513), channel_id=1, source_target_pairs={{0,2},{2,0},{1,3},{3,1},{4,6},{6,4},{5,7},{7,5},{8,10},{10,8},{9,1... | collective-permute-start | bytes 2506760 | tf_op jit(solution)/shard_map/ppermute | solution.py:137
  218.2 18.6 %collective-permute-start.50 = (bf16[1120,384]{1,0:T(8,128)(2,1)S(1)}, bf16[1120,384]{1,0:T(8,128)(2,1)S(1)}, u32[]{:S(2)}, u32[]{:S(2)}) collective-permute-start(bf16[1120,384]{1,0:T(8,128)(2,1)S(1)} %pad_maximum_fusion.6), channel_id=1, source_target_pairs={{0,4},{4,0},{8,12},{12,8},{16,20},{20,16},{24,28},{28,24},{1,5},{5... | collective-permute-start | bytes 2580488 | tf_op jit(solution)/shard_map/ppermute | solution.py:137
  218.8 18.3 %collective-permute-start.48 = (bf16[2,2,160,1024]{3,2,1,0:T(8,128)(2,1)S(1)}, bf16[2,2,160,1024]{3,2,1,0:T(8,128)(2,1)S(1)}, u32[]{:S(2)}, u32[]{:S(2)}) collective-permute-start(bf16[2,2,160,1024]{3,2,1,0:T(8,128)(2,1)S(1)} %get-tuple-element.501), channel_id=1, source_target_pairs={{0,1},{1,0},{2,3},{3,2},{4,5},{5,4},{6,7},{7,6},{8,9},{9,8},{10,11... | collective-permute-start | bytes 3932168 | tf_op jit(solution)/shard_map/ppermute | solution.py:137
  220.9 16.8 %collective-permute-start.51 = (bf16[8,2,144,384]{3,2,1,0:T(8,128)(2,1)S(1)}, bf16[8,2,144,384]{3,2,1,0:T(8,128)(2,1)S(1)}, u32[]{:S(2)}, u32[]{:S(2)}) collective-permute-start(bf16[8,2,144,384]{3,2,1,0:T(8,128)(2,1)S(1)} %shard_map.263), channel_id=1, source_target_pairs={{0,1},{1,0},{2,3},{3,2},{4,5},{5,4},{6,7},{7,6},{8,9},{9,8},{10,11... | collective-permute-start | bytes 5308424 | tf_op jit(solution)/shard_map/ppermute | solution.py:137
  239.4 6.6 %collective-permute-start.55 = (bf16[192,384]{1,0:T(8,128)(2,1)S(1)}, bf16[192,384]{1,0:T(8,128)(2,1)S(1)}, u32[]{:S(2)}, u32[]{:S(2)}) collective-permute-start(bf16[192,384]{1,0:T(8,128)(2,1)S(1)} %fusion.13), channel_id=1, source_target_pairs={{0,16},{16,0},{4,20},{20,4},{8,24},{24,8},{12,28},{28,12},{1,17},{... | collective-permute-start | bytes 442376 | tf_op jit(solution)/shard_map/ppermute | solution.py:137
  240.4 9.5 %collective-permute-start.57 = (bf16[4,160,384]{2,1,0:T(8,128)(2,1)S(1)}, bf16[4,160,384]{2,1,0:T(8,128)(2,1)S(1)}, u32[]{:S(2)}, u32[]{:S(2)}) collective-permute-start(bf16[4,160,384]{2,1,0:T(8,128)(2,1)S(1)} %get-tuple-element.524), channel_id=1, source_target_pairs={{0,2},{2,0},{1,3},{3,1},{4,6},{6,4},{5,7},{7,5},{8,10},{10,8},{9,1... | collective-permute-start | bytes 1474568 | tf_op jit(solution)/shard_map/ppermute | solution.py:137
  241.1 16.3 %collective-permute-start.56 = (bf16[784,384]{1,0:T(8,128)(2,1)S(1)}, bf16[784,384]{1,0:T(8,128)(2,1)S(1)}, u32[]{:S(2)}, u32[]{:S(2)}) collective-permute-start(bf16[784,384]{1,0:T(8,128)(2,1)S(1)} %pad_maximum_fusion.10), channel_id=1, source_target_pairs={{0,8},{8,0},{4,12},{12,4},{16,24},{24,16},{20,28},{28,20},{1,9},{9... | collective-permute-start | bytes 1806344 | tf_op jit(solution)/shard_map/ppermute | solution.py:137
  242.2 57.6 %collective-permute-start.53 = (bf16[2,160,1024]{2,1,0:T(8,128)(2,1)S(1)}, bf16[2,160,1024]{2,1,0:T(8,128)(2,1)S(1)}, u32[]{:S(2)}, u32[]{:S(2)}) collective-permute-start(bf16[2,160,1024]{2,1,0:T(8,128)(2,1)S(1)} %fusion.1), channel_id=1, source_target_pairs={{0,2},{2,0},{1,3},{3,1},{4,6},{6,4},{5,7},{7,5},{8,10},{10,8},{9,1... | collective-permute-start | bytes 1966088 | tf_op jit(solution)/shard_map/ppermute | solution.py:137
  243.1 16.8 %collective-permute-start.54 = (bf16[1136,384]{1,0:T(8,128)(2,1)S(1)}, bf16[1136,384]{1,0:T(8,128)(2,1)S(1)}, u32[]{:S(2)}, u32[]{:S(2)}) collective-permute-start(bf16[1136,384]{1,0:T(8,128)(2,1)S(1)} %pad_maximum_fusion.3), channel_id=1, source_target_pairs={{0,4},{4,0},{8,12},{12,8},{16,20},{20,16},{24,28},{28,24},{1,5},{5... | collective-permute-start | bytes 2617352 | tf_op jit(solution)/shard_map/ppermute | solution.py:137
  260.2 6.6 %collective-permute-start.60 = (bf16[192,384]{1,0:T(8,128)(2,1)S(1)}, bf16[192,384]{1,0:T(8,128)(2,1)S(1)}, u32[]{:S(2)}, u32[]{:S(2)}) collective-permute-start(bf16[192,384]{1,0:T(8,128)(2,1)S(1)} %fusion.11), channel_id=1, source_target_pairs={{0,16},{16,0},{4,20},{20,4},{8,24},{24,8},{12,28},{28,12},{1,17},{... | collective-permute-start | bytes 442376 | tf_op jit(solution)/shard_map/ppermute | solution.py:137
  261.2 22.4 %collective-permute-start.70 = (bf16[2,192,384]{2,1,0:T(8,128)(2,1)S(1)}, bf16[2,192,384]{2,1,0:T(8,128)(2,1)S(1)}, u32[]{:S(2)}, u32[]{:S(2)}) collective-permute-start(bf16[2,192,384]{2,1,0:T(8,128)(2,1)S(1)} %pad_maximum_fusion.17), channel_id=1, source_target_pairs={{0,2},{2,0},{1,3},{3,1},{4,6},{6,4},{5,7},{7,5},{8,10},{10,8},{9,1... | collective-permute-start | bytes 884744 | tf_op jit(solution)/shard_map/ppermute | solution.py:137
  261.9 7.9 %collective-permute-start.58 = (bf16[432,384]{1,0:T(8,128)(2,1)S(1)}, bf16[432,384]{1,0:T(8,128)(2,1)S(1)}, u32[]{:S(2)}, u32[]{:S(2)}) collective-permute-start(bf16[432,384]{1,0:T(8,128)(2,1)S(1)} %pad_maximum_fusion.16), channel_id=1, source_target_pairs={{0,8},{8,0},{4,12},{12,4},{16,24},{24,16},{20,28},{28,20},{1,9},{9... | collective-permute-start | bytes 995336 | tf_op jit(solution)/shard_map/ppermute | solution.py:137
  262.8 7.0 %collective-permute-start.59 = (bf16[3,160,384]{2,1,0:T(8,128)(2,1)S(1)}, bf16[3,160,384]{2,1,0:T(8,128)(2,1)S(1)}, u32[]{:S(2)}, u32[]{:S(2)}) collective-permute-start(bf16[3,160,384]{2,1,0:T(8,128)(2,1)S(1)} %add_convert_fusion.4), channel_id=1, source_target_pairs={{0,4},{4,0},{8,12},{12,8},{16,20},{20,16},{24,28},{28,24},{1,5},{5... | collective-permute-start | bytes 1105928 | tf_op jit(solution)/shard_map/ppermute | solution.py:137
  269.9 7.7 %collective-permute-start.61 = (bf16[160,384]{1,0:T(8,128)(2,1)S(1)}, bf16[160,384]{1,0:T(8,128)(2,1)S(1)}, u32[]{:S(2)}, u32[]{:S(2)}) collective-permute-start(bf16[160,384]{1,0:T(8,128)(2,1)S(1)} %fusion.39), channel_id=1, source_target_pairs={{0,8},{8,0},{4,12},{12,4},{16,24},{24,16},{20,28},{28,20},{1,9},{9... | collective-permute-start | bytes 368648 | tf_op jit(solution)/shard_map/ppermute | solution.py:137
  270.2 7.6 %collective-permute-start.66 = (bf16[272,384]{1,0:T(8,128)(2,1)S(1)}, bf16[272,384]{1,0:T(8,128)(2,1)S(1)}, u32[]{:S(2)}, u32[]{:S(2)}) collective-permute-start(bf16[272,384]{1,0:T(8,128)(2,1)S(1)} %fusion.4), channel_id=1, source_target_pairs={{0,16},{16,0},{4,20},{20,4},{8,24},{24,8},{12,28},{28,12},{1,17},{... | collective-permute-start | bytes 626696 | tf_op jit(solution)/shard_map/ppermute | solution.py:137
  271.6 25.6 %collective-permute-start.64 = (bf16[2,192,384]{2,1,0:T(8,128)(2,1)S(1)}, bf16[2,192,384]{2,1,0:T(8,128)(2,1)S(1)}, u32[]{:S(2)}, u32[]{:S(2)}) collective-permute-start(bf16[2,192,384]{2,1,0:T(8,128)(2,1)S(1)} %pad_maximum_fusion.18), channel_id=1, source_target_pairs={{0,2},{2,0},{1,3},{3,1},{4,6},{6,4},{5,7},{7,5},{8,10},{10,8},{9,1... | collective-permute-start | bytes 884744 | tf_op jit(solution)/shard_map/ppermute | solution.py:137
  277.7 5.1 %collective-permute-start.62 = (bf16[160,384]{1,0:T(8,128)(2,1)S(1)}, bf16[160,384]{1,0:T(8,128)(2,1)S(1)}, u32[]{:S(2)}, u32[]{:S(2)}) collective-permute-start(bf16[160,384]{1,0:T(8,128)(2,1)S(1)} %fusion.24), channel_id=1, source_target_pairs={{0,16},{16,0},{4,20},{20,4},{8,24},{24,8},{12,28},{28,12},{1,17},{... | collective-permute-start | bytes 368648 | tf_op jit(solution)/shard_map/ppermute | solution.py:1316
  277.9 16.1 %collective-permute-start.68 = (bf16[2,272,384]{2,1,0:T(8,128)(2,1)S(1)}, bf16[2,272,384]{2,1,0:T(8,128)(2,1)S(1)}, u32[]{:S(2)}, u32[]{:S(2)}) collective-permute-start(bf16[2,272,384]{2,1,0:T(8,128)(2,1)S(1)} %pad_maximum_fusion.13), channel_id=1, source_target_pairs={{0,2},{2,0},{1,3},{3,1},{4,6},{6,4},{5,7},{7,5},{8,10},{10,8},{9,1... | collective-permute-start | bytes 1253384 | tf_op jit(solution)/shard_map/ppermute | solution.py:1316
  282.9 14.6 %collective-permute-start.63 = (bf16[2,160,384]{2,1,0:T(8,128)(2,1)S(1)}, bf16[2,160,384]{2,1,0:T(8,128)(2,1)S(1)}, u32[]{:S(2)}, u32[]{:S(2)}) collective-permute-start(bf16[2,160,384]{2,1,0:T(8,128)(2,1)S(1)} %pad_maximum_fusion.19), channel_id=1, source_target_pairs={{0,2},{2,0},{1,3},{3,1},{4,6},{6,4},{5,7},{7,5},{8,10},{10,8},{9,1... | collective-permute-start | bytes 737288 | tf_op jit(solution)/shard_map/ppermute | solution.py:1316
  283.8 17.7 %collective-permute-start.71 = (bf16[2,192,384]{2,1,0:T(8,128)(2,1)S(1)}, bf16[2,192,384]{2,1,0:T(8,128)(2,1)S(1)}, u32[]{:S(2)}, u32[]{:S(2)}) collective-permute-start(bf16[2,192,384]{2,1,0:T(8,128)(2,1)S(1)} %add_convert_fusion.5.mine), channel_id=1, source_target_pairs={{0,1},{1,0},{2,3},{3,2},{4,5},{5,4},{6,7},{7,6},{8,9},{9,8},{10,11... | collective-permute-start | bytes 884744 | tf_op jit(solution)/shard_map/ppermute | solution.py:496
  294.2 11.1 %collective-permute-start.69 = (bf16[2,272,384]{2,1,0:T(8,128)(2,1)S(1)}, bf16[2,272,384]{2,1,0:T(8,128)(2,1)S(1)}, u32[]{:S(2)}, u32[]{:S(2)}) collective-permute-start(bf16[2,272,384]{2,1,0:T(8,128)(2,1)S(1)} %add_convert_fusion.3.mine), channel_id=1, source_target_pairs={{0,1},{1,0},{2,3},{3,2},{4,5},{5,4},{6,7},{7,6},{8,9},{9,8},{10,11... | collective-permute-start | bytes 1253384 | tf_op jit(solution)/shard_map/ppermute | solution.py:496
  297.3 5.2 %collective-permute-start.65 = (bf16[2,192,384]{2,1,0:T(8,128)(2,1)S(1)}, bf16[2,192,384]{2,1,0:T(8,128)(2,1)S(1)}, u32[]{:S(2)}, u32[]{:S(2)}) collective-permute-start(bf16[2,192,384]{2,1,0:T(8,128)(2,1)S(1)} %add_convert_fusion.6.mine), channel_id=1, source_target_pairs={{0,1},{1,0},{2,3},{3,2},{4,5},{5,4},{6,7},{7,6},{8,9},{9,8},{10,11... | collective-permute-start | bytes 884744 | tf_op jit(solution)/shard_map/ppermute | solution.py:496
  297.5 6.2 %collective-permute-start.67 = (bf16[2,160,384]{2,1,0:T(8,128)(2,1)S(1)}, bf16[2,160,384]{2,1,0:T(8,128)(2,1)S(1)}, u32[]{:S(2)}, u32[]{:S(2)}) collective-permute-start(bf16[2,160,384]{2,1,0:T(8,128)(2,1)S(1)} %add_convert_fusion.7.mine), channel_id=1, source_target_pairs={{0,1},{1,0},{2,3},{3,2},{4,5},{5,4},{6,7},{7,6},{8,9},{9,8},{10,11... | collective-permute-start | bytes 737288 | tf_op jit(solution)/shard_map/ppermute | solution.py:496
  (72 other events, 600.8 us)

commit v2 on v1

--- a/solution.py
+++ b/solution.py
@@ -108,7 +108,7 @@
         for mover, parts in given.items():
             mover.give([parts[at] for at in range(len(parts))])
 
-    def step(self, moving=(), compute=(), eager=False):
+    def step(self, moving=(), compute=(), eager=False, last=False):
         arrays = [array for array, _ in self.came]
         twins = [base.exchange(self.tie) for base in self.bases]
         arrays, twins, self.before = lax.optimization_barrier(
@@ -137,17 +137,33 @@
             (lax.ppermute(array, axis, hops), sends)
             for array, ((axis, hops, _), sends) in zip(joined, ways.items())
         ]
+        early = []
+        if last:
+            early = [item for item in self.came if item[1][0][0].early]
+            self.came = [item for item in self.came if not item[1][0][0].early]
+            for array, sends in early:
+                sends[0][0].give([array])
         after = []
+
+        def compute_all():
+            for work in compute() if callable(compute) else compute:
+                after.extend(jax.tree.leaves(work(self.tie)))
+
+        if last:
+            compute_all()
         if eager:
-            movers = [mover for sends in ways.values() for mover, _, _ in sends]
-            self.take([array for array, _ in self.came])
+            movers = [mover for _, sends in self.came for mover, _, _ in sends]
+            arrays = [array for array, _ in self.came]
+            if last:
+                arrays, after = lax.optimization_barrier((arrays, after))
+            self.take(arrays)
             for mover in dict.fromkeys(movers):
                 if mover.done:
                     after += jax.tree.leaves(mover.result)
                 else:
                     after += [array for array, _, _ in mover.requests]
-        for work in compute() if callable(compute) else compute:
-            after += jax.tree.leaves(work(self.tie))
+        if not last:
+            compute_all()
         if after:
             self.before = after
 
@@ -156,10 +172,11 @@
 
 
 class Mover:
-    def __init__(self, steps, pieces=False):
+    def __init__(self, steps, pieces=False, early=False):
         self.given = []
         self.steps = steps
         self.pieces = pieces
+        self.early = early
         self.done = False
         self.result = None
         self.requests = next(steps)
@@ -181,7 +198,7 @@
 ANY = pl.BlockSpec(memory_space=pl.ANY)
 
 
-def call(kernel, out_shape, in_specs, scratch=(), mib=24, flops=0, out_specs=None, **more):
+def call(kernel, out_shape, in_specs, scratch=(), mib=20, flops=0, out_specs=None, **more):
     return pl.pallas_call(
         kernel,
         out_shape=out_shape,
@@ -579,7 +596,7 @@
             (came,) = yield [(sent, STREAM, CORE)]
             self.came.append(came)
 
-        return Mover(steps(self.sent[-1]))
+        return Mover(steps(self.sent[-1]), early=True)
 
     def own(self, tie, small=()):
         deepest = max(job[-1] for job in self.jobs)
@@ -875,22 +892,26 @@
         copy.wait()
     keep = pltpu.make_async_copy(w, w_out, out_sem.at[0])
     keep.start()
-    for block in range(2 * in_units):
-        columns = slice(block * LANES, (block + 1) * LANES)
-        pre = dot(h2[...], hidden_weights(w, block, in_units)) + bias[block : block + 1]
+    for block in range(0, 2 * in_units, 2):
+        columns = slice(block * LANES, (block + 2) * LANES)
+        two = (block, block + 1)
+        weights = jnp.concatenate([hidden_weights(w, b, in_units) for b in two], axis=1)
+        shift = jnp.concatenate([bias[b : b + 1] for b in two], axis=1)
+        pre = dot(h2[...], weights) + shift
         cumulative = 0.5 * (1.0 + lax.erf(pre * ROOT_HALF))
         active[:, columns] = low(pre * cumulative)
         slope[:, columns] = low(cumulative + pre * INV_ROOT_TAU * jnp.exp(-0.5 * pre * pre))
     half_rows = w.shape[3] // 2
-    for c in range(2):
-        columns = slice(c * LANES, (c + 1) * LANES)
-        made = None
-        for part in range(4):
-            weights = w[2 * part : 2 * part + 2, :, c, half_rows:].reshape(-1, LANES)
-            depth = weights.shape[0]
-            term = dot(active[:, part * depth : (part + 1) * depth], weights)
-            made = term if made is None else made + term
-        total[:, columns] = made
+    made = None
+    for part in range(4):
+        weights = jnp.concatenate(
+            [w[2 * part : 2 * part + 2, :, c, half_rows:].reshape(-1, LANES) for c in range(2)],
+            axis=1,
+        )
+        depth = weights.shape[0]
+        term = dot(active[:, part * depth : (part + 1) * depth], weights)
+        made = term if made is None else made + term
+    total[...] = made
 
     def step(r, sums):
         rows = pl.ds(pl.multiple_of(r * seq, 8), seq)
@@ -1416,6 +1437,7 @@
             [move_out, move_in, mid_group.core_move()],
             [run_self_back, run_patch_grad, mid_group.own, begin_last],
             eager=True,
+            last=True,
         )
         move_mid, move_patch = mid_group.move(), Mover(patch_steps())
         clock.step(

time: 312 us -> 310 us (level)
    ppermute x4, starting transfers between devices: 15.8 us -> 12.3 us  [reduce_steps(): return (total, lax.ppermute(total, STREAM, CORE))]
  transfers between devices with their start and end apart: 72 -> 72, of which waited for: 27 -> 27; matrix products, arithmetic and copies ran while one was open for 2% -> 2% of each run, Pallas kernels for 24% -> 26%
where the time goes in v2:
time: 310 us; the launch traced here: 305 us
  waiting for transfers between devices  107 us (35%)
  Pallas kernels  98.9 us (32%)
  starting transfers between devices  72.1 us (23%)
  local copies, waits for them, and re-layouts  18.4 us (6%)
  other arithmetic  6.3 us (2%)
    ppermute x47, waiting for transfers between devices, step(): lax.ppermute(array, axis, hops)  95.7 us
    ppermute x47, starting transfers between devices, step(): lax.ppermute(array, axis, hops)  44.6 us
    pallas_call x1, Pallas kernels, run_patch(): call(functools.partial(patch_kernel, units, len(sources), spec, seq, patc...  15.7 us
    pallas_call x1, Pallas kernels, run_text(): call(functools.partial(text_kernel, units, len(sources), spec, seq), outs...  13.5 us
    ppermute x4, starting transfers between devices, reduce_steps(): return (total, lax.ppermute(total, STREAM, CORE))  12.3 us
    unnamed x130, local copies, waits for them, and re-layouts  11.9 us
    ppermute x18, starting transfers between devices, exchange(): self.twin = lax.ppermute(tie(self.array), STREAM, CORE)  11 us
    pallas_call x1, Pallas kernels, run_ffn(): call(functools.partial(ffn_kernel, len(sources), spec, in_units, seq), [s...  10.5 us
  transfers between devices with their start and end apart: 72, of which 27 were waited for; matrix products, arithmetic and copies ran while one was open for 2% of the time, Pallas kernels for 26%

profile of v2, /device:TPU:1, one launch (start us, length us, event | category | flops | bytes accessed | tf_op | source)
XLA Modules:
  0.0 304.8 jit_solution(8254305574446015101)
XLA Ops:
  1.5 1.3 copy.31
  4.8 2.0 collective-permute-start.4
  6.9 1.3 collective-permute-start
  8.1 1.2 collective-permute-start.3
  9.4 2.3 collective-permute-start.1
  11.8 8.1 %collective-permute-done.1.refs_3_ = bf16[256,384]{1,0:T(8,128)(2,1)S(1)} collective-permute-done((bf16[256,384]{1,0:T(8,128)(2,1)S(1)}, bf16[256,384]{1,0:T(8,128)(2,1)S(1)}, u32[]{:S(2)}, u32[]{:S(2)}) %collective-permute-start.1) | collective-permute-done | bytes 196640 | tf_op jit(solution)/shard_map/ppermute | solution.py:137
  19.9 7.1 %collective-permute-done.2.refs_4_ = bf16[256,384]{1,0:T(8,128)(2,1)S(1)} collective-permute-done((bf16[256,384]{1,0:T(8,128)(2,1)S(1)}, bf16[256,384]{1,0:T(8,128)(2,1)S(1)}, u32[]{:S(2)}, u32[]{:S(2)}) %collective-permute-start.2) | collective-permute-done | bytes 196640 | tf_op jit(solution)/shard_map/ppermute | solution.py:137
  28.2 1.3 collective-permute-start.5
  29.7 1.3 collective-permute-start.8
  31.1 2.2 collective-permute-start.9
  33.5 1.8 collective-permute-done.8.refs_3_
  35.3 5.5 %collective-permute-done.9.refs_4_ = bf16[176,384]{1,0:T(8,128)(2,1)S(1)} collective-permute-done((bf16[176,384]{1,0:T(8,128)(2,1)S(1)}, bf16[176,384]{1,0:T(8,128)(2,1)S(1)}, u32[]{:S(2)}, u32[]{:S(2)}) %collective-permute-start.9) | collective-permute-done | bytes 135200 | tf_op jit(solution)/shard_map/ppermute | solution.py:137
  41.0 5.9 %collective-permute-done.5.refs_6_.refs_2_ = bf16[1120,384]{1,0:T(8,128)(2,1)S(1)} collective-permute-done((bf16[1120,384]{1,0:T(8,128)(2,1)S(1)}, bf16[1120,384]{1,0:T(8,128)(2,1)S(1)}, u32[]{:S(2)}, u32[]{:S(2)}) %collective-permute-start.5) | collective-permute-done | bytes 860192 | tf_op jit(solution)/shard_map/ppermute | solution.py:137
  46.9 1.3 constant_dynamic-slice_fusion.1
  48.6 1.3 collective-permute-start.13
  51.4 2.3 collective-permute-start.12
  53.7 12.3 %collective-permute-done.11.refs_3_ = bf16[384,384]{1,0:T(8,128)(2,1)S(1)} collective-permute-done((bf16[384,384]{1,0:T(8,128)(2,1)S(1)}, bf16[384,384]{1,0:T(8,128)(2,1)S(1)}, u32[]{:S(2)}, u32[]{:S(2)}) %collective-permute-start.11) | collective-permute-done | bytes 294944 | tf_op jit(solution)/shard_map/ppermute | solution.py:137
  65.9 7.9 %collective-permute-done.12.refs_4_ = bf16[384,384]{1,0:T(8,128)(2,1)S(1)} collective-permute-done((bf16[384,384]{1,0:T(8,128)(2,1)S(1)}, bf16[384,384]{1,0:T(8,128)(2,1)S(1)}, u32[]{:S(2)}, u32[]{:S(2)}) %collective-permute-start.12) | collective-permute-done | bytes 294944 | tf_op jit(solution)/shard_map/ppermute | solution.py:137
  77.1 5.0 %collective-permute-start.15 = (bf16[512,384]{1,0:T(8,128)(2,1)S(1)}, bf16[512,384]{1,0:T(8,128)(2,1)S(1)}, u32[]{:S(2)}, u32[]{:S(2)}) collective-permute-start(bf16[512,384]{1,0:T(8,128)(2,1)S(1)} %bitcast.207), channel_id=1, source_target_pairs={{0,1},{1,0},{2,3},{3,2},{4,5},{5,4},{6,7},{7,6},{8,9},{9,8},{10,11... | collective-permute-start | bytes 1179656 | tf_op jit(solution)/shard_map/ppermute | solution.py:71
  85.3 2.2 collective-permute-done.16.refs_10_
  87.6 1.3 collective-permute-start.23
  93.4 13.5 %shard_map.250 = (f32[16,768]{1,0:T(8,128)}, f32[8,384]{1,0:T(8,128)}, bf16[320,768]{1,0:T(8,128)(2,1)}, f32[320,768]{1,0:T(8,128)}, f32[320,1]{1,0:T(8,128)}, /...) custom-call(s32[8]{0:T(128)} %reshape.233.lengths, ...), custom_call_target="tpu_custom_call" | custom-call | flops 3019898880 | bytes 4194304 | tf_op jit(solution)/shard_map/pallas_call | solution.py:1169
  107.0 2.7 collective-permute-done.24.refs_8_.refs_5_
  109.6 1.9 collective-permute-done.23.refs_7_.refs_6_
  115.3 2.4 collective-permute-done.28.refs_11_
  118.4 1.3 collective-permute-start.33
  121.5 15.7 %shard_map.251 = (bf16[320,768]{1,0:T(8,128)(2,1)}, f32[320,768]{1,0:T(8,128)}, f32[320,1]{1,0:T(8,128)}, bf16[320,768]{1,0:T(8,128)(2,1)}, bf16[4,2,2,160,768]{...) custom-call(s32[8]{0:T(128)} %xor.10.slots, ...), custom_call_target="tpu_custom_call" | custom-call | flops 6794772480 | bytes 4194304 | tf_op jit(solution)/shard_map/pallas_call | solution.py:1192
  137.9 2.1 collective-permute-done.37.refs_15_
  143.5 1.3 copy-done.14
  146.0 10.5 %shard_map.252 = (bf16[8,40,768]{2,1,0:T(8,128)(2,1)}, f32[320,768]{1,0:T(8,128)S(1)}, bf16[320,768]{1,0:T(8,128)(2,1)S(1)}, f32[8,768]{1,0:T(8,128)S(1)}, bf16[...) custom-call(s32[8]{0:T(128)S(1)} %copy-done.33, ...), custom_call_target="tpu_custom_call" | custom-call | flops 3019898880 | bytes 4194304 | tf_op jit(solution)/shard_map/pallas_call | solution.py:1211
  156.5 1.7 shard_map.253
  158.6 10.3 %shard_map.254 = (bf16[320,3072]{1,0:T(8,128)(2,1)S(1)}, f32[8,384]{1,0:T(8,128)S(1)}, f32[320,768]{1,0:T(8,128)S(1)}, bf16[320,768]{1,0:T(8,128)(2,1)S(1)}, f32[8,768]{1,0:T(8,128)S(1)}) custom-call(bf16[320,768]{1,0:T(8,128)(2,1)S(1)} %get-tuple-element.397.refs_1_.df, bf16[8,2,2,384,384]{4,3,2,1,0:T(8,128)(2,1)S(1)} %get-tuple-element.398.wout.win, ...), custom_call_target="tpu_custom_call" | custom-call | flops 3019898880 | bytes 4194304 | tf_op jit(solution)/shard_map/pallas_call | solution.py:1232
  168.9 1.4 shard_map.256
  170.4 2.0 shard_map.255
  174.6 8.3 %shard_map.257 = (bf16[320,768]{1,0:T(8,128)(2,1)S(1)}, bf16[2,4,2,160,768]{4,3,2,1,0:T(8,128)(2,1)S(1)}) custom-call(s32[8]{0:T(128)S(1)} %copy-done.34, bf16[320,768]{1,0:T(8,128)(2,1)S(1)} %get-tuple-element.410.dac.refs_1_, bf16[320,768]{1,0:T(8,128)(2,1)S(1)} %copy-done.23, bf16[4,2,2,160,768]{4,3,2,1,0:T(8,128)(2,1)S(1)} %copy-done.2, ...), custom_call_target="tpu_custom_call" | custom-call | flops 1509949440 | bytes 4194304 | tf_op jit(solution)/shard_map/pallas_call | solution.py:1262
  183.0 2.4 shard_map.258
  185.5 3.3 %shard_map.260 = bf16[8,2,272,384]{3,2,1,0:T(8,128)(2,1)S(1)} custom-call(bf16[320,768]{1,0:T(8,128)(2,1)S(1)} %copy-done.10, bf16[320,768]{1,0:T(8,128)(2,1)S(1)} %get-tuple-element.410.dac.refs_1_, bf16[320,768]{1,0:T(8,128)(2,1)S(1)} %copy-done.9, bf16[320,768]{1,0:T(8,128)(2,1)S(1)} %get-tuple-element.458.dqc.refs_3_, bf16[320,768]{1,0:T(8,128)(2,1)S(1)} %copy-done.8, ...), custom_call_target="tpu_custom_call" | custom-call | flops 2579496960 | bytes 4194304 | tf_op jit(solution)/shard_map/pallas_call | solution.py:581
  189.1 2.0 shard_map.259
  193.7 1.3 collective-permute-start.44
  195.0 5.6 %shard_map.262 = (bf16[2,2,160,1024]{3,2,1,0:T(8,128)(2,1)S(1)}, bf16[2,2,160,1024]{3,2,1,0:T(8,128)(2,1)S(1)}, f32[8,768]{1,0:T(8,128)S(1)}) custom-call(bf16[2,4,2,160,768]{4,3,2,1,0:T(8,128)(2,1)S(1)} %get-tuple-element.472.dkv, bf16[2,2,1024,384]{3,2,1,0:T(8,128)(2,1)S(1)} %copy-done.39), custom_call_target="tpu_custom_call" | custom-call | flops 6039797760 | bytes 4194304 | tf_op jit(solution)/shard_map/pallas_call | solution.py:1298
  200.6 7.2 %shard_map.261 = (bf16[3,320,768]{2,1,0:T(8,128)(2,1)S(1)}, f32[8,768]{1,0:T(8,128)S(1)}) custom-call(s32[8]{0:T(128)S(1)} %copy-done.33, bf16[320,768]{1,0:T(8,128)(2,1)S(1)} %get-tuple-element.468.refs_5_.da, bf16[3,320,768]{2,1,0:T(8,128)(2,1)S(1)} %copy-done.37, bf16[2,1,768,384]{3,2,1,0:T(8,128)(2,1)S(1)} %copy-done.38), custom_call_target="tpu_custom_call" | custom-call | flops 1509949440 | bytes 4194304 | tf_op jit(solution)/shard_map/pallas_call | solution.py:1288
  209.0 3.9 %shard_map.263 = (bf16[4,272,384]{2,1,0:T(8,128)(2,1)S(1)}, bf16[2,272,384]{2,1,0:T(8,128)(2,1)S(1)}, bf16[2,272,384]{2,1,0:T(8,128)(2,1)S(1)}, bf16[3,272,384]{...) custom-call(bf16[320,768]{1,0:T(8,128)(2,1)S(1)} %copy-done.10, ...), custom_call_target="tpu_custom_call" | custom-call | flops 2579496960 | bytes 4194304 | tf_op jit(solution)/shard_map/pallas_call | solution.py:608
  215.5 1.7 collective-permute-start.48
  217.2 2.5 shard_map.265
  219.7 10.6 %collective-permute-done.49 = bf16[928,384]{1,0:T(8,128)(2,1)S(1)} collective-permute-done((bf16[928,384]{1,0:T(8,128)(2,1)S(1)}, bf16[928,384]{1,0:T(8,128)(2,1)S(1)}, u32[]{:S(2)}, u32[]{:S(2)}) %collective-permute-start.49) | collective-permute-done | bytes 712736 | tf_op jit(solution)/shard_map/ppermute | solution.py:137
  230.4 2.6 collective-permute-done.52
  234.9 1.5 shard_map.266
  236.6 1.6 collective-permute-start.55
  241.0 3.1 %collective-permute-done.55 = bf16[192,384]{1,0:T(8,128)(2,1)S(1)} collective-permute-done((bf16[192,384]{1,0:T(8,128)(2,1)S(1)}, bf16[192,384]{1,0:T(8,128)(2,1)S(1)}, u32[]{:S(2)}, u32[]{:S(2)}) %collective-permute-start.55) | collective-permute-done | bytes 147488 | tf_op jit(solution)/shard_map/ppermute | solution.py:137
  244.2 4.3 %collective-permute-done.57 = bf16[4,160,384]{2,1,0:T(8,128)(2,1)S(1)} collective-permute-done((bf16[4,160,384]{2,1,0:T(8,128)(2,1)S(1)}, bf16[4,160,384]{2,1,0:T(8,128)(2,1)S(1)}, u32[]{:S(2)}, u32[]{:S(2)}) %collective-permute-start.57) | collective-permute-done | bytes 491552 | tf_op jit(solution)/shard_map/ppermute | solution.py:137
  248.6 6.5 %collective-permute-done.56 = bf16[784,384]{1,0:T(8,128)(2,1)S(1)} collective-permute-done((bf16[784,384]{1,0:T(8,128)(2,1)S(1)}, bf16[784,384]{1,0:T(8,128)(2,1)S(1)}, u32[]{:S(2)}, u32[]{:S(2)}) %collective-permute-start.56) | collective-permute-done | bytes 602144 | tf_op jit(solution)/shard_map/ppermute | solution.py:137
  255.2 3.1 %collective-permute-done.54 = bf16[1136,384]{1,0:T(8,128)(2,1)S(1)} collective-permute-done((bf16[1136,384]{1,0:T(8,128)(2,1)S(1)}, bf16[1136,384]{1,0:T(8,128)(2,1)S(1)}, u32[]{:S(2)}, u32[]{:S(2)}) %collective-permute-start.54) | collective-permute-done | bytes 872480 | tf_op jit(solution)/shard_map/ppermute | solution.py:137
  261.4 3.9 %collective-permute-done.60 = bf16[192,384]{1,0:T(8,128)(2,1)S(1)} collective-permute-done((bf16[192,384]{1,0:T(8,128)(2,1)S(1)}, bf16[192,384]{1,0:T(8,128)(2,1)S(1)}, u32[]{:S(2)}, u32[]{:S(2)}) %collective-permute-start.60) | collective-permute-done | bytes 147488 | tf_op jit(solution)/shard_map/ppermute | solution.py:137
  265.5 2.9 collective-permute-done.58
  268.6 3.4 %collective-permute-start.66 = (bf16[272,384]{1,0:T(8,128)(2,1)S(1)}, bf16[272,384]{1,0:T(8,128)(2,1)S(1)}, u32[]{:S(2)}, u32[]{:S(2)}) collective-permute-start(bf16[272,384]{1,0:T(8,128)(2,1)S(1)} %fusion.4), channel_id=1, source_target_pairs={{0,16},{16,0},{4,20},{20,4},{8,24},{24,8},{12,28},{28,12},{1,17},{... | collective-permute-start | bytes 626696 | tf_op jit(solution)/shard_map/ppermute | solution.py:137
  272.8 2.5 collective-permute-done.61
  275.4 2.1 collective-permute-done.66
  278.5 3.3 %collective-permute-done.62 = bf16[160,384]{1,0:T(8,128)(2,1)S(1)} collective-permute-done((bf16[160,384]{1,0:T(8,128)(2,1)S(1)}, bf16[160,384]{1,0:T(8,128)(2,1)S(1)}, u32[]{:S(2)}, u32[]{:S(2)}) %collective-permute-start.62) | collective-permute-done | bytes 122912 | tf_op jit(solution)/shard_map/ppermute | solution.py:1337
  281.9 3.3 %collective-permute-start.63 = (bf16[2,160,384]{2,1,0:T(8,128)(2,1)S(1)}, bf16[2,160,384]{2,1,0:T(8,128)(2,1)S(1)}, u32[]{:S(2)}, u32[]{:S(2)}) collective-permute-start(bf16[2,160,384]{2,1,0:T(8,128)(2,1)S(1)} %pad_maximum_fusion.19), channel_id=1, source_target_pairs={{0,2},{2,0},{1,3},{3,1},{4,6},{6,4},{5,7},{7,5},{8,10},{10,8},{9,1... | collective-permute-start | bytes 737288 | tf_op jit(solution)/shard_map/ppermute | solution.py:1337
  285.3 5.1 %collective-permute-start.71 = (bf16[2,192,384]{2,1,0:T(8,128)(2,1)S(1)}, bf16[2,192,384]{2,1,0:T(8,128)(2,1)S(1)}, u32[]{:S(2)}, u32[]{:S(2)}) collective-permute-start(bf16[2,192,384]{2,1,0:T(8,128)(2,1)S(1)} %add_convert_fusion.5.mine), channel_id=1, source_target_pairs={{0,1},{1,0},{2,3},{3,2},{4,5},{5,4},{6,7},{7,6},{8,9},{9,8},{10,11... | collective-permute-start | bytes 884744 | tf_op jit(solution)/shard_map/ppermute | solution.py:513
  290.5 4.8 %collective-permute-start.69 = (bf16[2,272,384]{2,1,0:T(8,128)(2,1)S(1)}, bf16[2,272,384]{2,1,0:T(8,128)(2,1)S(1)}, u32[]{:S(2)}, u32[]{:S(2)}) collective-permute-start(bf16[2,272,384]{2,1,0:T(8,128)(2,1)S(1)} %add_convert_fusion.3.mine), channel_id=1, source_target_pairs={{0,1},{1,0},{2,3},{3,2},{4,5},{5,4},{6,7},{7,6},{8,9},{9,8},{10,11... | collective-permute-start | bytes 1253384 | tf_op jit(solution)/shard_map/ppermute | solution.py:513
  295.5 2.3 collective-permute-start.67
  298.0 1.4 copy.29
  303.4 1.3 shard_map.269
  (314 shorter events, 53.1 us)
Async XLA Ops:
  4.8 23.0 %collective-permute-start.4 = (bf16[2,160,1024]{2,1,0:T(8,128)(2,1)}, bf16[2,160,1024]{2,1,0:T(8,128)(2,1)}, u32[]{:S(2)}, u32[]{:S(2)}) collective-permute-start(bf16[2,160,1024]{2,1,0:T(8,128)(2,1)} %shard_map.248.refs_17_), channel_id=1, source_target_pairs={{0,2},{2,0},{1,3},{3,1},{4,6},{6,4},{5,7},{7,5},{8,10},{10,8},{9,1... | collective-permute-start | bytes 1966088 | tf_op jit(solution)/shard_map/ppermute | solution.py:137
  6.9 20.2 %collective-permute-start = (bf16[2,256,384]{2,1,0:T(8,128)(2,1)S(1)}, bf16[2,256,384]{2,1,0:T(8,128)(2,1)S(1)}, u32[]{:S(2)}, u32[]{:S(2)}) collective-permute-start(bf16[2,256,384]{2,1,0:T(8,128)(2,1)S(1)} %get-tuple-element.298), channel_id=1, source_target_pairs={{0,8},{8,0},{4,12},{12,4},{16,24},{24,16},{20,28},{28,20},{1,9},{9... | collective-permute-start | bytes 1179656 | tf_op jit(solution)/shard_map/ppermute | solution.py:137
  8.1 18.9 %collective-permute-start.3 = (bf16[2,256,384]{2,1,0:T(8,128)(2,1)S(1)}, bf16[2,256,384]{2,1,0:T(8,128)(2,1)S(1)}, u32[]{:S(2)}, u32[]{:S(2)}) collective-permute-start(bf16[2,256,384]{2,1,0:T(8,128)(2,1)S(1)} %get-tuple-element.298), channel_id=1, source_target_pairs={{0,4},{4,0},{8,12},{12,8},{16,20},{20,16},{24,28},{28,24},{1,5},{5... | collective-permute-start | bytes 1179656 | tf_op jit(solution)/shard_map/ppermute | solution.py:137
  9.4 10.5 %collective-permute-start.1 = (bf16[256,384]{1,0:T(8,128)(2,1)S(1)}, bf16[256,384]{1,0:T(8,128)(2,1)S(1)}, u32[]{:S(2)}, u32[]{:S(2)}) collective-permute-start(bf16[256,384]{1,0:T(8,128)(2,1)S(1)} %get-tuple-element.297), channel_id=1, source_target_pairs={{0,16},{16,0},{4,20},{20,4},{8,24},{24,8},{12,28},{28,12},{1,17},{... | collective-permute-start | bytes 589832 | tf_op jit(solution)/shard_map/ppermute | solution.py:137
  11.7 15.3 %collective-permute-start.2 = (bf16[256,384]{1,0:T(8,128)(2,1)S(1)}, bf16[256,384]{1,0:T(8,128)(2,1)S(1)}, u32[]{:S(2)}, u32[]{:S(2)}) collective-permute-start(bf16[256,384]{1,0:T(8,128)(2,1)S(1)} %get-tuple-element.297), channel_id=1, source_target_pairs={{0,24},{24,0},{4,28},{28,4},{8,16},{16,8},{12,20},{20,12},{1,25},{... | collective-permute-start | bytes 589832 | tf_op jit(solution)/shard_map/ppermute | solution.py:137
  28.2 18.8 %collective-permute-start.5 = (bf16[1120,384]{1,0:T(8,128)(2,1)S(1)}, bf16[1120,384]{1,0:T(8,128)(2,1)S(1)}, u32[]{:S(2)}, u32[]{:S(2)}) collective-permute-start(bf16[1120,384]{1,0:T(8,128)(2,1)S(1)} %pad_maximum_fusion.4), channel_id=1, source_target_pairs={{0,4},{4,0},{8,12},{12,8},{16,20},{20,16},{24,28},{28,24},{1,5},{5... | collective-permute-start | bytes 2580488 | tf_op jit(solution)/shard_map/ppermute | solution.py:137
  29.5 11.5 %collective-permute-start.6 = (bf16[512,384]{1,0:T(8,128)(2,1)S(1)}, bf16[512,384]{1,0:T(8,128)(2,1)S(1)}, u32[]{:S(2)}, u32[]{:S(2)}) collective-permute-start(bf16[512,384]{1,0:T(8,128)(2,1)S(1)} %pad_maximum_fusion.15), channel_id=1, source_target_pairs={{0,2},{2,0},{1,3},{3,1},{4,6},{6,4},{5,7},{7,5},{8,10},{10,8},{9,1... | collective-permute-start | bytes 1179656 | tf_op jit(solution)/shard_map/ppermute | solution.py:137
  29.7 11.3 %collective-permute-start.7 = (bf16[2,176,384]{2,1,0:T(8,128)(2,1)S(1)}, bf16[2,176,384]{2,1,0:T(8,128)(2,1)}, u32[]{:S(2)}, u32[]{:S(2)}) collective-permute-start(bf16[2,176,384]{2,1,0:T(8,128)(2,1)S(1)} %get-tuple-element.308), channel_id=1, source_target_pairs={{0,8},{8,0},{4,12},{12,4},{16,24},{24,16},{20,28},{28,20},{1,9},{9... | collective-permute-start | bytes 811016 | tf_op jit(solution)/shard_map/ppermute | solution.py:137
  29.7 5.6 %collective-permute-start.8 = (bf16[176,384]{1,0:T(8,128)(2,1)S(1)}, bf16[176,384]{1,0:T(8,128)(2,1)S(1)}, u32[]{:S(2)}, u32[]{:S(2)}) collective-permute-start(bf16[176,384]{1,0:T(8,128)(2,1)S(1)} %get-tuple-element.310), channel_id=1, source_target_pairs={{0,16},{16,0},{4,20},{20,4},{8,24},{24,8},{12,28},{28,12},{1,17},{... | collective-permute-start | bytes 405512 | tf_op jit(solution)/shard_map/ppermute | solution.py:137
  31.1 9.7 %collective-permute-start.9 = (bf16[176,384]{1,0:T(8,128)(2,1)S(1)}, bf16[176,384]{1,0:T(8,128)(2,1)S(1)}, u32[]{:S(2)}, u32[]{:S(2)}) collective-permute-start(bf16[176,384]{1,0:T(8,128)(2,1)S(1)} %get-tuple-element.310), channel_id=1, source_target_pairs={{0,24},{24,0},{4,28},{28,4},{8,16},{16,8},{12,20},{20,12},{1,25},{... | collective-permute-start | bytes 405512 | tf_op jit(solution)/shard_map/ppermute | solution.py:137
  48.6 25.3 %collective-permute-start.13 = (bf16[1552,384]{1,0:T(8,128)(2,1)S(1)}, bf16[1552,384]{1,0:T(8,128)(2,1)S(1)}, u32[]{:S(2)}, u32[]{:S(2)}) collective-permute-start(bf16[1552,384]{1,0:T(8,128)(2,1)S(1)} %pad_maximum_fusion), channel_id=1, source_target_pairs={{0,4},{4,0},{8,12},{12,8},{16,20},{20,16},{24,28},{28,24},{1,5},{5... | collective-permute-start | bytes 3575816 | tf_op jit(solution)/shard_map/ppermute | solution.py:137
  49.9 24.0 %collective-permute-start.14 = (bf16[864,384]{1,0:T(8,128)(2,1)S(1)}, bf16[864,384]{1,0:T(8,128)(2,1)S(1)}, u32[]{:S(2)}, u32[]{:S(2)}) collective-permute-start(bf16[864,384]{1,0:T(8,128)(2,1)S(1)} %pad_maximum_fusion.9), channel_id=1, source_target_pairs={{0,2},{2,0},{1,3},{3,1},{4,6},{6,4},{5,7},{7,5},{8,10},{10,8},{9,1... | collective-permute-start | bytes 1990664 | tf_op jit(solution)/shard_map/ppermute | solution.py:137
  50.1 23.7 %collective-permute-start.10 = (bf16[2,384,384]{2,1,0:T(8,128)(2,1)S(1)}, bf16[2,384,384]{2,1,0:T(8,128)(2,1)S(1)}, u32[]{:S(2)}, u32[]{:S(2)}) collective-permute-start(bf16[2,384,384]{2,1,0:T(8,128)(2,1)S(1)} %get-tuple-element.318), channel_id=1, source_target_pairs={{0,8},{8,0},{4,12},{12,4},{16,24},{24,16},{20,28},{28,20},{1,9},{9... | collective-permute-start | bytes 1769480 | tf_op jit(solution)/shard_map/ppermute | solution.py:137
  50.1 15.8 %collective-permute-start.11 = (bf16[384,384]{1,0:T(8,128)(2,1)S(1)}, bf16[384,384]{1,0:T(8,128)(2,1)S(1)}, u32[]{:S(2)}, u32[]{:S(2)}) collective-permute-start(bf16[384,384]{1,0:T(8,128)(2,1)S(1)} %get-tuple-element.320), channel_id=1, source_target_pairs={{0,16},{16,0},{4,20},{20,4},{8,24},{24,8},{12,28},{28,12},{1,17},{... | collective-permute-start | bytes 884744 | tf_op jit(solution)/shard_map/ppermute | solution.py:137
  51.4 22.5 %collective-permute-start.12 = (bf16[384,384]{1,0:T(8,128)(2,1)S(1)}, bf16[384,384]{1,0:T(8,128)(2,1)S(1)}, u32[]{:S(2)}, u32[]{:S(2)}) collective-permute-start(bf16[384,384]{1,0:T(8,128)(2,1)S(1)} %get-tuple-element.320), channel_id=1, source_target_pairs={{0,24},{24,0},{4,28},{28,4},{8,16},{16,8},{12,20},{20,12},{1,25},{... | collective-permute-start | bytes 884744 | tf_op jit(solution)/shard_map/ppermute | solution.py:137
  77.1 7.5 %collective-permute-start.15 = (bf16[512,384]{1,0:T(8,128)(2,1)S(1)}, bf16[512,384]{1,0:T(8,128)(2,1)S(1)}, u32[]{:S(2)}, u32[]{:S(2)}) collective-permute-start(bf16[512,384]{1,0:T(8,128)(2,1)S(1)} %bitcast.207), channel_id=1, source_target_pairs={{0,1},{1,0},{2,3},{3,2},{4,5},{5,4},{6,7},{7,6},{8,9},{9,8},{10,11... | collective-permute-start | bytes 1179656 | tf_op jit(solution)/shard_map/ppermute | solution.py:71
  82.7 8.3 %collective-permute-start.20 = (bf16[1120,384]{1,0:T(8,128)(2,1)S(1)}, bf16[1120,384]{1,0:T(8,128)(2,1)S(1)}, u32[]{:S(2)}, u32[]{:S(2)}) collective-permute-start(bf16[1120,384]{1,0:T(8,128)(2,1)S(1)} %collective-permute-done.5.refs_6_.refs_2_), channel_id=1, source_target_pairs={{0,1},{1,0},{2,3},{3,2},{4,5},{5,4},{6,7},{7,6},{8,9},{9,8},{10,11... | collective-permute-start | bytes 2580488 | tf_op jit(solution)/shard_map/ppermute | solution.py:71
  82.7 10.7 %collective-permute-start.21 = (bf16[1552,384]{1,0:T(8,128)(2,1)S(1)}, bf16[1552,384]{1,0:T(8,128)(2,1)}, u32[]{:S(2)}, u32[]{:S(2)}) collective-permute-start(bf16[1552,384]{1,0:T(8,128)(2,1)S(1)} %collective-permute-done.13.refs_7_.refs_6_.refs_2_), channel_id=1, source_target_pairs={{0,1},{1,0},{2,3},{3,2},{4,5},{5,4},{6,7},{7,6},{8,9},{9,8},{10,11... | collective-permute-start | bytes 3575816 | tf_op jit(solution)/shard_map/ppermute | solution.py:71
  84.4 5.8 %collective-permute-start.22 = (bf16[864,384]{1,0:T(8,128)(2,1)S(1)}, bf16[864,384]{1,0:T(8,128)(2,1)S(1)}, u32[]{:S(2)}, u32[]{:S(2)}) collective-permute-start(bf16[864,384]{1,0:T(8,128)(2,1)S(1)} %collective-permute-done.14.refs_8_.refs_5_), channel_id=1, source_target_pairs={{0,1},{1,0},{2,3},{3,2},{4,5},{5,4},{6,7},{7,6},{8,9},{9,8},{10,11... | collective-permute-start | bytes 1990664 | tf_op jit(solution)/shard_map/ppermute | solution.py:71
  87.6 24.0 %collective-permute-start.23 = (bf16[1328,384]{1,0:T(8,128)(2,1)}, bf16[1328,384]{1,0:T(8,128)(2,1)S(1)}, u32[]{:S(2)}, u32[]{:S(2)}) collective-permute-start(bf16[1328,384]{1,0:T(8,128)(2,1)} %pad_maximum_fusion.1), channel_id=1, source_target_pairs={{0,4},{4,0},{8,12},{12,8},{16,20},{20,16},{24,28},{28,24},{1,5},{5... | collective-permute-start | bytes 3059720 | tf_op jit(solution)/shard_map/ppermute | solution.py:137
  89.1 20.6 %collective-permute-start.24 = (bf16[1120,384]{1,0:T(8,128)(2,1)}, bf16[1120,384]{1,0:T(8,128)(2,1)}, u32[]{:S(2)}, u32[]{:S(2)}) collective-permute-start(bf16[1120,384]{1,0:T(8,128)(2,1)} %pad_maximum_fusion.5), channel_id=1, source_target_pairs={{0,2},{2,0},{1,3},{3,1},{4,6},{6,4},{5,7},{7,5},{8,10},{10,8},{9,1... | collective-permute-start | bytes 2580488 | tf_op jit(solution)/shard_map/ppermute | solution.py:137
  90.3 16.7 %collective-permute-start.25 = (bf16[2,160,1024]{2,1,0:T(8,128)(2,1)}, bf16[2,160,1024]{2,1,0:T(8,128)(2,1)}, u32[]{:S(2)}, u32[]{:S(2)}) collective-permute-start(bf16[2,160,1024]{2,1,0:T(8,128)(2,1)} %shard_map.248.refs_17_), channel_id=1, source_target_pairs={{0,1},{1,0},{2,3},{3,2},{4,5},{5,4},{6,7},{7,6},{8,9},{9,8},{10,11... | collective-permute-start | bytes 1966088 | tf_op jit(solution)/shard_map/ppermute | solution.py:137
  92.1 14.9 %collective-permute-start.26 = (bf16[2,160,1024]{2,1,0:T(8,128)(2,1)}, bf16[2,160,1024]{2,1,0:T(8,128)(2,1)}, u32[]{:S(2)}, u32[]{:S(2)}) collective-permute-start(bf16[2,160,1024]{2,1,0:T(8,128)(2,1)} %collective-permute-done.4.refs_19_), channel_id=1, source_target_pairs={{0,1},{1,0},{2,3},{3,2},{4,5},{5,4},{6,7},{7,6},{8,9},{9,8},{10,11... | collective-permute-start | bytes 1966088 | tf_op jit(solution)/shard_map/ppermute | solution.py:137
  112.5 7.7 %collective-permute-start.30 = (bf16[1328,384]{1,0:T(8,128)(2,1)S(1)}, bf16[1328,384]{1,0:T(8,128)(2,1)S(1)}, u32[]{:S(2)}, u32[]{:S(2)}) collective-permute-start(bf16[1328,384]{1,0:T(8,128)(2,1)S(1)} %collective-permute-done.23.refs_7_.refs_6_), channel_id=1, source_target_pairs={{0,1},{1,0},{2,3},{3,2},{4,5},{5,4},{6,7},{7,6},{8,9},{9,8},{10,11... | collective-permute-start | bytes 3059720 | tf_op jit(solution)/shard_map/ppermute | solution.py:71
  113.7 6.0 %collective-permute-start.31 = (bf16[1120,384]{1,0:T(8,128)(2,1)}, bf16[1120,384]{1,0:T(8,128)(2,1)}, u32[]{:S(2)}, u32[]{:S(2)}) collective-permute-start(bf16[1120,384]{1,0:T(8,128)(2,1)} %collective-permute-done.24.refs_8_.refs_5_), channel_id=1, source_target_pairs={{0,1},{1,0},{2,3},{3,2},{4,5},{5,4},{6,7},{7,6},{8,9},{9,8},{10,11... | collective-permute-start | bytes 2580488 | tf_op jit(solution)/shard_map/ppermute | solution.py:71
  113.7 4.8 %collective-permute-start.27 = (bf16[352,384]{1,0:T(8,128)(2,1)}, bf16[352,384]{1,0:T(8,128)(2,1)}, u32[]{:S(2)}, u32[]{:S(2)}) collective-permute-start(bf16[352,384]{1,0:T(8,128)(2,1)} %bitcast.22.refs_1_), channel_id=1, source_target_pairs={{0,1},{1,0},{2,3},{3,2},{4,5},{5,4},{6,7},{7,6},{8,9},{9,8},{10,11... | collective-permute-start | bytes 811016 | tf_op jit(solution)/shard_map/ppermute | solution.py:71
  117.7 19.6 %collective-permute-start.35 = (bf16[384,384]{1,0:T(8,128)(2,1)S(1)}, bf16[384,384]{1,0:T(8,128)(2,1)}, u32[]{:S(2)}, u32[]{:S(2)}) collective-permute-start(bf16[384,384]{1,0:T(8,128)(2,1)S(1)} %collective-permute-done.11.refs_3_), channel_id=1, source_target_pairs={{0,1},{1,0},{2,3},{3,2},{4,5},{5,4},{6,7},{7,6},{8,9},{9,8},{10,11... | collective-permute-start | bytes 884744 | tf_op jit(solution)/shard_map/ppermute | solution.py:71
  118.1 19.2 %collective-permute-start.36 = (bf16[384,384]{1,0:T(8,128)(2,1)S(1)}, bf16[384,384]{1,0:T(8,128)(2,1)}, u32[]{:S(2)}, u32[]{:S(2)}) collective-permute-start(bf16[384,384]{1,0:T(8,128)(2,1)S(1)} %collective-permute-done.12.refs_4_), channel_id=1, source_target_pairs={{0,1},{1,0},{2,3},{3,2},{4,5},{5,4},{6,7},{7,6},{8,9},{9,8},{10,11... | collective-permute-start | bytes 884744 | tf_op jit(solution)/shard_map/ppermute | solution.py:71
  118.4 18.8 %collective-permute-start.33 = (bf16[384,384]{1,0:T(8,128)(2,1)}, bf16[384,384]{1,0:T(8,128)(2,1)}, u32[]{:S(2)}, u32[]{:S(2)}) collective-permute-start(bf16[384,384]{1,0:T(8,128)(2,1)} %get-tuple-element.373), channel_id=1, source_target_pairs={{0,4},{4,0},{8,12},{12,8},{16,20},{20,16},{24,28},{28,24},{1,5},{5... | collective-permute-start | bytes 884744 | tf_op jit(solution)/shard_map/ppermute | solution.py:137
  119.7 17.6 %collective-permute-start.34 = (bf16[768,384]{1,0:T(8,128)(2,1)S(1)}, bf16[768,384]{1,0:T(8,128)(2,1)}, u32[]{:S(2)}, u32[]{:S(2)}) collective-permute-start(bf16[768,384]{1,0:T(8,128)(2,1)S(1)} %bitcast.172), channel_id=1, source_target_pairs={{0,1},{1,0},{2,3},{3,2},{4,5},{5,4},{6,7},{7,6},{8,9},{9,8},{10,11... | collective-permute-start | bytes 1769480 | tf_op jit(solution)/shard_map/ppermute | solution.py:71
  120.2 17.1 %collective-permute-start.32 = (bf16[2,384,384]{2,1,0:T(8,128)(2,1)}, bf16[2,384,384]{2,1,0:T(8,128)(2,1)}, u32[]{:S(2)}, u32[]{:S(2)}) collective-permute-start(bf16[2,384,384]{2,1,0:T(8,128)(2,1)} %bitcast.201), channel_id=1, source_target_pairs={{0,2},{2,0},{1,3},{3,1},{4,6},{6,4},{5,7},{7,5},{8,10},{10,8},{9,1... | collective-permute-start | bytes 1769480 | tf_op jit(solution)/shard_map/ppermute | solution.py:137
  158.2 12.2 %collective-permute-start.39 = (bf16[8,2,192,384]{3,2,1,0:T(8,128)(2,1)S(1)}, bf16[8,2,192,384]{3,2,1,0:T(8,128)(2,1)S(1)}, u32[]{:S(2)}, u32[]{:S(2)}) collective-permute-start(bf16[8,2,192,384]{3,2,1,0:T(8,128)(2,1)S(1)} %shard_map.253), channel_id=1, source_target_pairs={{0,1},{1,0},{2,3},{3,2},{4,5},{5,4},{6,7},{7,6},{8,9},{9,8},{10,11... | collective-permute-start | bytes 7077896 | tf_op jit(solution)/shard_map/ppermute | solution.py:137
  172.4 16.8 %collective-permute-start.42 = (bf16[8,2,192,384]{3,2,1,0:T(8,128)(2,1)S(1)}, bf16[8,2,192,384]{3,2,1,0:T(8,128)(2,1)S(1)}, u32[]{:S(2)}, u32[]{:S(2)}) collective-permute-start(bf16[8,2,192,384]{3,2,1,0:T(8,128)(2,1)S(1)} %shard_map.256), channel_id=1, source_target_pairs={{0,1},{1,0},{2,3},{3,2},{4,5},{5,4},{6,7},{7,6},{8,9},{9,8},{10,11... | collective-permute-start | bytes 7077896 | tf_op jit(solution)/shard_map/ppermute | solution.py:137
  172.6 16.3 %collective-permute-start.41 = (bf16[2,192,384]{2,1,0:T(8,128)(2,1)S(1)}, bf16[2,192,384]{2,1,0:T(8,128)(2,1)S(1)}, u32[]{:S(2)}, u32[]{:S(2)}) collective-permute-start(bf16[2,192,384]{2,1,0:T(8,128)(2,1)S(1)} %get-tuple-element.422), channel_id=1, source_target_pairs={{0,8},{8,0},{4,12},{12,4},{16,24},{24,16},{20,28},{28,20},{1,9},{9... | collective-permute-start | bytes 884744 | tf_op jit(solution)/shard_map/ppermute | solution.py:137
  172.6 16.3 %collective-permute-start.43 = (bf16[2,192,384]{2,1,0:T(8,128)(2,1)S(1)}, bf16[2,192,384]{2,1,0:T(8,128)(2,1)S(1)}, u32[]{:S(2)}, u32[]{:S(2)}) collective-permute-start(bf16[2,192,384]{2,1,0:T(8,128)(2,1)S(1)} %get-tuple-element.427), channel_id=1, source_target_pairs={{0,4},{4,0},{8,12},{12,8},{16,20},{20,16},{24,28},{28,24},{1,5},{5... | collective-permute-start | bytes 884744 | tf_op jit(solution)/shard_map/ppermute | solution.py:137
  173.6 15.3 %collective-permute-start.40 = (bf16[4,192,384]{2,1,0:T(8,128)(2,1)S(1)}, bf16[4,192,384]{2,1,0:T(8,128)(2,1)S(1)}, u32[]{:S(2)}, u32[]{:S(2)}) collective-permute-start(bf16[4,192,384]{2,1,0:T(8,128)(2,1)S(1)} %get-tuple-element.420), channel_id=1, source_target_pairs={{0,2},{2,0},{1,3},{3,1},{4,6},{6,4},{5,7},{7,5},{8,10},{10,8},{9,1... | collective-permute-start | bytes 1769480 | tf_op jit(solution)/shard_map/ppermute | solution.py:137
  191.2 17.7 %collective-permute-start.47 = (bf16[8,2,272,384]{3,2,1,0:T(8,128)(2,1)S(1)}, bf16[8,2,272,384]{3,2,1,0:T(8,128)(2,1)S(1)}, u32[]{:S(2)}, u32[]{:S(2)}) collective-permute-start(bf16[8,2,272,384]{3,2,1,0:T(8,128)(2,1)S(1)} %shard_map.260), channel_id=1, source_target_pairs={{0,1},{1,0},{2,3},{3,2},{4,5},{5,4},{6,7},{7,6},{8,9},{9,8},{10,11... | collective-permute-start | bytes 10027016 | tf_op jit(solution)/shard_map/ppermute | solution.py:137
  192.4 20.6 %collective-permute-start.45 = (bf16[576,384]{1,0:T(8,128)(2,1)S(1)}, bf16[576,384]{1,0:T(8,128)(2,1)S(1)}, u32[]{:S(2)}, u32[]{:S(2)}) collective-permute-start(bf16[576,384]{1,0:T(8,128)(2,1)S(1)} %pad_maximum_fusion.12), channel_id=1, source_target_pairs={{0,8},{8,0},{4,12},{12,4},{16,24},{24,16},{20,28},{28,20},{1,9},{9... | collective-permute-start | bytes 1327112 | tf_op jit(solution)/shard_map/ppermute | solution.py:137
  193.0 20.0 %collective-permute-start.46 = (bf16[4,192,384]{2,1,0:T(8,128)(2,1)S(1)}, bf16[4,192,384]{2,1,0:T(8,128)(2,1)S(1)}, u32[]{:S(2)}, u32[]{:S(2)}) collective-permute-start(bf16[4,192,384]{2,1,0:T(8,128)(2,1)S(1)} %get-tuple-element.455), channel_id=1, source_target_pairs={{0,2},{2,0},{1,3},{3,1},{4,6},{6,4},{5,7},{7,5},{8,10},{10,8},{9,1... | collective-permute-start | bytes 1769480 | tf_op jit(solution)/shard_map/ppermute | solution.py:137
  193.7 19.3 %collective-permute-start.44 = (bf16[960,384]{1,0:T(8,128)(2,1)S(1)}, bf16[960,384]{1,0:T(8,128)(2,1)S(1)}, u32[]{:S(2)}, u32[]{:S(2)}) collective-permute-start(bf16[960,384]{1,0:T(8,128)(2,1)S(1)} %pad_maximum_fusion.7), channel_id=1, source_target_pairs={{0,4},{4,0},{8,12},{12,8},{16,20},{20,16},{24,28},{28,24},{1,5},{5... | collective-permute-start | bytes 2211848 | tf_op jit(solution)/shard_map/ppermute | solution.py:137
  213.6 16.7 %collective-permute-start.49 = (bf16[928,384]{1,0:T(8,128)(2,1)S(1)}, bf16[928,384]{1,0:T(8,128)(2,1)S(1)}, u32[]{:S(2)}, u32[]{:S(2)}) collective-permute-start(bf16[928,384]{1,0:T(8,128)(2,1)S(1)} %pad_maximum_fusion.8), channel_id=1, source_target_pairs={{0,8},{8,0},{4,12},{12,4},{16,24},{24,16},{20,28},{28,20},{1,9},{9... | collective-permute-start | bytes 2138120 | tf_op jit(solution)/shard_map/ppermute | solution.py:137
  213.7 19.3 %collective-permute-start.52 = (bf16[4,272,384]{2,1,0:T(8,128)(2,1)S(1)}, bf16[4,272,384]{2,1,0:T(8,128)(2,1)S(1)}, u32[]{:S(2)}, u32[]{:S(2)}) collective-permute-start(bf16[4,272,384]{2,1,0:T(8,128)(2,1)S(1)} %get-tuple-element.539), channel_id=1, source_target_pairs={{0,2},{2,0},{1,3},{3,1},{4,6},{6,4},{5,7},{7,5},{8,10},{10,8},{9,1... | collective-permute-start | bytes 2506760 | tf_op jit(solution)/shard_map/ppermute | solution.py:137
  214.5 19.5 %collective-permute-start.50 = (bf16[1120,384]{1,0:T(8,128)(2,1)S(1)}, bf16[1120,384]{1,0:T(8,128)(2,1)S(1)}, u32[]{:S(2)}, u32[]{:S(2)}) collective-permute-start(bf16[1120,384]{1,0:T(8,128)(2,1)S(1)} %pad_maximum_fusion.6), channel_id=1, source_target_pairs={{0,4},{4,0},{8,12},{12,8},{16,20},{20,16},{24,28},{28,24},{1,5},{5... | collective-permute-start | bytes 2580488 | tf_op jit(solution)/shard_map/ppermute | solution.py:137
  215.5 18.8 %collective-permute-start.48 = (bf16[2,2,160,1024]{3,2,1,0:T(8,128)(2,1)S(1)}, bf16[2,2,160,1024]{3,2,1,0:T(8,128)(2,1)S(1)}, u32[]{:S(2)}, u32[]{:S(2)}) collective-permute-start(bf16[2,2,160,1024]{3,2,1,0:T(8,128)(2,1)S(1)} %get-tuple-element.527), channel_id=1, source_target_pairs={{0,1},{1,0},{2,3},{3,2},{4,5},{5,4},{6,7},{7,6},{8,9},{9,8},{10,11... | collective-permute-start | bytes 3932168 | tf_op jit(solution)/shard_map/ppermute | solution.py:137
  217.2 17.7 %collective-permute-start.51 = (bf16[8,2,144,384]{3,2,1,0:T(8,128)(2,1)S(1)}, bf16[8,2,144,384]{3,2,1,0:T(8,128)(2,1)S(1)}, u32[]{:S(2)}, u32[]{:S(2)}) collective-permute-start(bf16[8,2,144,384]{3,2,1,0:T(8,128)(2,1)S(1)} %shard_map.264), channel_id=1, source_target_pairs={{0,1},{1,0},{2,3},{3,2},{4,5},{5,4},{6,7},{7,6},{8,9},{9,8},{10,11... | collective-permute-start | bytes 5308424 | tf_op jit(solution)/shard_map/ppermute | solution.py:137
  236.6 7.5 %collective-permute-start.55 = (bf16[192,384]{1,0:T(8,128)(2,1)S(1)}, bf16[192,384]{1,0:T(8,128)(2,1)S(1)}, u32[]{:S(2)}, u32[]{:S(2)}) collective-permute-start(bf16[192,384]{1,0:T(8,128)(2,1)S(1)} %fusion.13), channel_id=1, source_target_pairs={{0,16},{16,0},{4,20},{20,4},{8,24},{24,8},{12,28},{28,12},{1,17},{... | collective-permute-start | bytes 442376 | tf_op jit(solution)/shard_map/ppermute | solution.py:137
  238.2 10.4 %collective-permute-start.57 = (bf16[4,160,384]{2,1,0:T(8,128)(2,1)S(1)}, bf16[4,160,384]{2,1,0:T(8,128)(2,1)S(1)}, u32[]{:S(2)}, u32[]{:S(2)}) collective-permute-start(bf16[4,160,384]{2,1,0:T(8,128)(2,1)S(1)} %get-tuple-element.550), channel_id=1, source_target_pairs={{0,2},{2,0},{1,3},{3,1},{4,6},{6,4},{5,7},{7,5},{8,10},{10,8},{9,1... | collective-permute-start | bytes 1474568 | tf_op jit(solution)/shard_map/ppermute | solution.py:137
  238.9 16.2 %collective-permute-start.56 = (bf16[784,384]{1,0:T(8,128)(2,1)S(1)}, bf16[784,384]{1,0:T(8,128)(2,1)S(1)}, u32[]{:S(2)}, u32[]{:S(2)}) collective-permute-start(bf16[784,384]{1,0:T(8,128)(2,1)S(1)} %pad_maximum_fusion.10), channel_id=1, source_target_pairs={{0,8},{8,0},{4,12},{12,4},{16,24},{24,16},{20,28},{28,20},{1,9},{9... | collective-permute-start | bytes 1806344 | tf_op jit(solution)/shard_map/ppermute | solution.py:137
  240.1 57.8 %collective-permute-start.53 = (bf16[2,160,1024]{2,1,0:T(8,128)(2,1)S(1)}, bf16[2,160,1024]{2,1,0:T(8,128)(2,1)S(1)}, u32[]{:S(2)}, u32[]{:S(2)}) collective-permute-start(bf16[2,160,1024]{2,1,0:T(8,128)(2,1)S(1)} %fusion.1), channel_id=1, source_target_pairs={{0,2},{2,0},{1,3},{3,1},{4,6},{6,4},{5,7},{7,5},{8,10},{10,8},{9,1... | collective-permute-start | bytes 1966088 | tf_op jit(solution)/shard_map/ppermute | solution.py:137
  240.9 17.4 %collective-permute-start.54 = (bf16[1136,384]{1,0:T(8,128)(2,1)S(1)}, bf16[1136,384]{1,0:T(8,128)(2,1)S(1)}, u32[]{:S(2)}, u32[]{:S(2)}) collective-permute-start(bf16[1136,384]{1,0:T(8,128)(2,1)S(1)} %pad_maximum_fusion.3), channel_id=1, source_target_pairs={{0,4},{4,0},{8,12},{12,8},{16,20},{20,16},{24,28},{28,24},{1,5},{5... | collective-permute-start | bytes 2617352 | tf_op jit(solution)/shard_map/ppermute | solution.py:137
  258.7 6.6 %collective-permute-start.60 = (bf16[192,384]{1,0:T(8,128)(2,1)S(1)}, bf16[192,384]{1,0:T(8,128)(2,1)S(1)}, u32[]{:S(2)}, u32[]{:S(2)}) collective-permute-start(bf16[192,384]{1,0:T(8,128)(2,1)S(1)} %fusion.11), channel_id=1, source_target_pairs={{0,16},{16,0},{4,20},{20,4},{8,24},{24,8},{12,28},{28,12},{1,17},{... | collective-permute-start | bytes 442376 | tf_op jit(solution)/shard_map/ppermute | solution.py:137
  259.6 25.6 %collective-permute-start.70 = (bf16[2,192,384]{2,1,0:T(8,128)(2,1)S(1)}, bf16[2,192,384]{2,1,0:T(8,128)(2,1)S(1)}, u32[]{:S(2)}, u32[]{:S(2)}) collective-permute-start(bf16[2,192,384]{2,1,0:T(8,128)(2,1)S(1)} %pad_maximum_fusion.17), channel_id=1, source_target_pairs={{0,2},{2,0},{1,3},{3,1},{4,6},{6,4},{5,7},{7,5},{8,10},{10,8},{9,1... | collective-permute-start | bytes 884744 | tf_op jit(solution)/shard_map/ppermute | solution.py:137
  260.3 8.0 %collective-permute-start.58 = (bf16[432,384]{1,0:T(8,128)(2,1)S(1)}, bf16[432,384]{1,0:T(8,128)(2,1)S(1)}, u32[]{:S(2)}, u32[]{:S(2)}) collective-permute-start(bf16[432,384]{1,0:T(8,128)(2,1)S(1)} %pad_maximum_fusion.16), channel_id=1, source_target_pairs={{0,8},{8,0},{4,12},{12,4},{16,24},{24,16},{20,28},{28,20},{1,9},{9... | collective-permute-start | bytes 995336 | tf_op jit(solution)/shard_map/ppermute | solution.py:137
  260.9 7.4 %collective-permute-start.59 = (bf16[3,160,384]{2,1,0:T(8,128)(2,1)S(1)}, bf16[3,160,384]{2,1,0:T(8,128)(2,1)S(1)}, u32[]{:S(2)}, u32[]{:S(2)}) collective-permute-start(bf16[3,160,384]{2,1,0:T(8,128)(2,1)S(1)} %add_convert_fusion.4), channel_id=1, source_target_pairs={{0,4},{4,0},{8,12},{12,8},{16,20},{20,16},{24,28},{28,24},{1,5},{5... | collective-permute-start | bytes 1105928 | tf_op jit(solution)/shard_map/ppermute | solution.py:137
  268.5 6.8 %collective-permute-start.61 = (bf16[160,384]{1,0:T(8,128)(2,1)S(1)}, bf16[160,384]{1,0:T(8,128)(2,1)S(1)}, u32[]{:S(2)}, u32[]{:S(2)}) collective-permute-start(bf16[160,384]{1,0:T(8,128)(2,1)S(1)} %fusion.39), channel_id=1, source_target_pairs={{0,8},{8,0},{4,12},{12,4},{16,24},{24,16},{20,28},{28,20},{1,9},{9... | collective-permute-start | bytes 368648 | tf_op jit(solution)/shard_map/ppermute | solution.py:137
  268.6 8.9 %collective-permute-start.66 = (bf16[272,384]{1,0:T(8,128)(2,1)S(1)}, bf16[272,384]{1,0:T(8,128)(2,1)S(1)}, u32[]{:S(2)}, u32[]{:S(2)}) collective-permute-start(bf16[272,384]{1,0:T(8,128)(2,1)S(1)} %fusion.4), channel_id=1, source_target_pairs={{0,16},{16,0},{4,20},{20,4},{8,24},{24,8},{12,28},{28,12},{1,17},{... | collective-permute-start | bytes 626696 | tf_op jit(solution)/shard_map/ppermute | solution.py:137
  272.0 23.3 %collective-permute-start.64 = (bf16[2,192,384]{2,1,0:T(8,128)(2,1)S(1)}, bf16[2,192,384]{2,1,0:T(8,128)(2,1)S(1)}, u32[]{:S(2)}, u32[]{:S(2)}) collective-permute-start(bf16[2,192,384]{2,1,0:T(8,128)(2,1)S(1)} %pad_maximum_fusion.18), channel_id=1, source_target_pairs={{0,2},{2,0},{1,3},{3,1},{4,6},{6,4},{5,7},{7,5},{8,10},{10,8},{9,1... | collective-permute-start | bytes 884744 | tf_op jit(solution)/shard_map/ppermute | solution.py:137
  275.3 6.5 %collective-permute-start.62 = (bf16[160,384]{1,0:T(8,128)(2,1)S(1)}, bf16[160,384]{1,0:T(8,128)(2,1)S(1)}, u32[]{:S(2)}, u32[]{:S(2)}) collective-permute-start(bf16[160,384]{1,0:T(8,128)(2,1)S(1)} %fusion.24), channel_id=1, source_target_pairs={{0,16},{16,0},{4,20},{20,4},{8,24},{24,8},{12,28},{28,12},{1,17},{... | collective-permute-start | bytes 368648 | tf_op jit(solution)/shard_map/ppermute | solution.py:1337
  277.6 12.7 %collective-permute-start.68 = (bf16[2,272,384]{2,1,0:T(8,128)(2,1)S(1)}, bf16[2,272,384]{2,1,0:T(8,128)(2,1)S(1)}, u32[]{:S(2)}, u32[]{:S(2)}) collective-permute-start(bf16[2,272,384]{2,1,0:T(8,128)(2,1)S(1)} %pad_maximum_fusion.13), channel_id=1, source_target_pairs={{0,2},{2,0},{1,3},{3,1},{4,6},{6,4},{5,7},{7,5},{8,10},{10,8},{9,1... | collective-permute-start | bytes 1253384 | tf_op jit(solution)/shard_map/ppermute | solution.py:1337
  281.9 13.5 %collective-permute-start.63 = (bf16[2,160,384]{2,1,0:T(8,128)(2,1)S(1)}, bf16[2,160,384]{2,1,0:T(8,128)(2,1)S(1)}, u32[]{:S(2)}, u32[]{:S(2)}) collective-permute-start(bf16[2,160,384]{2,1,0:T(8,128)(2,1)S(1)} %pad_maximum_fusion.19), channel_id=1, source_target_pairs={{0,2},{2,0},{1,3},{3,1},{4,6},{6,4},{5,7},{7,5},{8,10},{10,8},{9,1... | collective-permute-start | bytes 737288 | tf_op jit(solution)/shard_map/ppermute | solution.py:1337
  285.3 14.2 %collective-permute-start.71 = (bf16[2,192,384]{2,1,0:T(8,128)(2,1)S(1)}, bf16[2,192,384]{2,1,0:T(8,128)(2,1)S(1)}, u32[]{:S(2)}, u32[]{:S(2)}) collective-permute-start(bf16[2,192,384]{2,1,0:T(8,128)(2,1)S(1)} %add_convert_fusion.5.mine), channel_id=1, source_target_pairs={{0,1},{1,0},{2,3},{3,2},{4,5},{5,4},{6,7},{7,6},{8,9},{9,8},{10,11... | collective-permute-start | bytes 884744 | tf_op jit(solution)/shard_map/ppermute | solution.py:513
  290.5 12.9 %collective-permute-start.69 = (bf16[2,272,384]{2,1,0:T(8,128)(2,1)S(1)}, bf16[2,272,384]{2,1,0:T(8,128)(2,1)S(1)}, u32[]{:S(2)}, u32[]{:S(2)}) collective-permute-start(bf16[2,272,384]{2,1,0:T(8,128)(2,1)S(1)} %add_convert_fusion.3.mine), channel_id=1, source_target_pairs={{0,1},{1,0},{2,3},{3,2},{4,5},{5,4},{6,7},{7,6},{8,9},{9,8},{10,11... | collective-permute-start | bytes 1253384 | tf_op jit(solution)/shard_map/ppermute | solution.py:513
  295.3 5.2 %collective-permute-start.65 = (bf16[2,192,384]{2,1,0:T(8,128)(2,1)S(1)}, bf16[2,192,384]{2,1,0:T(8,128)(2,1)S(1)}, u32[]{:S(2)}, u32[]{:S(2)}) collective-permute-start(bf16[2,192,384]{2,1,0:T(8,128)(2,1)S(1)} %add_convert_fusion.6.mine), channel_id=1, source_target_pairs={{0,1},{1,0},{2,3},{3,2},{4,5},{5,4},{6,7},{7,6},{8,9},{9,8},{10,11... | collective-permute-start | bytes 884744 | tf_op jit(solution)/shard_map/ppermute | solution.py:513
  295.5 6.2 %collective-permute-start.67 = (bf16[2,160,384]{2,1,0:T(8,128)(2,1)S(1)}, bf16[2,160,384]{2,1,0:T(8,128)(2,1)S(1)}, u32[]{:S(2)}, u32[]{:S(2)}) collective-permute-start(bf16[2,160,384]{2,1,0:T(8,128)(2,1)S(1)} %add_convert_fusion.7.mine), channel_id=1, source_target_pairs={{0,1},{1,0},{2,3},{3,2},{4,5},{5,4},{6,7},{7,6},{8,9},{9,8},{10,11... | collective-permute-start | bytes 737288 | tf_op jit(solution)/shard_map/ppermute | solution.py:513
  (72 other events, 591.4 us)

commit v3 on v2

--- a/solution.py
+++ b/solution.py
@@ -198,7 +198,7 @@
 ANY = pl.BlockSpec(memory_space=pl.ANY)
 
 
-def call(kernel, out_shape, in_specs, scratch=(), mib=20, flops=0, out_specs=None, **more):
+def call(kernel, out_shape, in_specs, scratch=(), mib=18, flops=0, out_specs=None, **more):
     return pl.pallas_call(
         kernel,
         out_shape=out_shape,

time: 310 us -> 310 us (level)
  starting transfers between devices: 72.1 us -> 68.9 us
    ppermute x3, starting transfers between devices: 4.16 us -> 0.56 us  [finish(): lax.ppermute(array, axis, hops)]
where the time goes in v3:
time: 310 us; the launch traced here: 305 us
  waiting for transfers between devices  110 us (35%)
  Pallas kernels  99.1 us (32%)
  starting transfers between devices  68.9 us (22%)
  local copies, waits for them, and re-layouts  18.3 us (6%)
  other arithmetic  6.3 us (2%)
    ppermute x47, waiting for transfers between devices, step(): lax.ppermute(array, axis, hops)  96.1 us
    ppermute x47, starting transfers between devices, step(): lax.ppermute(array, axis, hops)  44.1 us
    pallas_call x1, Pallas kernels, run_patch(): call(functools.partial(patch_kernel, units, len(sources), spec, seq, patc...  15.7 us
    pallas_call x1, Pallas kernels, run_text(): call(functools.partial(text_kernel, units, len(sources), spec, seq), outs...  13.5 us
    ppermute x4, starting transfers between devices, reduce_steps(): return (total, lax.ppermute(total, STREAM, CORE))  13.2 us
    unnamed x130, local copies, waits for them, and re-layouts  11.7 us
    ppermute x18, starting transfers between devices, exchange(): self.twin = lax.ppermute(tie(self.array), STREAM, CORE)  11 us
    pallas_call x1, Pallas kernels, run_ffn(): call(functools.partial(ffn_kernel, len(sources), spec, in_units, seq), [s...  10.5 us
  transfers between devices with their start and end apart: 72, of which 27 were waited for; matrix products, arithmetic and copies ran while one was open for 2% of the time, Pallas kernels for 26%

profile of v3, /device:TPU:1, one launch (start us, length us, event | category | flops | bytes accessed | tf_op | source)
XLA Modules:
  0.0 304.8 jit_solution(14001390281432539188)
XLA Ops:
  1.5 1.3 copy.31
  4.8 2.0 collective-permute-start.4
  6.9 1.3 collective-permute-start
  8.1 1.2 collective-permute-start.3
  9.4 2.3 collective-permute-start.1
  11.8 8.1 %collective-permute-done.1.refs_3_ = bf16[256,384]{1,0:T(8,128)(2,1)S(1)} collective-permute-done((bf16[256,384]{1,0:T(8,128)(2,1)S(1)}, bf16[256,384]{1,0:T(8,128)(2,1)S(1)}, u32[]{:S(2)}, u32[]{:S(2)}) %collective-permute-start.1) | collective-permute-done | bytes 196640 | tf_op jit(solution)/shard_map/ppermute | solution.py:137
  19.9 7.1 %collective-permute-done.2.refs_4_ = bf16[256,384]{1,0:T(8,128)(2,1)S(1)} collective-permute-done((bf16[256,384]{1,0:T(8,128)(2,1)S(1)}, bf16[256,384]{1,0:T(8,128)(2,1)S(1)}, u32[]{:S(2)}, u32[]{:S(2)}) %collective-permute-start.2) | collective-permute-done | bytes 196640 | tf_op jit(solution)/shard_map/ppermute | solution.py:137
  28.0 1.2 collective-permute-start.5
  29.5 1.3 collective-permute-start.8
  30.8 2.2 collective-permute-start.9
  33.2 1.8 collective-permute-done.8.refs_3_
  35.0 5.4 %collective-permute-done.9.refs_4_ = bf16[176,384]{1,0:T(8,128)(2,1)S(1)} collective-permute-done((bf16[176,384]{1,0:T(8,128)(2,1)S(1)}, bf16[176,384]{1,0:T(8,128)(2,1)S(1)}, u32[]{:S(2)}, u32[]{:S(2)}) %collective-permute-start.9) | collective-permute-done | bytes 135200 | tf_op jit(solution)/shard_map/ppermute | solution.py:137
  40.8 5.8 %collective-permute-done.5.refs_6_.refs_2_ = bf16[1120,384]{1,0:T(8,128)(2,1)S(1)} collective-permute-done((bf16[1120,384]{1,0:T(8,128)(2,1)S(1)}, bf16[1120,384]{1,0:T(8,128)(2,1)S(1)}, u32[]{:S(2)}, u32[]{:S(2)}) %collective-permute-start.5) | collective-permute-done | bytes 860192 | tf_op jit(solution)/shard_map/ppermute | solution.py:137
  46.6 1.3 constant_dynamic-slice_fusion.1
  48.3 1.3 collective-permute-start.13
  49.8 1.2 collective-permute-start.11
  51.1 2.3 collective-permute-start.12
  53.4 12.3 %collective-permute-done.11.refs_3_ = bf16[384,384]{1,0:T(8,128)(2,1)S(1)} collective-permute-done((bf16[384,384]{1,0:T(8,128)(2,1)S(1)}, bf16[384,384]{1,0:T(8,128)(2,1)S(1)}, u32[]{:S(2)}, u32[]{:S(2)}) %collective-permute-start.11) | collective-permute-done | bytes 294944 | tf_op jit(solution)/shard_map/ppermute | solution.py:137
  65.7 7.9 %collective-permute-done.12.refs_4_ = bf16[384,384]{1,0:T(8,128)(2,1)S(1)} collective-permute-done((bf16[384,384]{1,0:T(8,128)(2,1)S(1)}, bf16[384,384]{1,0:T(8,128)(2,1)S(1)}, u32[]{:S(2)}, u32[]{:S(2)}) %collective-permute-start.12) | collective-permute-done | bytes 294944 | tf_op jit(solution)/shard_map/ppermute | solution.py:137
  76.8 5.0 %collective-permute-start.15 = (bf16[512,384]{1,0:T(8,128)(2,1)S(1)}, bf16[512,384]{1,0:T(8,128)(2,1)S(1)}, u32[]{:S(2)}, u32[]{:S(2)}) collective-permute-start(bf16[512,384]{1,0:T(8,128)(2,1)S(1)} %bitcast.207), channel_id=1, source_target_pairs={{0,1},{1,0},{2,3},{3,2},{4,5},{5,4},{6,7},{7,6},{8,9},{9,8},{10,11... | collective-permute-start | bytes 1179656 | tf_op jit(solution)/shard_map/ppermute | solution.py:71
  85.0 2.2 collective-permute-done.16.refs_10_
  87.3 1.3 collective-permute-start.23
  93.1 13.5 %shard_map.250 = (f32[16,768]{1,0:T(8,128)}, f32[8,384]{1,0:T(8,128)}, bf16[320,768]{1,0:T(8,128)(2,1)}, f32[320,768]{1,0:T(8,128)}, f32[320,1]{1,0:T(8,128)}, /...) custom-call(s32[8]{0:T(128)} %reshape.233.lengths, ...), custom_call_target="tpu_custom_call" | custom-call | flops 3019898880 | bytes 4194304 | tf_op jit(solution)/shard_map/pallas_call | solution.py:1169
  106.7 2.7 collective-permute-done.24.refs_8_.refs_5_
  109.4 1.9 collective-permute-done.23.refs_7_.refs_6_
  115.0 2.4 collective-permute-done.28.refs_11_
  118.1 1.3 collective-permute-start.33
  121.2 15.7 %shard_map.251 = (bf16[320,768]{1,0:T(8,128)(2,1)}, f32[320,768]{1,0:T(8,128)}, f32[320,1]{1,0:T(8,128)}, bf16[320,768]{1,0:T(8,128)(2,1)}, bf16[4,2,2,160,768]{...) custom-call(s32[8]{0:T(128)} %xor.10.slots, ...), custom_call_target="tpu_custom_call" | custom-call | flops 6794772480 | bytes 4194304 | tf_op jit(solution)/shard_map/pallas_call | solution.py:1192
  137.6 2.1 collective-permute-done.37.refs_15_
  143.2 1.3 copy-done.14
  145.7 10.5 %shard_map.252 = (bf16[8,40,768]{2,1,0:T(8,128)(2,1)}, f32[320,768]{1,0:T(8,128)S(1)}, bf16[320,768]{1,0:T(8,128)(2,1)S(1)}, f32[8,768]{1,0:T(8,128)S(1)}, bf16[...) custom-call(s32[8]{0:T(128)S(1)} %copy-done.33, ...), custom_call_target="tpu_custom_call" | custom-call | flops 3019898880 | bytes 4194304 | tf_op jit(solution)/shard_map/pallas_call | solution.py:1211
  156.2 1.7 shard_map.253
  158.3 10.3 %shard_map.254 = (bf16[320,3072]{1,0:T(8,128)(2,1)S(1)}, f32[8,384]{1,0:T(8,128)S(1)}, f32[320,768]{1,0:T(8,128)S(1)}, bf16[320,768]{1,0:T(8,128)(2,1)S(1)}, f32[8,768]{1,0:T(8,128)S(1)}) custom-call(bf16[320,768]{1,0:T(8,128)(2,1)S(1)} %get-tuple-element.397.refs_1_.df, bf16[8,2,2,384,384]{4,3,2,1,0:T(8,128)(2,1)S(1)} %get-tuple-element.398.wout.win, ...), custom_call_target="tpu_custom_call" | custom-call | flops 3019898880 | bytes 4194304 | tf_op jit(solution)/shard_map/pallas_call | solution.py:1232
  168.6 1.4 shard_map.256
  170.1 2.0 shard_map.255
  174.3 8.5 %shard_map.257 = (bf16[320,768]{1,0:T(8,128)(2,1)S(1)}, bf16[2,4,2,160,768]{4,3,2,1,0:T(8,128)(2,1)S(1)}) custom-call(s32[8]{0:T(128)S(1)} %copy-done.34, bf16[320,768]{1,0:T(8,128)(2,1)S(1)} %get-tuple-element.410.dac.refs_1_, bf16[320,768]{1,0:T(8,128)(2,1)S(1)} %copy-done.23, bf16[4,2,2,160,768]{4,3,2,1,0:T(8,128)(2,1)S(1)} %copy-done.2, ...), custom_call_target="tpu_custom_call" | custom-call | flops 1509949440 | bytes 4194304 | tf_op jit(solution)/shard_map/pallas_call | solution.py:1262
  182.9 2.5 shard_map.258
  185.4 3.4 %shard_map.260 = bf16[8,2,272,384]{3,2,1,0:T(8,128)(2,1)S(1)} custom-call(bf16[320,768]{1,0:T(8,128)(2,1)S(1)} %copy-done.10, bf16[320,768]{1,0:T(8,128)(2,1)S(1)} %get-tuple-element.410.dac.refs_1_, bf16[320,768]{1,0:T(8,128)(2,1)S(1)} %copy-done.9, bf16[320,768]{1,0:T(8,128)(2,1)S(1)} %get-tuple-element.458.dqc.refs_3_, bf16[320,768]{1,0:T(8,128)(2,1)S(1)} %copy-done.8, ...), custom_call_target="tpu_custom_call" | custom-call | flops 2579496960 | bytes 4194304 | tf_op jit(solution)/shard_map/pallas_call | solution.py:581
  189.0 1.9 shard_map.259
  193.5 1.3 collective-permute-start.44
  194.8 5.6 %shard_map.262 = (bf16[2,2,160,1024]{3,2,1,0:T(8,128)(2,1)S(1)}, bf16[2,2,160,1024]{3,2,1,0:T(8,128)(2,1)S(1)}, f32[8,768]{1,0:T(8,128)S(1)}) custom-call(bf16[2,4,2,160,768]{4,3,2,1,0:T(8,128)(2,1)S(1)} %get-tuple-element.472.dkv, bf16[2,2,1024,384]{3,2,1,0:T(8,128)(2,1)S(1)} %copy-done.39), custom_call_target="tpu_custom_call" | custom-call | flops 6039797760 | bytes 4194304 | tf_op jit(solution)/shard_map/pallas_call | solution.py:1298
  200.5 7.1 %shard_map.261 = (bf16[3,320,768]{2,1,0:T(8,128)(2,1)S(1)}, f32[8,768]{1,0:T(8,128)S(1)}) custom-call(s32[8]{0:T(128)S(1)} %copy-done.33, bf16[320,768]{1,0:T(8,128)(2,1)S(1)} %get-tuple-element.468.refs_5_.da, bf16[3,320,768]{2,1,0:T(8,128)(2,1)S(1)} %copy-done.37, bf16[2,1,768,384]{3,2,1,0:T(8,128)(2,1)S(1)} %copy-done.38), custom_call_target="tpu_custom_call" | custom-call | flops 1509949440 | bytes 4194304 | tf_op jit(solution)/shard_map/pallas_call | solution.py:1288
  208.8 4.0 %shard_map.263 = (bf16[4,272,384]{2,1,0:T(8,128)(2,1)S(1)}, bf16[2,272,384]{2,1,0:T(8,128)(2,1)S(1)}, bf16[2,272,384]{2,1,0:T(8,128)(2,1)S(1)}, bf16[3,272,384]{...) custom-call(bf16[320,768]{1,0:T(8,128)(2,1)S(1)} %copy-done.10, ...), custom_call_target="tpu_custom_call" | custom-call | flops 2579496960 | bytes 4194304 | tf_op jit(solution)/shard_map/pallas_call | solution.py:608
  215.5 1.7 collective-permute-start.48
  217.2 2.5 shard_map.265
  219.7 10.6 %collective-permute-done.49 = bf16[928,384]{1,0:T(8,128)(2,1)S(1)} collective-permute-done((bf16[928,384]{1,0:T(8,128)(2,1)S(1)}, bf16[928,384]{1,0:T(8,128)(2,1)S(1)}, u32[]{:S(2)}, u32[]{:S(2)}) %collective-permute-start.49) | collective-permute-done | bytes 712736 | tf_op jit(solution)/shard_map/ppermute | solution.py:137
  230.3 2.6 collective-permute-done.52
  234.8 1.5 shard_map.266
  236.5 1.6 collective-permute-start.55
  240.9 2.9 collective-permute-done.55
  244.0 4.4 %collective-permute-done.57 = bf16[4,160,384]{2,1,0:T(8,128)(2,1)S(1)} collective-permute-done((bf16[4,160,384]{2,1,0:T(8,128)(2,1)S(1)}, bf16[4,160,384]{2,1,0:T(8,128)(2,1)S(1)}, u32[]{:S(2)}, u32[]{:S(2)}) %collective-permute-start.57) | collective-permute-done | bytes 491552 | tf_op jit(solution)/shard_map/ppermute | solution.py:137
  248.4 6.6 %collective-permute-done.56 = bf16[784,384]{1,0:T(8,128)(2,1)S(1)} collective-permute-done((bf16[784,384]{1,0:T(8,128)(2,1)S(1)}, bf16[784,384]{1,0:T(8,128)(2,1)S(1)}, u32[]{:S(2)}, u32[]{:S(2)}) %collective-permute-start.56) | collective-permute-done | bytes 602144 | tf_op jit(solution)/shard_map/ppermute | solution.py:137
  255.2 3.0 collective-permute-done.54
  261.3 3.9 %collective-permute-done.60 = bf16[192,384]{1,0:T(8,128)(2,1)S(1)} collective-permute-done((bf16[192,384]{1,0:T(8,128)(2,1)S(1)}, bf16[192,384]{1,0:T(8,128)(2,1)S(1)}, u32[]{:S(2)}, u32[]{:S(2)}) %collective-permute-start.60) | collective-permute-done | bytes 147488 | tf_op jit(solution)/shard_map/ppermute | solution.py:137
  265.4 2.9 collective-permute-done.58
  268.6 3.3 %collective-permute-start.66 = (bf16[272,384]{1,0:T(8,128)(2,1)S(1)}, bf16[272,384]{1,0:T(8,128)(2,1)S(1)}, u32[]{:S(2)}, u32[]{:S(2)}) collective-permute-start(bf16[272,384]{1,0:T(8,128)(2,1)S(1)} %fusion.4), channel_id=1, source_target_pairs={{0,16},{16,0},{4,20},{20,4},{8,24},{24,8},{12,28},{28,12},{1,17},{... | collective-permute-start | bytes 626696 | tf_op jit(solution)/shard_map/ppermute | solution.py:137
  272.3 3.0 collective-permute-done.61
  275.5 1.9 collective-permute-done.66
  278.0 6.1 %collective-permute-done.62 = bf16[160,384]{1,0:T(8,128)(2,1)S(1)} collective-permute-done((bf16[160,384]{1,0:T(8,128)(2,1)S(1)}, bf16[160,384]{1,0:T(8,128)(2,1)S(1)}, u32[]{:S(2)}, u32[]{:S(2)}) %collective-permute-start.62) | collective-permute-done | bytes 122912 | tf_op jit(solution)/shard_map/ppermute | solution.py:1337
  284.4 6.4 %collective-permute-start.71 = (bf16[2,192,384]{2,1,0:T(8,128)(2,1)S(1)}, bf16[2,192,384]{2,1,0:T(8,128)(2,1)S(1)}, u32[]{:S(2)}, u32[]{:S(2)}) collective-permute-start(bf16[2,192,384]{2,1,0:T(8,128)(2,1)S(1)} %add_convert_fusion.5.mine), channel_id=1, source_target_pairs={{0,1},{1,0},{2,3},{3,2},{4,5},{5,4},{6,7},{7,6},{8,9},{9,8},{10,11... | collective-permute-start | bytes 884744 | tf_op jit(solution)/shard_map/ppermute | solution.py:513
  290.9 4.3 %collective-permute-start.69 = (bf16[2,272,384]{2,1,0:T(8,128)(2,1)S(1)}, bf16[2,272,384]{2,1,0:T(8,128)(2,1)S(1)}, u32[]{:S(2)}, u32[]{:S(2)}) collective-permute-start(bf16[2,272,384]{2,1,0:T(8,128)(2,1)S(1)} %add_convert_fusion.3.mine), channel_id=1, source_target_pairs={{0,1},{1,0},{2,3},{3,2},{4,5},{5,4},{6,7},{7,6},{8,9},{9,8},{10,11... | collective-permute-start | bytes 1253384 | tf_op jit(solution)/shard_map/ppermute | solution.py:513
  295.5 2.3 collective-permute-start.67
  298.0 1.4 copy.29
  303.3 1.3 shard_map.269
  (314 shorter events, 51.2 us)
Async XLA Ops:
  4.8 22.2 %collective-permute-start.4 = (bf16[2,160,1024]{2,1,0:T(8,128)(2,1)}, bf16[2,160,1024]{2,1,0:T(8,128)(2,1)}, u32[]{:S(2)}, u32[]{:S(2)}) collective-permute-start(bf16[2,160,1024]{2,1,0:T(8,128)(2,1)} %shard_map.248.refs_17_), channel_id=1, source_target_pairs={{0,2},{2,0},{1,3},{3,1},{4,6},{6,4},{5,7},{7,5},{8,10},{10,8},{9,1... | collective-permute-start | bytes 1966088 | tf_op jit(solution)/shard_map/ppermute | solution.py:137
  6.9 20.2 %collective-permute-start = (bf16[2,256,384]{2,1,0:T(8,128)(2,1)S(1)}, bf16[2,256,384]{2,1,0:T(8,128)(2,1)S(1)}, u32[]{:S(2)}, u32[]{:S(2)}) collective-permute-start(bf16[2,256,384]{2,1,0:T(8,128)(2,1)S(1)} %get-tuple-element.298), channel_id=1, source_target_pairs={{0,8},{8,0},{4,12},{12,4},{16,24},{24,16},{20,28},{28,20},{1,9},{9... | collective-permute-start | bytes 1179656 | tf_op jit(solution)/shard_map/ppermute | solution.py:137
  8.1 18.9 %collective-permute-start.3 = (bf16[2,256,384]{2,1,0:T(8,128)(2,1)S(1)}, bf16[2,256,384]{2,1,0:T(8,128)(2,1)S(1)}, u32[]{:S(2)}, u32[]{:S(2)}) collective-permute-start(bf16[2,256,384]{2,1,0:T(8,128)(2,1)S(1)} %get-tuple-element.298), channel_id=1, source_target_pairs={{0,4},{4,0},{8,12},{12,8},{16,20},{20,16},{24,28},{28,24},{1,5},{5... | collective-permute-start | bytes 1179656 | tf_op jit(solution)/shard_map/ppermute | solution.py:137
  9.4 10.5 %collective-permute-start.1 = (bf16[256,384]{1,0:T(8,128)(2,1)S(1)}, bf16[256,384]{1,0:T(8,128)(2,1)S(1)}, u32[]{:S(2)}, u32[]{:S(2)}) collective-permute-start(bf16[256,384]{1,0:T(8,128)(2,1)S(1)} %get-tuple-element.297), channel_id=1, source_target_pairs={{0,16},{16,0},{4,20},{20,4},{8,24},{24,8},{12,28},{28,12},{1,17},{... | collective-permute-start | bytes 589832 | tf_op jit(solution)/shard_map/ppermute | solution.py:137
  11.7 15.3 %collective-permute-start.2 = (bf16[256,384]{1,0:T(8,128)(2,1)S(1)}, bf16[256,384]{1,0:T(8,128)(2,1)S(1)}, u32[]{:S(2)}, u32[]{:S(2)}) collective-permute-start(bf16[256,384]{1,0:T(8,128)(2,1)S(1)} %get-tuple-element.297), channel_id=1, source_target_pairs={{0,24},{24,0},{4,28},{28,4},{8,16},{16,8},{12,20},{20,12},{1,25},{... | collective-permute-start | bytes 589832 | tf_op jit(solution)/shard_map/ppermute | solution.py:137
  28.0 18.7 %collective-permute-start.5 = (bf16[1120,384]{1,0:T(8,128)(2,1)S(1)}, bf16[1120,384]{1,0:T(8,128)(2,1)S(1)}, u32[]{:S(2)}, u32[]{:S(2)}) collective-permute-start(bf16[1120,384]{1,0:T(8,128)(2,1)S(1)} %pad_maximum_fusion.4), channel_id=1, source_target_pairs={{0,4},{4,0},{8,12},{12,8},{16,20},{20,16},{24,28},{28,24},{1,5},{5... | collective-permute-start | bytes 2580488 | tf_op jit(solution)/shard_map/ppermute | solution.py:137
  29.2 11.6 %collective-permute-start.6 = (bf16[512,384]{1,0:T(8,128)(2,1)S(1)}, bf16[512,384]{1,0:T(8,128)(2,1)S(1)}, u32[]{:S(2)}, u32[]{:S(2)}) collective-permute-start(bf16[512,384]{1,0:T(8,128)(2,1)S(1)} %pad_maximum_fusion.15), channel_id=1, source_target_pairs={{0,2},{2,0},{1,3},{3,1},{4,6},{6,4},{5,7},{7,5},{8,10},{10,8},{9,1... | collective-permute-start | bytes 1179656 | tf_op jit(solution)/shard_map/ppermute | solution.py:137
  29.4 11.4 %collective-permute-start.7 = (bf16[2,176,384]{2,1,0:T(8,128)(2,1)S(1)}, bf16[2,176,384]{2,1,0:T(8,128)(2,1)}, u32[]{:S(2)}, u32[]{:S(2)}) collective-permute-start(bf16[2,176,384]{2,1,0:T(8,128)(2,1)S(1)} %get-tuple-element.308), channel_id=1, source_target_pairs={{0,8},{8,0},{4,12},{12,4},{16,24},{24,16},{20,28},{28,20},{1,9},{9... | collective-permute-start | bytes 811016 | tf_op jit(solution)/shard_map/ppermute | solution.py:137
  29.5 5.6 %collective-permute-start.8 = (bf16[176,384]{1,0:T(8,128)(2,1)S(1)}, bf16[176,384]{1,0:T(8,128)(2,1)S(1)}, u32[]{:S(2)}, u32[]{:S(2)}) collective-permute-start(bf16[176,384]{1,0:T(8,128)(2,1)S(1)} %get-tuple-element.310), channel_id=1, source_target_pairs={{0,16},{16,0},{4,20},{20,4},{8,24},{24,8},{12,28},{28,12},{1,17},{... | collective-permute-start | bytes 405512 | tf_op jit(solution)/shard_map/ppermute | solution.py:137
  30.8 9.6 %collective-permute-start.9 = (bf16[176,384]{1,0:T(8,128)(2,1)S(1)}, bf16[176,384]{1,0:T(8,128)(2,1)S(1)}, u32[]{:S(2)}, u32[]{:S(2)}) collective-permute-start(bf16[176,384]{1,0:T(8,128)(2,1)S(1)} %get-tuple-element.310), channel_id=1, source_target_pairs={{0,24},{24,0},{4,28},{28,4},{8,16},{16,8},{12,20},{20,12},{1,25},{... | collective-permute-start | bytes 405512 | tf_op jit(solution)/shard_map/ppermute | solution.py:137
  48.3 25.3 %collective-permute-start.13 = (bf16[1552,384]{1,0:T(8,128)(2,1)S(1)}, bf16[1552,384]{1,0:T(8,128)(2,1)S(1)}, u32[]{:S(2)}, u32[]{:S(2)}) collective-permute-start(bf16[1552,384]{1,0:T(8,128)(2,1)S(1)} %pad_maximum_fusion), channel_id=1, source_target_pairs={{0,4},{4,0},{8,12},{12,8},{16,20},{20,16},{24,28},{28,24},{1,5},{5... | collective-permute-start | bytes 3575816 | tf_op jit(solution)/shard_map/ppermute | solution.py:137
  49.6 24.0 %collective-permute-start.14 = (bf16[864,384]{1,0:T(8,128)(2,1)S(1)}, bf16[864,384]{1,0:T(8,128)(2,1)S(1)}, u32[]{:S(2)}, u32[]{:S(2)}) collective-permute-start(bf16[864,384]{1,0:T(8,128)(2,1)S(1)} %pad_maximum_fusion.9), channel_id=1, source_target_pairs={{0,2},{2,0},{1,3},{3,1},{4,6},{6,4},{5,7},{7,5},{8,10},{10,8},{9,1... | collective-permute-start | bytes 1990664 | tf_op jit(solution)/shard_map/ppermute | solution.py:137
  49.8 23.7 %collective-permute-start.10 = (bf16[2,384,384]{2,1,0:T(8,128)(2,1)S(1)}, bf16[2,384,384]{2,1,0:T(8,128)(2,1)S(1)}, u32[]{:S(2)}, u32[]{:S(2)}) collective-permute-start(bf16[2,384,384]{2,1,0:T(8,128)(2,1)S(1)} %get-tuple-element.318), channel_id=1, source_target_pairs={{0,8},{8,0},{4,12},{12,4},{16,24},{24,16},{20,28},{28,20},{1,9},{9... | collective-permute-start | bytes 1769480 | tf_op jit(solution)/shard_map/ppermute | solution.py:137
  49.8 15.8 %collective-permute-start.11 = (bf16[384,384]{1,0:T(8,128)(2,1)S(1)}, bf16[384,384]{1,0:T(8,128)(2,1)S(1)}, u32[]{:S(2)}, u32[]{:S(2)}) collective-permute-start(bf16[384,384]{1,0:T(8,128)(2,1)S(1)} %get-tuple-element.320), channel_id=1, source_target_pairs={{0,16},{16,0},{4,20},{20,4},{8,24},{24,8},{12,28},{28,12},{1,17},{... | collective-permute-start | bytes 884744 | tf_op jit(solution)/shard_map/ppermute | solution.py:137
  51.1 22.5 %collective-permute-start.12 = (bf16[384,384]{1,0:T(8,128)(2,1)S(1)}, bf16[384,384]{1,0:T(8,128)(2,1)S(1)}, u32[]{:S(2)}, u32[]{:S(2)}) collective-permute-start(bf16[384,384]{1,0:T(8,128)(2,1)S(1)} %get-tuple-element.320), channel_id=1, source_target_pairs={{0,24},{24,0},{4,28},{28,4},{8,16},{16,8},{12,20},{20,12},{1,25},{... | collective-permute-start | bytes 884744 | tf_op jit(solution)/shard_map/ppermute | solution.py:137
  76.8 7.5 %collective-permute-start.15 = (bf16[512,384]{1,0:T(8,128)(2,1)S(1)}, bf16[512,384]{1,0:T(8,128)(2,1)S(1)}, u32[]{:S(2)}, u32[]{:S(2)}) collective-permute-start(bf16[512,384]{1,0:T(8,128)(2,1)S(1)} %bitcast.207), channel_id=1, source_target_pairs={{0,1},{1,0},{2,3},{3,2},{4,5},{5,4},{6,7},{7,6},{8,9},{9,8},{10,11... | collective-permute-start | bytes 1179656 | tf_op jit(solution)/shard_map/ppermute | solution.py:71
  82.4 8.3 %collective-permute-start.20 = (bf16[1120,384]{1,0:T(8,128)(2,1)S(1)}, bf16[1120,384]{1,0:T(8,128)(2,1)S(1)}, u32[]{:S(2)}, u32[]{:S(2)}) collective-permute-start(bf16[1120,384]{1,0:T(8,128)(2,1)S(1)} %collective-permute-done.5.refs_6_.refs_2_), channel_id=1, source_target_pairs={{0,1},{1,0},{2,3},{3,2},{4,5},{5,4},{6,7},{7,6},{8,9},{9,8},{10,11... | collective-permute-start | bytes 2580488 | tf_op jit(solution)/shard_map/ppermute | solution.py:71
  82.4 10.7 %collective-permute-start.21 = (bf16[1552,384]{1,0:T(8,128)(2,1)S(1)}, bf16[1552,384]{1,0:T(8,128)(2,1)}, u32[]{:S(2)}, u32[]{:S(2)}) collective-permute-start(bf16[1552,384]{1,0:T(8,128)(2,1)S(1)} %collective-permute-done.13.refs_7_.refs_6_.refs_2_), channel_id=1, source_target_pairs={{0,1},{1,0},{2,3},{3,2},{4,5},{5,4},{6,7},{7,6},{8,9},{9,8},{10,11... | collective-permute-start | bytes 3575816 | tf_op jit(solution)/shard_map/ppermute | solution.py:71
  84.2 5.8 %collective-permute-start.22 = (bf16[864,384]{1,0:T(8,128)(2,1)S(1)}, bf16[864,384]{1,0:T(8,128)(2,1)S(1)}, u32[]{:S(2)}, u32[]{:S(2)}) collective-permute-start(bf16[864,384]{1,0:T(8,128)(2,1)S(1)} %collective-permute-done.14.refs_8_.refs_5_), channel_id=1, source_target_pairs={{0,1},{1,0},{2,3},{3,2},{4,5},{5,4},{6,7},{7,6},{8,9},{9,8},{10,11... | collective-permute-start | bytes 1990664 | tf_op jit(solution)/shard_map/ppermute | solution.py:71
  87.3 24.0 %collective-permute-start.23 = (bf16[1328,384]{1,0:T(8,128)(2,1)}, bf16[1328,384]{1,0:T(8,128)(2,1)S(1)}, u32[]{:S(2)}, u32[]{:S(2)}) collective-permute-start(bf16[1328,384]{1,0:T(8,128)(2,1)} %pad_maximum_fusion.1), channel_id=1, source_target_pairs={{0,4},{4,0},{8,12},{12,8},{16,20},{20,16},{24,28},{28,24},{1,5},{5... | collective-permute-start | bytes 3059720 | tf_op jit(solution)/shard_map/ppermute | solution.py:137
  88.8 20.6 %collective-permute-start.24 = (bf16[1120,384]{1,0:T(8,128)(2,1)}, bf16[1120,384]{1,0:T(8,128)(2,1)}, u32[]{:S(2)}, u32[]{:S(2)}) collective-permute-start(bf16[1120,384]{1,0:T(8,128)(2,1)} %pad_maximum_fusion.5), channel_id=1, source_target_pairs={{0,2},{2,0},{1,3},{3,1},{4,6},{6,4},{5,7},{7,5},{8,10},{10,8},{9,1... | collective-permute-start | bytes 2580488 | tf_op jit(solution)/shard_map/ppermute | solution.py:137
  90.0 16.7 %collective-permute-start.25 = (bf16[2,160,1024]{2,1,0:T(8,128)(2,1)}, bf16[2,160,1024]{2,1,0:T(8,128)(2,1)}, u32[]{:S(2)}, u32[]{:S(2)}) collective-permute-start(bf16[2,160,1024]{2,1,0:T(8,128)(2,1)} %shard_map.248.refs_17_), channel_id=1, source_target_pairs={{0,1},{1,0},{2,3},{3,2},{4,5},{5,4},{6,7},{7,6},{8,9},{9,8},{10,11... | collective-permute-start | bytes 1966088 | tf_op jit(solution)/shard_map/ppermute | solution.py:137
  91.8 14.9 %collective-permute-start.26 = (bf16[2,160,1024]{2,1,0:T(8,128)(2,1)}, bf16[2,160,1024]{2,1,0:T(8,128)(2,1)}, u32[]{:S(2)}, u32[]{:S(2)}) collective-permute-start(bf16[2,160,1024]{2,1,0:T(8,128)(2,1)} %collective-permute-done.4.refs_19_), channel_id=1, source_target_pairs={{0,1},{1,0},{2,3},{3,2},{4,5},{5,4},{6,7},{7,6},{8,9},{9,8},{10,11... | collective-permute-start | bytes 1966088 | tf_op jit(solution)/shard_map/ppermute | solution.py:137
  112.2 7.7 %collective-permute-start.30 = (bf16[1328,384]{1,0:T(8,128)(2,1)S(1)}, bf16[1328,384]{1,0:T(8,128)(2,1)S(1)}, u32[]{:S(2)}, u32[]{:S(2)}) collective-permute-start(bf16[1328,384]{1,0:T(8,128)(2,1)S(1)} %collective-permute-done.23.refs_7_.refs_6_), channel_id=1, source_target_pairs={{0,1},{1,0},{2,3},{3,2},{4,5},{5,4},{6,7},{7,6},{8,9},{9,8},{10,11... | collective-permute-start | bytes 3059720 | tf_op jit(solution)/shard_map/ppermute | solution.py:71
  113.4 6.0 %collective-permute-start.31 = (bf16[1120,384]{1,0:T(8,128)(2,1)}, bf16[1120,384]{1,0:T(8,128)(2,1)}, u32[]{:S(2)}, u32[]{:S(2)}) collective-permute-start(bf16[1120,384]{1,0:T(8,128)(2,1)} %collective-permute-done.24.refs_8_.refs_5_), channel_id=1, source_target_pairs={{0,1},{1,0},{2,3},{3,2},{4,5},{5,4},{6,7},{7,6},{8,9},{9,8},{10,11... | collective-permute-start | bytes 2580488 | tf_op jit(solution)/shard_map/ppermute | solution.py:71
  113.4 4.8 %collective-permute-start.27 = (bf16[352,384]{1,0:T(8,128)(2,1)}, bf16[352,384]{1,0:T(8,128)(2,1)}, u32[]{:S(2)}, u32[]{:S(2)}) collective-permute-start(bf16[352,384]{1,0:T(8,128)(2,1)} %bitcast.22.refs_1_), channel_id=1, source_target_pairs={{0,1},{1,0},{2,3},{3,2},{4,5},{5,4},{6,7},{7,6},{8,9},{9,8},{10,11... | collective-permute-start | bytes 811016 | tf_op jit(solution)/shard_map/ppermute | solution.py:71
  117.4 19.6 %collective-permute-start.35 = (bf16[384,384]{1,0:T(8,128)(2,1)S(1)}, bf16[384,384]{1,0:T(8,128)(2,1)}, u32[]{:S(2)}, u32[]{:S(2)}) collective-permute-start(bf16[384,384]{1,0:T(8,128)(2,1)S(1)} %collective-permute-done.11.refs_3_), channel_id=1, source_target_pairs={{0,1},{1,0},{2,3},{3,2},{4,5},{5,4},{6,7},{7,6},{8,9},{9,8},{10,11... | collective-permute-start | bytes 884744 | tf_op jit(solution)/shard_map/ppermute | solution.py:71
  117.8 19.2 %collective-permute-start.36 = (bf16[384,384]{1,0:T(8,128)(2,1)S(1)}, bf16[384,384]{1,0:T(8,128)(2,1)}, u32[]{:S(2)}, u32[]{:S(2)}) collective-permute-start(bf16[384,384]{1,0:T(8,128)(2,1)S(1)} %collective-permute-done.12.refs_4_), channel_id=1, source_target_pairs={{0,1},{1,0},{2,3},{3,2},{4,5},{5,4},{6,7},{7,6},{8,9},{9,8},{10,11... | collective-permute-start | bytes 884744 | tf_op jit(solution)/shard_map/ppermute | solution.py:71
  118.1 18.8 %collective-permute-start.33 = (bf16[384,384]{1,0:T(8,128)(2,1)}, bf16[384,384]{1,0:T(8,128)(2,1)}, u32[]{:S(2)}, u32[]{:S(2)}) collective-permute-start(bf16[384,384]{1,0:T(8,128)(2,1)} %get-tuple-element.373), channel_id=1, source_target_pairs={{0,4},{4,0},{8,12},{12,8},{16,20},{20,16},{24,28},{28,24},{1,5},{5... | collective-permute-start | bytes 884744 | tf_op jit(solution)/shard_map/ppermute | solution.py:137
  119.4 17.5 %collective-permute-start.34 = (bf16[768,384]{1,0:T(8,128)(2,1)S(1)}, bf16[768,384]{1,0:T(8,128)(2,1)}, u32[]{:S(2)}, u32[]{:S(2)}) collective-permute-start(bf16[768,384]{1,0:T(8,128)(2,1)S(1)} %bitcast.172), channel_id=1, source_target_pairs={{0,1},{1,0},{2,3},{3,2},{4,5},{5,4},{6,7},{7,6},{8,9},{9,8},{10,11... | collective-permute-start | bytes 1769480 | tf_op jit(solution)/shard_map/ppermute | solution.py:71
  119.9 17.1 %collective-permute-start.32 = (bf16[2,384,384]{2,1,0:T(8,128)(2,1)}, bf16[2,384,384]{2,1,0:T(8,128)(2,1)}, u32[]{:S(2)}, u32[]{:S(2)}) collective-permute-start(bf16[2,384,384]{2,1,0:T(8,128)(2,1)} %bitcast.201), channel_id=1, source_target_pairs={{0,2},{2,0},{1,3},{3,1},{4,6},{6,4},{5,7},{7,5},{8,10},{10,8},{9,1... | collective-permute-start | bytes 1769480 | tf_op jit(solution)/shard_map/ppermute | solution.py:137
  157.9 12.2 %collective-permute-start.39 = (bf16[8,2,192,384]{3,2,1,0:T(8,128)(2,1)S(1)}, bf16[8,2,192,384]{3,2,1,0:T(8,128)(2,1)S(1)}, u32[]{:S(2)}, u32[]{:S(2)}) collective-permute-start(bf16[8,2,192,384]{3,2,1,0:T(8,128)(2,1)S(1)} %shard_map.253), channel_id=1, source_target_pairs={{0,1},{1,0},{2,3},{3,2},{4,5},{5,4},{6,7},{7,6},{8,9},{9,8},{10,11... | collective-permute-start | bytes 7077896 | tf_op jit(solution)/shard_map/ppermute | solution.py:137
  172.0 17.0 %collective-permute-start.42 = (bf16[8,2,192,384]{3,2,1,0:T(8,128)(2,1)S(1)}, bf16[8,2,192,384]{3,2,1,0:T(8,128)(2,1)S(1)}, u32[]{:S(2)}, u32[]{:S(2)}) collective-permute-start(bf16[8,2,192,384]{3,2,1,0:T(8,128)(2,1)S(1)} %shard_map.256), channel_id=1, source_target_pairs={{0,1},{1,0},{2,3},{3,2},{4,5},{5,4},{6,7},{7,6},{8,9},{9,8},{10,11... | collective-permute-start | bytes 7077896 | tf_op jit(solution)/shard_map/ppermute | solution.py:137
  172.3 16.5 %collective-permute-start.41 = (bf16[2,192,384]{2,1,0:T(8,128)(2,1)S(1)}, bf16[2,192,384]{2,1,0:T(8,128)(2,1)S(1)}, u32[]{:S(2)}, u32[]{:S(2)}) collective-permute-start(bf16[2,192,384]{2,1,0:T(8,128)(2,1)S(1)} %get-tuple-element.422), channel_id=1, source_target_pairs={{0,8},{8,0},{4,12},{12,4},{16,24},{24,16},{20,28},{28,20},{1,9},{9... | collective-permute-start | bytes 884744 | tf_op jit(solution)/shard_map/ppermute | solution.py:137
  172.3 16.5 %collective-permute-start.43 = (bf16[2,192,384]{2,1,0:T(8,128)(2,1)S(1)}, bf16[2,192,384]{2,1,0:T(8,128)(2,1)S(1)}, u32[]{:S(2)}, u32[]{:S(2)}) collective-permute-start(bf16[2,192,384]{2,1,0:T(8,128)(2,1)S(1)} %get-tuple-element.427), channel_id=1, source_target_pairs={{0,4},{4,0},{8,12},{12,8},{16,20},{20,16},{24,28},{28,24},{1,5},{5... | collective-permute-start | bytes 884744 | tf_op jit(solution)/shard_map/ppermute | solution.py:137
  173.3 15.5 %collective-permute-start.40 = (bf16[4,192,384]{2,1,0:T(8,128)(2,1)S(1)}, bf16[4,192,384]{2,1,0:T(8,128)(2,1)S(1)}, u32[]{:S(2)}, u32[]{:S(2)}) collective-permute-start(bf16[4,192,384]{2,1,0:T(8,128)(2,1)S(1)} %get-tuple-element.420), channel_id=1, source_target_pairs={{0,2},{2,0},{1,3},{3,1},{4,6},{6,4},{5,7},{7,5},{8,10},{10,8},{9,1... | collective-permute-start | bytes 1769480 | tf_op jit(solution)/shard_map/ppermute | solution.py:137
  191.1 17.7 %collective-permute-start.47 = (bf16[8,2,272,384]{3,2,1,0:T(8,128)(2,1)S(1)}, bf16[8,2,272,384]{3,2,1,0:T(8,128)(2,1)S(1)}, u32[]{:S(2)}, u32[]{:S(2)}) collective-permute-start(bf16[8,2,272,384]{3,2,1,0:T(8,128)(2,1)S(1)} %shard_map.260), channel_id=1, source_target_pairs={{0,1},{1,0},{2,3},{3,2},{4,5},{5,4},{6,7},{7,6},{8,9},{9,8},{10,11... | collective-permute-start | bytes 10027016 | tf_op jit(solution)/shard_map/ppermute | solution.py:137
  192.2 20.7 %collective-permute-start.45 = (bf16[576,384]{1,0:T(8,128)(2,1)S(1)}, bf16[576,384]{1,0:T(8,128)(2,1)S(1)}, u32[]{:S(2)}, u32[]{:S(2)}) collective-permute-start(bf16[576,384]{1,0:T(8,128)(2,1)S(1)} %pad_maximum_fusion.12), channel_id=1, source_target_pairs={{0,8},{8,0},{4,12},{12,4},{16,24},{24,16},{20,28},{28,20},{1,9},{9... | collective-permute-start | bytes 1327112 | tf_op jit(solution)/shard_map/ppermute | solution.py:137
  192.8 20.1 %collective-permute-start.46 = (bf16[4,192,384]{2,1,0:T(8,128)(2,1)S(1)}, bf16[4,192,384]{2,1,0:T(8,128)(2,1)S(1)}, u32[]{:S(2)}, u32[]{:S(2)}) collective-permute-start(bf16[4,192,384]{2,1,0:T(8,128)(2,1)S(1)} %get-tuple-element.455), channel_id=1, source_target_pairs={{0,2},{2,0},{1,3},{3,1},{4,6},{6,4},{5,7},{7,5},{8,10},{10,8},{9,1... | collective-permute-start | bytes 1769480 | tf_op jit(solution)/shard_map/ppermute | solution.py:137
  193.5 19.4 %collective-permute-start.44 = (bf16[960,384]{1,0:T(8,128)(2,1)S(1)}, bf16[960,384]{1,0:T(8,128)(2,1)S(1)}, u32[]{:S(2)}, u32[]{:S(2)}) collective-permute-start(bf16[960,384]{1,0:T(8,128)(2,1)S(1)} %pad_maximum_fusion.7), channel_id=1, source_target_pairs={{0,4},{4,0},{8,12},{12,8},{16,20},{20,16},{24,28},{28,24},{1,5},{5... | collective-permute-start | bytes 2211848 | tf_op jit(solution)/shard_map/ppermute | solution.py:137
  213.6 16.7 %collective-permute-start.49 = (bf16[928,384]{1,0:T(8,128)(2,1)S(1)}, bf16[928,384]{1,0:T(8,128)(2,1)S(1)}, u32[]{:S(2)}, u32[]{:S(2)}) collective-permute-start(bf16[928,384]{1,0:T(8,128)(2,1)S(1)} %pad_maximum_fusion.8), channel_id=1, source_target_pairs={{0,8},{8,0},{4,12},{12,4},{16,24},{24,16},{20,28},{28,20},{1,9},{9... | collective-permute-start | bytes 2138120 | tf_op jit(solution)/shard_map/ppermute | solution.py:137
  213.7 19.3 %collective-permute-start.52 = (bf16[4,272,384]{2,1,0:T(8,128)(2,1)S(1)}, bf16[4,272,384]{2,1,0:T(8,128)(2,1)S(1)}, u32[]{:S(2)}, u32[]{:S(2)}) collective-permute-start(bf16[4,272,384]{2,1,0:T(8,128)(2,1)S(1)} %get-tuple-element.539), channel_id=1, source_target_pairs={{0,2},{2,0},{1,3},{3,1},{4,6},{6,4},{5,7},{7,5},{8,10},{10,8},{9,1... | collective-permute-start | bytes 2506760 | tf_op jit(solution)/shard_map/ppermute | solution.py:137
  214.5 19.4 %collective-permute-start.50 = (bf16[1120,384]{1,0:T(8,128)(2,1)S(1)}, bf16[1120,384]{1,0:T(8,128)(2,1)S(1)}, u32[]{:S(2)}, u32[]{:S(2)}) collective-permute-start(bf16[1120,384]{1,0:T(8,128)(2,1)S(1)} %pad_maximum_fusion.6), channel_id=1, source_target_pairs={{0,4},{4,0},{8,12},{12,8},{16,20},{20,16},{24,28},{28,24},{1,5},{5... | collective-permute-start | bytes 2580488 | tf_op jit(solution)/shard_map/ppermute | solution.py:137
  215.5 18.7 %collective-permute-start.48 = (bf16[2,2,160,1024]{3,2,1,0:T(8,128)(2,1)S(1)}, bf16[2,2,160,1024]{3,2,1,0:T(8,128)(2,1)S(1)}, u32[]{:S(2)}, u32[]{:S(2)}) collective-permute-start(bf16[2,2,160,1024]{3,2,1,0:T(8,128)(2,1)S(1)} %get-tuple-element.527), channel_id=1, source_target_pairs={{0,1},{1,0},{2,3},{3,2},{4,5},{5,4},{6,7},{7,6},{8,9},{9,8},{10,11... | collective-permute-start | bytes 3932168 | tf_op jit(solution)/shard_map/ppermute | solution.py:137
  217.2 17.6 %collective-permute-start.51 = (bf16[8,2,144,384]{3,2,1,0:T(8,128)(2,1)S(1)}, bf16[8,2,144,384]{3,2,1,0:T(8,128)(2,1)S(1)}, u32[]{:S(2)}, u32[]{:S(2)}) collective-permute-start(bf16[8,2,144,384]{3,2,1,0:T(8,128)(2,1)S(1)} %shard_map.264), channel_id=1, source_target_pairs={{0,1},{1,0},{2,3},{3,2},{4,5},{5,4},{6,7},{7,6},{8,9},{9,8},{10,11... | collective-permute-start | bytes 5308424 | tf_op jit(solution)/shard_map/ppermute | solution.py:137
  236.5 7.4 %collective-permute-start.55 = (bf16[192,384]{1,0:T(8,128)(2,1)S(1)}, bf16[192,384]{1,0:T(8,128)(2,1)S(1)}, u32[]{:S(2)}, u32[]{:S(2)}) collective-permute-start(bf16[192,384]{1,0:T(8,128)(2,1)S(1)} %fusion.13), channel_id=1, source_target_pairs={{0,16},{16,0},{4,20},{20,4},{8,24},{24,8},{12,28},{28,12},{1,17},{... | collective-permute-start | bytes 442376 | tf_op jit(solution)/shard_map/ppermute | solution.py:137
  238.1 10.3 %collective-permute-start.57 = (bf16[4,160,384]{2,1,0:T(8,128)(2,1)S(1)}, bf16[4,160,384]{2,1,0:T(8,128)(2,1)S(1)}, u32[]{:S(2)}, u32[]{:S(2)}) collective-permute-start(bf16[4,160,384]{2,1,0:T(8,128)(2,1)S(1)} %get-tuple-element.550), channel_id=1, source_target_pairs={{0,2},{2,0},{1,3},{3,1},{4,6},{6,4},{5,7},{7,5},{8,10},{10,8},{9,1... | collective-permute-start | bytes 1474568 | tf_op jit(solution)/shard_map/ppermute | solution.py:137
  238.8 16.2 %collective-permute-start.56 = (bf16[784,384]{1,0:T(8,128)(2,1)S(1)}, bf16[784,384]{1,0:T(8,128)(2,1)S(1)}, u32[]{:S(2)}, u32[]{:S(2)}) collective-permute-start(bf16[784,384]{1,0:T(8,128)(2,1)S(1)} %pad_maximum_fusion.10), channel_id=1, source_target_pairs={{0,8},{8,0},{4,12},{12,4},{16,24},{24,16},{20,28},{28,20},{1,9},{9... | collective-permute-start | bytes 1806344 | tf_op jit(solution)/shard_map/ppermute | solution.py:137
  240.1 57.8 %collective-permute-start.53 = (bf16[2,160,1024]{2,1,0:T(8,128)(2,1)S(1)}, bf16[2,160,1024]{2,1,0:T(8,128)(2,1)S(1)}, u32[]{:S(2)}, u32[]{:S(2)}) collective-permute-start(bf16[2,160,1024]{2,1,0:T(8,128)(2,1)S(1)} %fusion.1), channel_id=1, source_target_pairs={{0,2},{2,0},{1,3},{3,1},{4,6},{6,4},{5,7},{7,5},{8,10},{10,8},{9,1... | collective-permute-start | bytes 1966088 | tf_op jit(solution)/shard_map/ppermute | solution.py:137
  240.8 17.4 %collective-permute-start.54 = (bf16[1136,384]{1,0:T(8,128)(2,1)S(1)}, bf16[1136,384]{1,0:T(8,128)(2,1)S(1)}, u32[]{:S(2)}, u32[]{:S(2)}) collective-permute-start(bf16[1136,384]{1,0:T(8,128)(2,1)S(1)} %pad_maximum_fusion.3), channel_id=1, source_target_pairs={{0,4},{4,0},{8,12},{12,8},{16,20},{20,16},{24,28},{28,24},{1,5},{5... | collective-permute-start | bytes 2617352 | tf_op jit(solution)/shard_map/ppermute | solution.py:137
  258.6 6.6 %collective-permute-start.60 = (bf16[192,384]{1,0:T(8,128)(2,1)S(1)}, bf16[192,384]{1,0:T(8,128)(2,1)S(1)}, u32[]{:S(2)}, u32[]{:S(2)}) collective-permute-start(bf16[192,384]{1,0:T(8,128)(2,1)S(1)} %fusion.11), channel_id=1, source_target_pairs={{0,16},{16,0},{4,20},{20,4},{8,24},{24,8},{12,28},{28,12},{1,17},{... | collective-permute-start | bytes 442376 | tf_op jit(solution)/shard_map/ppermute | solution.py:137
  259.5 24.8 %collective-permute-start.70 = (bf16[2,192,384]{2,1,0:T(8,128)(2,1)S(1)}, bf16[2,192,384]{2,1,0:T(8,128)(2,1)S(1)}, u32[]{:S(2)}, u32[]{:S(2)}) collective-permute-start(bf16[2,192,384]{2,1,0:T(8,128)(2,1)S(1)} %pad_maximum_fusion.17), channel_id=1, source_target_pairs={{0,2},{2,0},{1,3},{3,1},{4,6},{6,4},{5,7},{7,5},{8,10},{10,8},{9,1... | collective-permute-start | bytes 884744 | tf_op jit(solution)/shard_map/ppermute | solution.py:137
  260.3 8.0 %collective-permute-start.58 = (bf16[432,384]{1,0:T(8,128)(2,1)S(1)}, bf16[432,384]{1,0:T(8,128)(2,1)S(1)}, u32[]{:S(2)}, u32[]{:S(2)}) collective-permute-start(bf16[432,384]{1,0:T(8,128)(2,1)S(1)} %pad_maximum_fusion.16), channel_id=1, source_target_pairs={{0,8},{8,0},{4,12},{12,4},{16,24},{24,16},{20,28},{28,20},{1,9},{9... | collective-permute-start | bytes 995336 | tf_op jit(solution)/shard_map/ppermute | solution.py:137
  260.9 7.5 %collective-permute-start.59 = (bf16[3,160,384]{2,1,0:T(8,128)(2,1)S(1)}, bf16[3,160,384]{2,1,0:T(8,128)(2,1)S(1)}, u32[]{:S(2)}, u32[]{:S(2)}) collective-permute-start(bf16[3,160,384]{2,1,0:T(8,128)(2,1)S(1)} %add_convert_fusion.4), channel_id=1, source_target_pairs={{0,4},{4,0},{8,12},{12,8},{16,20},{20,16},{24,28},{28,24},{1,5},{5... | collective-permute-start | bytes 1105928 | tf_op jit(solution)/shard_map/ppermute | solution.py:137
  268.5 6.9 %collective-permute-start.61 = (bf16[160,384]{1,0:T(8,128)(2,1)S(1)}, bf16[160,384]{1,0:T(8,128)(2,1)S(1)}, u32[]{:S(2)}, u32[]{:S(2)}) collective-permute-start(bf16[160,384]{1,0:T(8,128)(2,1)S(1)} %fusion.39), channel_id=1, source_target_pairs={{0,8},{8,0},{4,12},{12,4},{16,24},{24,16},{20,28},{28,20},{1,9},{9... | collective-permute-start | bytes 368648 | tf_op jit(solution)/shard_map/ppermute | solution.py:137
  268.6 8.8 %collective-permute-start.66 = (bf16[272,384]{1,0:T(8,128)(2,1)S(1)}, bf16[272,384]{1,0:T(8,128)(2,1)S(1)}, u32[]{:S(2)}, u32[]{:S(2)}) collective-permute-start(bf16[272,384]{1,0:T(8,128)(2,1)S(1)} %fusion.4), channel_id=1, source_target_pairs={{0,16},{16,0},{4,20},{20,4},{8,24},{24,8},{12,28},{28,12},{1,17},{... | collective-permute-start | bytes 626696 | tf_op jit(solution)/shard_map/ppermute | solution.py:137
  271.9 23.3 %collective-permute-start.64 = (bf16[2,192,384]{2,1,0:T(8,128)(2,1)S(1)}, bf16[2,192,384]{2,1,0:T(8,128)(2,1)S(1)}, u32[]{:S(2)}, u32[]{:S(2)}) collective-permute-start(bf16[2,192,384]{2,1,0:T(8,128)(2,1)S(1)} %pad_maximum_fusion.18), channel_id=1, source_target_pairs={{0,2},{2,0},{1,3},{3,1},{4,6},{6,4},{5,7},{7,5},{8,10},{10,8},{9,1... | collective-permute-start | bytes 884744 | tf_op jit(solution)/shard_map/ppermute | solution.py:137
  275.4 8.7 %collective-permute-start.62 = (bf16[160,384]{1,0:T(8,128)(2,1)S(1)}, bf16[160,384]{1,0:T(8,128)(2,1)S(1)}, u32[]{:S(2)}, u32[]{:S(2)}) collective-permute-start(bf16[160,384]{1,0:T(8,128)(2,1)S(1)} %fusion.24), channel_id=1, source_target_pairs={{0,16},{16,0},{4,20},{20,4},{8,24},{24,8},{12,28},{28,12},{1,17},{... | collective-permute-start | bytes 368648 | tf_op jit(solution)/shard_map/ppermute | solution.py:1337
  277.6 13.3 %collective-permute-start.68 = (bf16[2,272,384]{2,1,0:T(8,128)(2,1)S(1)}, bf16[2,272,384]{2,1,0:T(8,128)(2,1)S(1)}, u32[]{:S(2)}, u32[]{:S(2)}) collective-permute-start(bf16[2,272,384]{2,1,0:T(8,128)(2,1)S(1)} %pad_maximum_fusion.13), channel_id=1, source_target_pairs={{0,2},{2,0},{1,3},{3,1},{4,6},{6,4},{5,7},{7,5},{8,10},{10,8},{9,1... | collective-permute-start | bytes 1253384 | tf_op jit(solution)/shard_map/ppermute | solution.py:1337
  284.2 11.2 %collective-permute-start.63 = (bf16[2,160,384]{2,1,0:T(8,128)(2,1)S(1)}, bf16[2,160,384]{2,1,0:T(8,128)(2,1)S(1)}, u32[]{:S(2)}, u32[]{:S(2)}) collective-permute-start(bf16[2,160,384]{2,1,0:T(8,128)(2,1)S(1)} %pad_maximum_fusion.19), channel_id=1, source_target_pairs={{0,2},{2,0},{1,3},{3,1},{4,6},{6,4},{5,7},{7,5},{8,10},{10,8},{9,1... | collective-permute-start | bytes 737288 | tf_op jit(solution)/shard_map/ppermute | solution.py:1337
  284.4 15.1 %collective-permute-start.71 = (bf16[2,192,384]{2,1,0:T(8,128)(2,1)S(1)}, bf16[2,192,384]{2,1,0:T(8,128)(2,1)S(1)}, u32[]{:S(2)}, u32[]{:S(2)}) collective-permute-start(bf16[2,192,384]{2,1,0:T(8,128)(2,1)S(1)} %add_convert_fusion.5.mine), channel_id=1, source_target_pairs={{0,1},{1,0},{2,3},{3,2},{4,5},{5,4},{6,7},{7,6},{8,9},{9,8},{10,11... | collective-permute-start | bytes 884744 | tf_op jit(solution)/shard_map/ppermute | solution.py:513
  290.9 12.4 %collective-permute-start.69 = (bf16[2,272,384]{2,1,0:T(8,128)(2,1)S(1)}, bf16[2,272,384]{2,1,0:T(8,128)(2,1)S(1)}, u32[]{:S(2)}, u32[]{:S(2)}) collective-permute-start(bf16[2,272,384]{2,1,0:T(8,128)(2,1)S(1)} %add_convert_fusion.3.mine), channel_id=1, source_target_pairs={{0,1},{1,0},{2,3},{3,2},{4,5},{5,4},{6,7},{7,6},{8,9},{9,8},{10,11... | collective-permute-start | bytes 1253384 | tf_op jit(solution)/shard_map/ppermute | solution.py:513
  295.3 5.2 %collective-permute-start.65 = (bf16[2,192,384]{2,1,0:T(8,128)(2,1)S(1)}, bf16[2,192,384]{2,1,0:T(8,128)(2,1)S(1)}, u32[]{:S(2)}, u32[]{:S(2)}) collective-permute-start(bf16[2,192,384]{2,1,0:T(8,128)(2,1)S(1)} %add_convert_fusion.6.mine), channel_id=1, source_target_pairs={{0,1},{1,0},{2,3},{3,2},{4,5},{5,4},{6,7},{7,6},{8,9},{9,8},{10,11... | collective-permute-start | bytes 884744 | tf_op jit(solution)/shard_map/ppermute | solution.py:513
  295.5 6.2 %collective-permute-start.67 = (bf16[2,160,384]{2,1,0:T(8,128)(2,1)S(1)}, bf16[2,160,384]{2,1,0:T(8,128)(2,1)S(1)}, u32[]{:S(2)}, u32[]{:S(2)}) collective-permute-start(bf16[2,160,384]{2,1,0:T(8,128)(2,1)S(1)} %add_convert_fusion.7.mine), channel_id=1, source_target_pairs={{0,1},{1,0},{2,3},{3,2},{4,5},{5,4},{6,7},{7,6},{8,9},{9,8},{10,11... | collective-permute-start | bytes 737288 | tf_op jit(solution)/shard_map/ppermute | solution.py:513
  (72 other events, 590.7 us)
